TPU v7x, 32 devices: a whole 2x2x4 slice. The times are simulated.
32 devices in a mesh: dp: 8 (over z, y), chan: 4 (over x, core).
Axes of the slice: x: 2, y: 2, z: 4, core: 2. Of those that a mesh axis runs over, the one named last changes fastest.
Arguments:
- features: bfloat16 [128, 10, 10, 2048], P('dp', None, None, 'chan'), may hold values from -6 to 6
- labels: int32 [128], P('dp'), may hold values from 0 to 999
- class_weights: int32 [1000], replicated, may hold values from 1 to 10
- conv_in: float32 [2048, 512], P('dp', 'chan'), may hold values from -0.125 to 0.125
- conv_mid: float32 [3, 3, 512, 512], P(None, None, 'dp', 'chan'), may hold values from -0.09375 to 0.09375
- conv_out: float32 [512, 2048], P('chan', 'dp'), may hold values from -0.25 to 0.25
- classifier: float32 [2048, 1000], P('dp', 'chan'), may hold values from -0.44194174 to 0.44194174
- norms: float32 [2, 4, 768], P(None, 'chan'), may hold values from -1 to 2, as said below
- momentum_in: float32 [2048, 512], P('dp', 'chan'), may hold values from -0.03125 to 0.03125
- momentum_mid: float32 [3, 3, 512, 512], P(None, None, 'dp', 'chan'), may hold values from -0.03125 to 0.03125
- momentum_out: float32 [512, 2048], P('chan', 'dp'), may hold values from -0.03125 to 0.03125
- momentum_head: float32 [2048, 1000], P('dp', 'chan'), may hold values from -0.03125 to 0.03125
- momentum_norms: float32 [2, 4, 768], P(None, 'chan'), may hold values from -0.046875 to 0.046875
- average_in: float32 [2048, 512], P('dp', 'chan'), may hold values from -0.125 to 0.125
- average_mid: float32 [3, 3, 512, 512], P(None, None, 'dp', 'chan'), may hold values from -0.09375 to 0.09375
- average_out: float32 [512, 2048], P('chan', 'dp'), may hold values from -0.25 to 0.25
- average_head: float32 [2048, 1000], P('dp', 'chan'), may hold values from -0.125 to 0.125
- average_norms: float32 [2, 4, 768], P(None, 'chan'), may hold values from 0.5 to 1.5
Outputs:
- loss_sum: float32 [], replicated
- weight_sum: float32 [], replicated
- new_in: float32 [2048, 512], P('dp', 'chan')
- new_mid: float32 [3, 3, 512, 512], P(None, None, 'dp', 'chan')
- new_out: float32 [512, 2048], P('chan', 'dp')
- new_head: float32 [2048, 1000], P('dp', 'chan')
- new_norms: float32 [2, 4, 768], P(None, 'chan')
- fresh_in: float32 [2048, 512], P('dp', 'chan')
- fresh_mid: float32 [3, 3, 512, 512], P(None, None, 'dp', 'chan')
- fresh_out: float32 [512, 2048], P('chan', 'dp')
- fresh_head: float32 [2048, 1000], P('dp', 'chan')
- fresh_norms: float32 [2, 4, 768], P(None, 'chan')
- mean_in: float32 [2048, 512], P('dp', 'chan')
- mean_mid: float32 [3, 3, 512, 512], P(None, None, 'dp', 'chan')
- mean_out: float32 [512, 2048], P('chan', 'dp')
- mean_head: float32 [2048, 1000], P('dp', 'chan')
- mean_norms: float32 [2, 4, 768], P(None, 'chan')
- copy_in: bfloat16 [2048, 512], P('dp', 'chan')
- copy_mid: bfloat16 [3, 3, 512, 512], P(None, None, 'dp', 'chan')
- copy_out: bfloat16 [512, 2048], P('chan', 'dp')
- copy_head: bfloat16 [2048, 1000], P('dp', 'chan')
- copy_norms: bfloat16 [2, 4, 768], P(None, 'chan')
Inputs may be any that keep to these rules, and one draw needn't show every extreme that they name: `norms`: gains in row 0, shifts in row 1.
All inputs are finite; a program needn't handle non-finite values.
Results may differ from a plain program's by a relative error of at most 0.025.
Values may be sent and summed in bfloat16 or wider, within the bound.
No kernel may reach another device: no remote copies, remote signals or barrier semaphores. Data moves between devices by JAX's collectives and lax.ppermute only.
A program may use at most 128 MiB of HBM per device.

v0:
```python
import jax
import jax.numpy as jnp
from jax import lax
from jax.sharding import PartitionSpec as P

EPS = 1e-05
MOMENTUM = 0.5
AVERAGE = 0.5
RATE_MATRIX = 16.0
RATE_NORM = 64.0


def merged(array, axis, combine):
    everything = jax.tree.map(lambda part: lax.all_gather(part, axis), array)
    leading = jax.tree.map(lambda part: part[0], everything)

    def step(k, so_far):
        return combine(so_far, jax.tree.map(lambda part: part[k], everything))

    return lax.fori_loop(1, lax.axis_size(axis), step, leading)


def silu_grad(value):
    sigma = jax.nn.sigmoid(value)
    return sigma * (1.0 + value * (1.0 - sigma))


def norm_forward(hidden, gain, shift, count):
    totals = lax.psum(
        (jnp.sum(hidden, axis=(0, 1, 2)), jnp.sum(hidden * hidden, axis=(0, 1, 2))), "dp"
    )
    mean = totals[0] / count
    scale = lax.rsqrt(totals[1] / count - mean * mean + EPS)
    normed = (hidden - mean) * scale
    return (normed * gain + shift, normed, scale)


def norm_backward(upper, normed, scale, gain, count):
    sums = lax.psum((jnp.sum(upper, axis=(0, 1, 2)), jnp.sum(upper * normed, axis=(0, 1, 2))), "dp")
    lower = scale * gain * (upper - sums[0] / count - normed * (sums[1] / count))
    return (lower, sums[1], sums[0])


def spatial_forward(padded, kernel, size):
    total = jnp.zeros(padded.shape[:1] + (size, size, kernel.shape[3]), jnp.float32)
    for row in range(3):
        for col in range(3):
            window = padded[:, row : row + size, col : col + size, :]
            total = total + jnp.einsum(
                "bhwc,cd->bhwd", window, kernel[row, col], preferred_element_type=jnp.float32
            )
    return total


def spatial_backward(padded, kernel, upper, size):
    grad_input = jnp.zeros(padded.shape, jnp.float32)
    pieces = []
    for row in range(3):
        for col in range(3):
            window = padded[:, row : row + size, col : col + size, :]
            spread = jnp.einsum(
                "bhwd,cd->bhwc", upper, kernel[row, col], preferred_element_type=jnp.float32
            )
            grad_input = grad_input.at[:, row : row + size, col : col + size, :].add(spread)
            pieces.append(
                jnp.einsum("bhwc,bhwd->cd", window, upper, preferred_element_type=jnp.float32)
            )
    stacked = jnp.stack(pieces).reshape((3, 3) + pieces[0].shape)
    return (grad_input[:, 1:-1, 1:-1, :], stacked)


def advance(weight, grad, momentum, average, rate):
    fresh = MOMENTUM * momentum + grad
    weight_new = weight - rate * (grad + MOMENTUM * fresh)
    return (weight_new, fresh, AVERAGE * average + (1.0 - AVERAGE) * weight_new)


def shards(
    features,
    labels,
    class_weights,
    conv_in,
    conv_mid,
    conv_out,
    classifier,
    norms,
    momentum_in,
    momentum_mid,
    momentum_out,
    momentum_head,
    momentum_norms,
    average_in,
    average_mid,
    average_out,
    average_head,
    average_norms,
):
    images = features.shape[0]
    size = features.shape[1]
    count = images * size * size * lax.axis_size("dp")
    low_in, low_mid, low_out, low_head = (
        lax.all_gather(conv_in.astype(jnp.bfloat16), "dp", axis=0, tiled=True),
        lax.all_gather(conv_mid.astype(jnp.bfloat16), "dp", axis=2, tiled=True),
        lax.all_gather(conv_out.astype(jnp.bfloat16), "dp", axis=1, tiled=True),
        lax.all_gather(classifier.astype(jnp.bfloat16), "dp", axis=0, tiled=True),
    )
    gains = norms[0, 0]
    shifts = norms[1, 0]
    narrow = conv_in.shape[1]
    gain_one, shift_one = (gains[:narrow], shifts[:narrow])
    gain_two, shift_two = (gains[narrow : 2 * narrow], shifts[narrow : 2 * narrow])
    gain_three, shift_three = (gains[2 * narrow :], shifts[2 * narrow :])
    gathered = lax.all_gather(features, "chan", axis=3, tiled=True)
    hidden_one = jnp.einsum("bhwc,cd->bhwd", gathered, low_in, preferred_element_type=jnp.float32)
    pre_one, normed_one, scale_one = norm_forward(hidden_one, gain_one, shift_one, count)
    act_one = jax.nn.silu(pre_one).astype(jnp.bfloat16)
    whole_one = lax.all_gather(act_one, "chan", axis=3, tiled=True)
    padded = jnp.pad(whole_one, ((0, 0), (1, 1), (1, 1), (0, 0)))
    hidden_two = spatial_forward(padded, low_mid, size)
    pre_two, normed_two, scale_two = norm_forward(hidden_two, gain_two, shift_two, count)
    act_two = jax.nn.silu(pre_two).astype(jnp.bfloat16)
    partial_value = jnp.einsum(
        "bhwc,cd->bhwd", act_two, low_out, preferred_element_type=jnp.float32
    )
    hidden_three = lax.psum_scatter(
        partial_value.astype(jnp.bfloat16), "chan", scatter_dimension=3, tiled=True
    ).astype(jnp.float32)
    pre_three, normed_three, scale_three = norm_forward(
        hidden_three, gain_three, shift_three, count
    )
    summed = pre_three + features.astype(jnp.float32)
    output = jax.nn.silu(summed)
    pooled = jnp.mean(output, axis=(1, 2)).astype(jnp.bfloat16)
    pooled_all = lax.all_gather(pooled, "chan", axis=1, tiled=True)
    logits = jnp.dot(pooled_all, low_head, preferred_element_type=jnp.float32)
    offset = lax.axis_index("chan") * logits.shape[1]
    classes = offset + lax.broadcasted_iota(jnp.int32, logits.shape, 1)
    target = (classes == labels[:, None]).astype(jnp.float32)
    top = jnp.max(logits, axis=1)
    mass = jnp.sum(jnp.exp(logits - top[:, None]), axis=1)
    picked = jnp.sum(target * logits, axis=1)

    def combine(first, second):
        high = jnp.maximum(first[0], second[0])
        total = first[1] * jnp.exp(first[0] - high) + second[1] * jnp.exp(second[0] - high)
        return (high, total, first[2] + second[2])

    top, mass, picked = merged((top, mass, picked), "chan", combine)
    spread = top + jnp.log(mass)
    catalog = lax.broadcasted_iota(jnp.int32, (images, class_weights.shape[0]), 1)
    weight_row = jnp.sum(
        jnp.where(catalog == labels[:, None], class_weights[None, :], 0), axis=1
    ).astype(jnp.float32)
    loss_sum, weight_sum = lax.psum(
        (jnp.sum(weight_row * (spread - picked)), jnp.sum(weight_row)), "dp"
    )
    upper_logits = (
        (weight_row / weight_sum)[:, None] * (jnp.exp(logits - spread[:, None]) - target)
    ).astype(jnp.bfloat16)
    grad_head = jnp.dot(pooled_all.T, upper_logits, preferred_element_type=jnp.float32)
    grad_pooled = lax.psum_scatter(
        jnp.dot(upper_logits, low_head.T, preferred_element_type=jnp.float32).astype(jnp.bfloat16),
        "chan",
        scatter_dimension=1,
        tiled=True,
    ).astype(jnp.float32)
    upper_three = grad_pooled[:, None, None, :] / (size * size) * silu_grad(summed)
    down_three, gain_grad_three, shift_grad_three = norm_backward(
        upper_three, normed_three, scale_three, gain_three, count
    )
    low_three = down_three.astype(jnp.bfloat16)
    sent = lax.all_gather(low_three, "chan", axis=3, tiled=True)
    grad_out = jnp.einsum("bhwc,bhwd->cd", act_two, sent, preferred_element_type=jnp.float32)
    back_two = jnp.einsum("bhwd,cd->bhwc", sent, low_out, preferred_element_type=jnp.float32)
    upper_two = back_two * silu_grad(pre_two)
    down_two, gain_grad_two, shift_grad_two = norm_backward(
        upper_two, normed_two, scale_two, gain_two, count
    )
    partial_input, grad_mid = spatial_backward(padded, low_mid, down_two.astype(jnp.bfloat16), size)
    upper_one = lax.psum_scatter(
        partial_input.astype(jnp.bfloat16), "chan", scatter_dimension=3, tiled=True
    ).astype(jnp.float32) * silu_grad(pre_one)
    down_one, gain_grad_one, shift_grad_one = norm_backward(
        upper_one, normed_one, scale_one, gain_one, count
    )
    grad_in = jnp.einsum(
        "bhwc,bhwd->cd", gathered, down_one.astype(jnp.bfloat16), preferred_element_type=jnp.float32
    )
    grad_in, grad_mid, grad_out, grad_head = (
        lax.psum_scatter(
            grad_in.astype(jnp.bfloat16), "dp", scatter_dimension=0, tiled=True
        ).astype(jnp.float32),
        lax.psum_scatter(
            grad_mid.astype(jnp.bfloat16), "dp", scatter_dimension=2, tiled=True
        ).astype(jnp.float32),
        lax.psum_scatter(
            grad_out.astype(jnp.bfloat16), "dp", scatter_dimension=1, tiled=True
        ).astype(jnp.float32),
        lax.psum_scatter(
            grad_head.astype(jnp.bfloat16), "dp", scatter_dimension=0, tiled=True
        ).astype(jnp.float32),
    )
    grad_norms = jnp.stack(
        [
            jnp.concatenate([gain_grad_one, gain_grad_two, gain_grad_three]),
            jnp.concatenate([shift_grad_one, shift_grad_two, shift_grad_three]),
        ]
    )[:, None, :]
    params = (conv_in, conv_mid, conv_out, classifier, norms)
    grads = (grad_in, grad_mid, grad_out, grad_head, grad_norms)
    moments = (momentum_in, momentum_mid, momentum_out, momentum_head, momentum_norms)
    averages = (average_in, average_mid, average_out, average_head, average_norms)
    rates = (RATE_MATRIX, RATE_MATRIX, RATE_MATRIX, RATE_MATRIX, RATE_NORM)
    results = [
        advance(p, g, m, a, r) for p, g, m, a, r in zip(params, grads, moments, averages, rates)
    ]
    news = [item[0] for item in results]
    freshs = [item[1] for item in results]
    means = [item[2] for item in results]
    copies = [item.astype(jnp.bfloat16) for item in news]
    return (
        loss_sum,
        weight_sum,
        news[0],
        news[1],
        news[2],
        news[3],
        news[4],
        freshs[0],
        freshs[1],
        freshs[2],
        freshs[3],
        freshs[4],
        means[0],
        means[1],
        means[2],
        means[3],
        means[4],
        copies[0],
        copies[1],
        copies[2],
        copies[3],
        copies[4],
    )


def solution(mesh):
    return jax.shard_map(
        shards,
        mesh=mesh,
        in_specs=(
            P("dp", None, None, "chan"),
            P("dp"),
            P(),
            P("dp", "chan"),
            P(None, None, "dp", "chan"),
            P("chan", "dp"),
            P("dp", "chan"),
            P(None, "chan", None),
            P("dp", "chan"),
            P(None, None, "dp", "chan"),
            P("chan", "dp"),
            P("dp", "chan"),
            P(None, "chan", None),
            P("dp", "chan"),
            P(None, None, "dp", "chan"),
            P("chan", "dp"),
            P("dp", "chan"),
            P(None, "chan", None),
        ),
        out_specs=(
            P(),
            P(),
            P("dp", "chan"),
            P(None, None, "dp", "chan"),
            P("chan", "dp"),
            P("dp", "chan"),
            P(None, "chan", None),
            P("dp", "chan"),
            P(None, None, "dp", "chan"),
            P("chan", "dp"),
            P("dp", "chan"),
            P(None, "chan", None),
            P("dp", "chan"),
            P(None, None, "dp", "chan"),
            P("chan", "dp"),
            P("dp", "chan"),
            P(None, "chan", None),
            P("dp", "chan"),
            P(None, None, "dp", "chan"),
            P("chan", "dp"),
            P("dp", "chan"),
            P(None, "chan", None),
        ),
        check_vma=False,
    )
```

profile of v0, /device:TPU:0, one launch (start us, length us, event | category | flops | bytes accessed | tf_op | source)
XLA Modules:
  0.0 702.3 jit_solution(4323367283911798892)
XLA Ops:
  8.0 1.6 convert_element_type.110
  11.3 33.1 %all_gather.43 = bf16[2048,128]{1,0:T(8,128)(2,1)S(1)} all-gather(bf16[256,128]{1,0:T(8,128)(2,1)S(1)} %convert_element_type.108), channel_id=1, replica_groups=mesh['dp'=8,'chan'=4] {'dp'}, dimensions={0}, use_global_device_ids=true | all-gather | bytes 589824 | tf_op jit(solution)/shard_map/all_gather | solution.py:102
  44.4 15.8 %all-gather.8.cloned.1.call-done = bf16[16,10,10,2048]{3,0,2,1:T(8,128)(2,1)} async-done(((bf16[16,10,10,512]{3,0,2,1:T(8,128)(2,1)}), bf16[16,10,10,2048]{3,0,2,1:T(8,128)(2,1)}) %all-gather.8.cloned.1.call-update) | async-done | bytes 6553616 | tf_op jit(solution)/shard_map/all_gather | solution.py:113
  60.2 4.7 fusion.89
  64.9 21.5 %all-reduce.10 = (f32[128]{0:T(128)S(1)}, f32[128]{0:T(128)S(1)}) all-reduce(f32[128]{0:T(128)S(1)} %get-tuple-element.388, f32[128]{0:T(128)S(1)} %get-tuple-element.387), channel_id=1, replica_groups=mesh['dp'=8,'chan'=4] {'dp'}, use_global_device_ids=true, to_apply=%region_4.5 | all-reduce | flops 256 | bytes 2048 | tf_op jit(solution)/shard_map/psum | solution.py:29
  87.6 33.9 %all_gather.46 = bf16[128,2048]{1,0:T(8,128)(2,1)} all-gather(bf16[128,256]{1,0:T(8,128)(2,1)S(1)} %convert_element_type.112), channel_id=1, replica_groups=mesh['dp'=8,'chan'=4] {'dp'}, dimensions={1}, use_global_device_ids=true | all-gather | bytes 589824 | tf_op jit(solution)/shard_map/all_gather | solution.py:104
  121.6 6.6 all-gather.10.cloned.1.call-done
  128.2 2.1 fusion.74
  130.3 1.5 fusion.75
  135.9 21.4 %all-reduce.9 = (f32[128]{0:T(128)S(1)}, f32[128]{0:T(128)S(1)}) all-reduce(f32[128]{0:T(128)S(1)} %get-tuple-element.386, f32[128]{0:T(128)S(1)} %get-tuple-element.385), channel_id=1, replica_groups=mesh['dp'=8,'chan'=4] {'dp'}, use_global_device_ids=true, to_apply=%region_8.9 | all-reduce | flops 256 | bytes 2048 | tf_op jit(solution)/shard_map/psum | solution.py:29
  157.8 5.6 convolution_convert_fusion
  168.3 35.0 %all_gather.48 = bf16[2048,250]{1,0:T(8,128)(2,1)} all-gather(bf16[256,250]{1,0:T(8,128)(2,1)} %convert_element_type.117), channel_id=1, replica_groups=mesh['dp'=8,'chan'=4] {'dp'}, dimensions={0}, use_global_device_ids=true | all-gather | bytes 1152000 | tf_op jit(solution)/shard_map/all_gather | solution.py:105
  203.3 16.8 %reduce-scatter.10.cloned.1.call-done = bf16[16,10,10,512]{3,0,2,1:T(8,128)(2,1)} async-done(((bf16[16,10,10,2048]{3,0,2,1:T(8,128)(2,1)}), bf16[16,10,10,512]{3,0,2,1:T(8,128)(2,1)}) %reduce-scatter.10.cloned.1.call-update) | async-done | bytes 1638416 | tf_op jit(solution)/shard_map/reduce_scatter | solution.py:125
  220.2 1.9 convert_reduce_fusion
  222.1 22.1 %all-reduce.8 = (f32[512]{0:T(512)}, f32[512]{0:T(512)}) all-reduce(f32[512]{0:T(512)S(1)} %get-tuple-element.380, f32[512]{0:T(512)S(1)} %get-tuple-element.379), channel_id=1, replica_groups=mesh['dp'=8,'chan'=4] {'dp'}, use_global_device_ids=true, to_apply=%region_13.14 | all-reduce | flops 1024 | bytes 8192 | tf_op jit(solution)/shard_map/psum | solution.py:29
  245.6 2.8 multiply_reduce_fusion
  248.4 5.2 all_gather.47
  261.3 6.8 all-reduce.11
  272.0 3.9 while.28
  275.9 1.8 convert_reduce_fusion.1
  277.7 17.7 %psum.105 = f32[]{:T(128)} all-reduce(f32[]{:T(128)} %get-tuple-element.391), channel_id=1, replica_groups=mesh['dp'=8,'chan'=4] {'dp'}, use_global_device_ids=true, to_apply=%region_23.24 | all-reduce | flops 1 | bytes 8 | tf_op jit(solution)/shard_map/psum | solution.py:154
  297.3 2.3 convolution_convert_fusion.2
  299.7 18.2 %reduce-scatter.12.cloned.1.call-done = bf16[16,512]{1,0:T(8,128)(2,1)} async-done(((bf16[16,2048]{1,0:T(8,128)(2,1)}), bf16[16,512]{1,0:T(8,128)(2,1)}) %reduce-scatter.12.cloned.1.call-update) | async-done | bytes 16400 | tf_op jit(solution)/shard_map/reduce_scatter | solution.py:161
  319.2 3.9 fusion.86
  323.1 22.0 %all-reduce.7 = (f32[512]{0:T(512)}, f32[512]{0:T(512)}) all-reduce(f32[512]{0:T(512)} %get-tuple-element.378, f32[512]{0:T(512)} %get-tuple-element.377), channel_id=1, replica_groups=mesh['dp'=8,'chan'=4] {'dp'}, use_global_device_ids=true, to_apply=%region_28.29 | all-reduce | flops 1024 | bytes 8192 | tf_op jit(solution)/shard_map/psum | solution.py:39
  346.5 4.3 fusion.16
  350.9 2.5 convolution_convert_fusion.1
  355.4 39.9 %all-gather.14.cloned.1.call-done = bf16[16,10,10,2048]{3,0,2,1:T(8,128)(2,1)} async-done(((bf16[16,10,10,512]{3,0,2,1:T(8,128)(2,1)}), bf16[16,10,10,2048]{3,0,2,1:T(8,128)(2,1)}) %all-gather.14.cloned.1.call-update) | async-done | bytes 6553616 | tf_op jit(solution)/shard_map/all_gather | solution.py:172
  395.3 5.8 fusion.87
  401.1 21.4 %all-reduce.6 = (f32[128]{0:T(128)S(1)}, f32[128]{0:T(128)S(1)}) all-reduce(f32[128]{0:T(128)S(1)} %get-tuple-element.384, f32[128]{0:T(128)S(1)} %get-tuple-element.383), channel_id=1, replica_groups=mesh['dp'=8,'chan'=4] {'dp'}, use_global_device_ids=true, to_apply=%region_32.33 | all-reduce | flops 256 | bytes 2048 | tf_op jit(solution)/shard_map/psum | solution.py:39
  422.5 5.0 fusion.26
  429.1 1.5 fusion.73
  431.9 2.1 add_dynamic-update-slice_fusion
  434.1 2.8 fusion.18
  440.7 1.4 slice.534
  442.2 15.8 %copy.86 = bf16[16,10,10,512]{0,2,1,3:T(8,128)(2,1)} copy(bf16[16,10,10,512]{3,0,2,1:T(8,128)(2,1)} %slice.534) | data formatting | bytes 3276800
  458.0 22.4 %reshape.500 = bf16[512,1600]{1,0:T(8,128)(2,1)} reshape(bf16[512,10,10,16]{3,2,1,0:T(8,128)(2,1)} %bitcast.321) | data formatting | bytes 3276800
  491.1 1.8 fusion.91
  493.7 33.5 %reduce-scatter.18.cloned.1.call-done = bf16[128,256]{1,0:T(8,128)(2,1)} async-done(((bf16[128,2048]{1,0:T(8,128)(2,1)}), bf16[128,256]{1,0:T(8,128)(2,1)}) %reduce-scatter.18.cloned.1.call-update) | async-done | bytes 65552 | tf_op jit(solution)/shard_map/reduce_scatter | solution.py:196
  527.2 1.5 fusion.93
  528.8 29.1 %reduce-scatter.22.cloned.1.call-done = bf16[128,1600]{1,0:T(8,128)(2,1)} async-done(((bf16[512,1600]{1,0:T(8,128)(2,1)}), bf16[128,1600]{1,0:T(8,128)(2,1)}) %reduce-scatter.22.cloned.1.call-update) | async-done | bytes 409616
  557.9 6.4 reshape.501
  564.3 4.8 copy.87
  569.6 22.0 %all-reduce.5 = (f32[]{:T(128)}, f32[128]{0:T(128)S(1)}, f32[128]{0:T(128)S(1)}) all-reduce(f32[]{:T(128)} %get-tuple-element.392, f32[128]{0:T(128)S(1)} %get-tuple-element.382, f32[128]{0:T(128)S(1)} %get-tuple-element.381), channel_id=1, replica_groups=mesh['dp'=8,'chan'=4] {'dp'}, use_global_device_ids=true, to_apply=%region_21.22 | all-reduce | flops 257 | bytes 2056 | tf_op jit(solution)/shard_map/psum | solution.py:154
  591.6 5.4 fusion.27
  597.7 28.4 %reduce-scatter.16.cloned.1.call-done = bf16[3,3,64,128]{3,2,1,0:T(8,128)(2,1)} async-done(((bf16[3,3,512,128]{3,2,1,0:T(8,128)(2,1)}), bf16[3,3,64,128]{3,2,1,0:T(8,128)(2,1)}) %reduce-scatter.16.cloned.1.call-update) | async-done | bytes 147472 | tf_op jit(solution)/shard_map/reduce_scatter | solution.py:193
  626.1 1.8 fusion.95
  630.0 61.4 %reduce-scatter.14.cloned.1.call-done = bf16[256,128]{0,1:T(8,128)(2,1)} async-done(((bf16[2048,128]{0,1:T(8,128)(2,1)}), bf16[256,128]{0,1:T(8,128)(2,1)}) %reduce-scatter.14.cloned.1.call-update) | async-done | bytes 65552 | tf_op jit(solution)/shard_map/reduce_scatter | solution.py:190
  (220 shorter events, 61.1 us)
Async XLA Ops:
  7.2 53.0 %all-gather.8.cloned.1.call-start = ((), (), s32[]{:S(2)}) async-start(), calls=%async_computation.7 | async-start | bytes 8192000 | tf_op jit(solution)/shard_map/all_gather | solution.py:113
  7.9 113.6 %all-gather.12.cloned.1.call-start = ((), (), s32[]{:S(2)}) async-start(), calls=%async_computation.9 | async-start | bytes 1327104 | tf_op jit(solution)/shard_map/all_gather | solution.py:103
  9.6 118.5 %all-gather.10.cloned.1.call-start = ((), (), s32[]{:S(2)}) async-start(), calls=%async_computation.8 | async-start | bytes 2048000 | tf_op jit(solution)/shard_map/all_gather | solution.py:117
  11.3 75.1 %copy-start.40 = (f32[128]{0:T(128)}, f32[128]{0:T(128)S(1)}, u32[]{:S(2)}) copy-start(f32[128]{0:T(128)S(1)} %get-tuple-element.448) | copy-start | bytes 1540
  11.3 75.1 %copy-start.42 = (f32[128]{0:T(128)}, f32[128]{0:T(128)S(1)}, u32[]{:S(2)}) copy-start(f32[128]{0:T(128)S(1)} %get-tuple-element.449) | copy-start | bytes 1540
  11.3 146.5 %copy-start.50 = (f32[128]{0:T(128)}, f32[128]{0:T(128)S(1)}, u32[]{:S(2)}) copy-start(f32[128]{0:T(128)S(1)} %get-tuple-element.446) | copy-start | bytes 1540
  11.3 146.5 %copy-start.52 = (f32[128]{0:T(128)}, f32[128]{0:T(128)S(1)}, u32[]{:S(2)}) copy-start(f32[128]{0:T(128)S(1)} %get-tuple-element.447) | copy-start | bytes 1540
  44.4 43.2 %copy-start.16 = (f32[128,256]{1,0:T(8,128)S(1)}, f32[128,256]{1,0:T(8,128)}, u32[]{:S(2)}) copy-start(f32[128,256]{1,0:T(8,128)} %param.43) | copy-start | bytes 393220
  64.9 56.6 %copy-start.7 = (f32[16,10,10,128]{3,0,2,1:T(8,128)}, f32[16,10,10,128]{3,0,2,1:T(8,128)S(1)}, u32[]{:S(2)}) copy-start(f32[16,10,10,128]{3,0,2,1:T(8,128)S(1)} %get-tuple-element.461) | copy-start | bytes 2457604
  87.5 132.6 %reduce-scatter.10.cloned.1.call-start = ((), (), s32[]{:S(2)}) async-start(), calls=%async_computation.10 | async-start | bytes 8192000 | tf_op jit(solution)/shard_map/reduce_scatter | solution.py:125
  134.7 22.6 %copy-start.28 = (f32[2,1,768]{2,1,0:T(1,128)S(1)}, f32[2,1,768]{2,1,0:T(1,128)}, u32[]{:S(2)}) copy-start(f32[2,1,768]{2,1,0:T(1,128)} %param.45) | copy-start | bytes 18436
  135.9 27.6 %copy-start.3 = (f32[16,10,10,128]{3,0,2,1:T(8,128)}, f32[16,10,10,128]{3,0,2,1:T(8,128)S(1)}, u32[]{:S(2)}) copy-start(f32[16,10,10,128]{3,0,2,1:T(8,128)S(1)} %get-tuple-element.462) | copy-start | bytes 2457604
  157.8 5.7 copy-start.44
  157.8 5.7 copy-start.46
  163.6 82.0 %copy-start.1 = (bf16[16,10,10,512]{3,0,2,1:T(8,128)(2,1)S(1)}, bf16[16,10,10,512]{3,0,2,1:T(8,128)(2,1)}, u32[]{:S(2)}) copy-start(bf16[16,10,10,512]{3,0,2,1:T(8,128)(2,1)} %param.38) | copy-start | bytes 4915204
  163.6 154.3 %reduce-scatter.12.cloned.1.call-start = ((), (), s32[]{:S(2)}) async-start(), calls=%async_computation.11 | async-start | bytes 81920 | tf_op jit(solution)/shard_map/reduce_scatter | solution.py:161
  168.3 80.1 %copy-start.24 = (f32[1,1,512]{2,1,0:T(1,128)}, f32[1,1,512]{2,1,0:T(1,128)S(1)}, u32[]{:S(2)}) copy-start(f32[1,1,512]{2,1,0:T(1,128)S(1)} %get-tuple-element.444) | copy-start | bytes 6148
  168.3 80.1 %copy-start.25 = (f32[1,1,512]{2,1,0:T(1,128)}, f32[1,1,512]{2,1,0:T(1,128)S(1)}, u32[]{:S(2)}) copy-start(f32[1,1,512]{2,1,0:T(1,128)S(1)} %get-tuple-element.445) | copy-start | bytes 6148
  244.2 9.5 %copy-start.2 = (bf16[2048,250]{1,0:T(8,128)(2,1)S(1)}, bf16[2048,250]{1,0:T(8,128)(2,1)}, u32[]{:S(2)}) copy-start(bf16[2048,250]{1,0:T(8,128)(2,1)} %all_gather.48) | copy-start | bytes 3072004
  245.5 9.0 %copy-start.26 = (f32[512]{0:T(512)}, f32[512]{0:T(512)S(1)}, u32[]{:S(2)}) copy-start(f32[512]{0:T(512)S(1)} %get-tuple-element.451) | copy-start | bytes 6148
  245.5 9.0 %copy-start.27 = (f32[512]{0:T(512)}, f32[512]{0:T(512)S(1)}, u32[]{:S(2)}) copy-start(f32[512]{0:T(512)S(1)} %get-tuple-element.452) | copy-start | bytes 6148
  299.6 95.6 %all-gather.14.cloned.1.call-start = ((), (), s32[]{:S(2)}) async-start(), calls=%async_computation.12 | async-start | bytes 8192000 | tf_op jit(solution)/shard_map/all_gather | solution.py:172
  350.8 44.5 %copy-start.4 = (f32[16,10,10,128]{3,0,2,1:T(8,128)S(1)}, f32[16,10,10,128]{3,0,2,1:T(8,128)}, u32[]{:S(2)}) copy-start(f32[16,10,10,128]{3,0,2,1:T(8,128)} %copy-done.3) | copy-start | bytes 2457604
  350.8 44.5 %copy-start.45 = (f32[128]{0:T(128)S(1)}, f32[128]{0:T(128)}, u32[]{:S(2)}) copy-start(f32[128]{0:T(128)} %copy-done.44) | copy-start | bytes 1540
  350.8 44.5 %copy-start.47 = (f32[128]{0:T(128)S(1)}, f32[128]{0:T(128)}, u32[]{:S(2)}) copy-start(f32[128]{0:T(128)} %copy-done.46) | copy-start | bytes 1540
  350.8 44.4 %copy-start.51 = (f32[128]{0:T(128)S(1)}, f32[128]{0:T(128)}, u32[]{:S(2)}) copy-start(f32[128]{0:T(128)} %copy-done.50) | copy-start | bytes 1540
  350.8 44.4 %copy-start.53 = (f32[128]{0:T(128)S(1)}, f32[128]{0:T(128)}, u32[]{:S(2)}) copy-start(f32[128]{0:T(128)} %copy-done.52) | copy-start | bytes 1540
  350.9 140.2 %reduce-scatter.20.cloned.1.call-start = ((), (), s32[]{:S(2)}) async-start(), calls=%async_computation.16 | async-start | bytes 1179648 | tf_op jit(solution)/shard_map/reduce_scatter | solution.py:199
  353.4 173.8 %reduce-scatter.18.cloned.1.call-start = ((), (), s32[]{:S(2)}) async-start(), calls=%async_computation.15 | async-start | bytes 589824 | tf_op jit(solution)/shard_map/reduce_scatter | solution.py:196
  427.5 130.3 %reduce-scatter.22.cloned.1.call-start = ((), (), s32[]{:S(2)}) async-start(), calls=%async_computation.17 | async-start | bytes 2129920
  480.4 145.7 %reduce-scatter.16.cloned.1.call-start = ((), (), s32[]{:S(2)}) async-start(), calls=%async_computation.14 | async-start | bytes 1327104 | tf_op jit(solution)/shard_map/reduce_scatter | solution.py:193
  486.9 6.0 copy-start.21
  486.9 40.3 %copy-start.17 = (f32[128,256]{1,0:T(8,128)S(1)}, f32[128,256]{1,0:T(8,128)}, u32[]{:S(2)}) copy-start(f32[128,256]{1,0:T(8,128)} %param.43) | copy-start | bytes 393220
  486.9 40.3 %copy-start.22 = (f32[128,256]{1,0:T(8,128)S(1)}, f32[128,256]{1,0:T(8,128)}, u32[]{:S(2)}) copy-start(f32[128,256]{1,0:T(8,128)} %param.48) | copy-start | bytes 393220
  487.9 203.4 %reduce-scatter.14.cloned.1.call-start = ((), (), s32[]{:S(2)}) async-start(), calls=%async_computation.13 | async-start | bytes 589824 | tf_op jit(solution)/shard_map/reduce_scatter | solution.py:190
  492.9 71.3 %copy-start.12 = (f32[256,250]{1,0:T(8,128)}, f32[256,250]{1,0:T(8,128)S(1)}, u32[]{:S(2)}) copy-start(f32[256,250]{1,0:T(8,128)S(1)} %get-tuple-element.426) | copy-start | bytes 768004
  528.8 68.3 %copy-start.15 = (f32[128,256]{1,0:T(8,128)}, f32[128,256]{1,0:T(8,128)S(1)}, u32[]{:S(2)}) copy-start(f32[128,256]{1,0:T(8,128)S(1)} %get-tuple-element.429) | copy-start | bytes 393220
  564.3 27.3 %copy-start.55 = (f32[128]{0:T(128)S(1)}, f32[128]{0:T(128)}, u32[]{:S(2)}) copy-start(f32[128]{0:T(128)} %get-tuple-element.442) | copy-start | bytes 1540
  591.6 34.6 %copy-start.11 = (f32[3,3,64,128]{3,2,1,0:T(8,128)S(1)}, f32[3,3,64,128]{3,2,1,0:T(8,128)}, u32[]{:S(2)}) copy-start(f32[3,3,64,128]{3,2,1,0:T(8,128)} %param.42) | copy-start | bytes 884740
  591.6 34.6 %copy-start.20 = (f32[3,3,64,128]{3,2,1,0:T(8,128)S(1)}, f32[3,3,64,128]{3,2,1,0:T(8,128)}, u32[]{:S(2)}) copy-start(f32[3,3,64,128]{3,2,1,0:T(8,128)} %param.47) | copy-start | bytes 884740
  591.6 36.3 %copy-start.19 = (f32[3,3,64,128]{3,2,1,0:T(8,128)S(1)}, f32[3,3,64,128]{3,2,1,0:T(8,128)}, u32[]{:S(2)}) copy-start(f32[3,3,64,128]{3,2,1,0:T(8,128)} %param.52) | copy-start | bytes 884740
  597.0 31.7 %copy-start.32 = (f32[512]{0:T(512)S(1)}, f32[512]{0:T(512)}, u32[]{:S(2)}) copy-start(f32[512]{0:T(512)} %get-tuple-element.412) | copy-start | bytes 6148
  597.0 31.7 %copy-start.33 = (f32[512]{0:T(512)S(1)}, f32[512]{0:T(512)}, u32[]{:S(2)}) copy-start(f32[512]{0:T(512)} %get-tuple-element.413) | copy-start | bytes 6148
  597.0 31.8 %copy-start.29 = (f32[2,1,768]{2,1,0:T(1,128)S(1)}, f32[2,1,768]{2,1,0:T(1,128)}, u32[]{:S(2)}) copy-start(f32[2,1,768]{2,1,0:T(1,128)} %param.45) | copy-start | bytes 18436
  597.0 31.8 %copy-start.34 = (f32[2,1,768]{2,1,0:T(1,128)S(1)}, f32[2,1,768]{2,1,0:T(1,128)}, u32[]{:S(2)}) copy-start(f32[2,1,768]{2,1,0:T(1,128)} %param.55) | copy-start | bytes 18436
  597.0 31.8 %copy-start.35 = (f32[2,1,768]{2,1,0:T(1,128)S(1)}, f32[2,1,768]{2,1,0:T(1,128)}, u32[]{:S(2)}) copy-start(f32[2,1,768]{2,1,0:T(1,128)} %param.50) | copy-start | bytes 18436
  627.9 67.4 %copy-start.10 = (f32[3,3,64,128]{3,2,1,0:T(8,128)}, f32[3,3,64,128]{3,2,1,0:T(8,128)S(1)}, u32[]{:S(2)}) copy-start(f32[3,3,64,128]{3,2,1,0:T(8,128)S(1)} %get-tuple-element.432) | copy-start | bytes 884740
  629.4 65.9 %copy-start.30 = (f32[2,1,768]{2,1,0:T(1,128)}, f32[2,1,768]{2,1,0:T(1,128)S(1)}, u32[]{:S(2)}) copy-start(f32[2,1,768]{2,1,0:T(1,128)S(1)} %get-tuple-element.437) | copy-start | bytes 18436
  (20 other events, 60.2 us)
Sparse Core Ops, SparseCore 0:
  9.6 50.5 all-gather.7
  62.9 45.0 all-gather.11
  109.6 18.5 all-gather.9
  163.7 56.4 reduce-scatter.9
  299.7 18.1 reduce-scatter.11
  351.0 44.2 all-gather.13
  398.7 63.3 reduce-scatter.19
  465.8 61.3 reduce-scatter.17
  529.8 28.0 reduce-scatter.21
  561.5 64.5 reduce-scatter.15
  629.8 61.4 reduce-scatter.13
where the time goes:
time: 712 us; the launch traced here: 702 us
  blocking collectives  262 us (37%)
  waiting for transfers between devices  251 us (35%)
  local copies, waits for them, and re-layouts  74.2 us (10%)
  matrix products  56.3 us (8%)
  other arithmetic  42.4 us (6%)
  between operations  15.7 us (2%)
    unnamed x132, local copies, waits for them, and re-layouts  65.6 us
    psum x3, blocking collectives, norm_forward(): lax.psum((jnp.sum(hidden, axis=(0, 1, 2)), jnp.sum(hidden * hidden, axis=...  64.9 us
    reduce_scatter x1, waiting for transfers between devices, shards(): lax.psum_scatter(grad_in.astype(jnp.bfloat16), 'dp', scatter_dimension=0,...  61.4 us
    psum x2, blocking collectives, norm_backward(): lax.psum((jnp.sum(upper, axis=(0, 1, 2)), jnp.sum(upper * normed, axis=(0...  43.4 us
    all_gather x1, waiting for transfers between devices, shards(): sent = lax.all_gather(low_three, 'chan', axis=3, tiled=True)  39.9 us
    psum x2, blocking collectives, shards(): lax.psum((jnp.sum(weight_row * (spread - picked)), jnp.sum(weight_row)),...  39.7 us
    all_gather x1, blocking collectives, shards(): lax.all_gather(classifier.astype(jnp.bfloat16), 'dp', axis=0, tiled=True)  35 us
    all_gather x1, blocking collectives, shards(): lax.all_gather(conv_out.astype(jnp.bfloat16), 'dp', axis=1, tiled=True)  33.9 us
  transfers between devices with their start and end apart: 11, of which 9 were waited for; matrix products, arithmetic and copies ran while one was open for 16% of the time, Pallas kernels for 0%

commit v1 on v0

v1 whole, which is shorter than its diff:
```python
import functools

import jax
import jax.numpy as jnp
from jax import lax
from jax.experimental import pallas as pl
from jax.experimental.pallas import tpu as pltpu
from jax.sharding import PartitionSpec as P

EPS = 1e-05
MOMENTUM = 0.5
AVERAGE = 0.5
RATE_MATRIX = 16.0
RATE_NORM = 64.0
AXES = ("dp", "chan")
F32 = jnp.float32
BF16 = jnp.bfloat16
CHUNK = 80
LANES = 128


def swap(array, mask, n):
    return lax.ppermute(array, AXES, [(d, d ^ mask) for d in range(n)])


def tree_sum(parts):
    while len(parts) > 1:
        parts = [parts[k] + parts[k + 1] for k in range(0, len(parts), 2)]
    return parts[0]


def high_masks(n):
    return [8 * k for k in range(n // 8)]


def total(array, n):
    array = array + swap(array, 1, n)
    array = tree_sum([array] + [swap(array, mask, n) for mask in (2, 4, 6)])
    return tree_sum([array] + [swap(array, mask, n) for mask in high_masks(n)[1:]])


def gather(shard, n):
    stack = jnp.stack([shard] + [swap(shard, mask, n) for mask in high_masks(n)[1:]])
    even = [stack] + [swap(stack, mask, n) for mask in (2, 4, 6)]
    odd = [swap(part, 1, n) for part in even]
    return [even[0], odd[0], even[1], odd[1], even[2], odd[2], even[3], odd[3]]


def scatter_sum(parts, n):
    arrived = [swap(parts[k], 1, n) for k in (3, 5, 7, 1)]
    merged = [
        (own.astype(F32) + other.astype(F32)).astype(BF16)
        for own, other in zip((parts[2], parts[4], parts[6], parts[0]), arrived)
    ]
    across = [swap(merged[k], 2 * k + 2, n) for k in range(3)]
    both = tree_sum([part.astype(F32) for part in [merged[3]] + across]).astype(BF16)
    last = [both[0]] + [swap(both[a], mask, n) for a, mask in enumerate(high_masks(n)) if a]
    return tree_sum([part.astype(F32) for part in last])


def call(kernel, outs, *inputs, flops=0):
    moved = sum(x.size * x.dtype.itemsize for x in inputs)
    shapes = [jax.ShapeDtypeStruct(*out) for out in outs]
    moved += sum(s.size * s.dtype.itemsize for s in shapes)
    return pl.pallas_call(
        kernel,
        out_shape=shapes,
        in_specs=[pl.BlockSpec(memory_space=pltpu.SMEM)]
        + [pl.BlockSpec(memory_space=pltpu.VMEM)] * (len(inputs) - 1),
        out_specs=[pl.BlockSpec(memory_space=pltpu.VMEM)] * len(outs),
        compiler_params=pltpu.CompilerParams(vmem_limit_bytes=56 * 2**20),
        cost_estimate=pl.CostEstimate(flops=flops, bytes_accessed=moved, transcendentals=0),
    )(*inputs)


def sigmoid(value):
    return 0.5 * jnp.tanh(0.5 * value) + 0.5


def silu_grad(value):
    sigma = sigmoid(value)
    return sigma * (1.0 + value * (1.0 - sigma))


def dot(a, b, dims=((1,), (0,))):
    return lax.dot_general(a, b, (dims, ((), ())), preferred_element_type=F32)


def statistics(sums_ref, count, cols):
    mean = sums_ref[0:1, cols] / count
    square = sums_ref[1:2, cols] / count
    return mean, lax.rsqrt(square - mean * mean + EPS)


def col_sum(value):
    return jnp.sum(value, axis=0, keepdims=True)


def rows_of(step):
    return pl.ds(pl.multiple_of(step * CHUNK, CHUNK), CHUNK)


def assemble_kernel(c, *refs):
    me, *parts, out = refs
    number = me[0] * c + me[1]
    for k, part in enumerate(parts):
        for a in range(part.shape[0]):
            other = number ^ (8 * a + k)
            i, j = lax.div(other, c), lax.rem(other, c)
            if len(out.shape) == 3:
                rows, cols = part.shape[2:]
                out[
                    :,
                    pl.ds(pl.multiple_of(i * rows, rows), rows),
                    pl.ds(pl.multiple_of(j * cols, cols), cols),
                ] = part[a]
            else:
                rows, cols = part.shape[1:]
                out[
                    pl.ds(pl.multiple_of(i * rows, rows), rows),
                    pl.ds(pl.multiple_of(j * cols, cols), cols),
                ] = part[a]


def assemble_out_kernel(c, *refs):
    me, *parts, out = refs
    number = me[0] * c + me[1]
    for k, part in enumerate(parts):
        for a in range(part.shape[0]):
            other = number ^ (8 * a + k)
            i, j = lax.div(other, c), lax.rem(other, c)
            rows, cols = part.shape[1:]
            out[
                pl.ds(pl.multiple_of(j * rows, rows), rows),
                pl.ds(pl.multiple_of(i * cols, cols), cols),
            ] = part[a]


def first_kernel(me, weight_sum, *refs):
    *features, weights, hidden, sums = refs
    chan, depth = me[1], features[0].shape[1]
    width = hidden.shape[1]
    for start in range(0, width, 256):
        cols = slice(start, start + 256)
        value = None
        for k, part in enumerate(features):
            rows = pl.ds(pl.multiple_of((chan ^ k) * depth, depth), depth)
            term = dot(part[...], weights[rows, cols])
            value = term if value is None else value + term
        hidden[:, cols] = value
        sums[0:1, cols] = col_sum(value)
        sums[1:2, cols] = col_sum(value * value)
    sums[2:3, :] = jnp.broadcast_to(weight_sum[...], (1, width))


def windows(pad, out, size, group):
    line = size * group
    rows, width = out.shape[0], pad.shape[2]
    for i in range(3):
        for j in range(3):
            tap = 3 * i + j
            out[:, tap * width : (tap + 1) * width] = pad[
                j, i * line : i * line + rows, :
            ].astype(BF16)


def fill(pad, size, group):
    line = size * group
    rows, width = pad.shape[1] - 2 * line, pad.shape[2]
    place = lax.broadcasted_iota(jnp.int32, (rows, 1), 0)
    column = lax.rem(lax.div(place, group), size)
    here = pad[1, line : line + rows, :]
    empty = jnp.zeros((line, width), F32)
    for j in (0, 2):
        moved = pltpu.roll(here, group if j == 0 else rows - group, 0)
        valid = column != (0 if j == 0 else size - 1)
        pad[j, 0:line, :] = empty
        pad[j, line : line + rows, :] = jnp.where(valid, moved, 0.0)
        pad[j, line + rows :, :] = empty


def second_kernel(count, size, group, me, hidden, sums, norms, weights, cols, out, out_sums, pad):
    rows, width = hidden.shape
    line = size * group
    mean, scale = statistics(sums, count, slice(None))
    gain, shift = norms[0:1, :], norms[1:2, :]
    pad[1, 0:line, :] = jnp.zeros((line, width), F32)
    pad[1, line + rows :, :] = jnp.zeros((line, width), F32)
    for step in range(rows // CHUNK):
        part = slice(step * CHUNK, (step + 1) * CHUNK)
        value = (hidden[part, :] - mean) * scale * gain + shift
        act = (value * sigmoid(value)).astype(BF16).astype(F32)
        pad[1, line + step * CHUNK : line + (step + 1) * CHUNK, :] = act
    fill(pad, size, group)
    windows(pad, cols, size, group)
    for start in range(0, out.shape[1], 256):
        block = slice(start, start + 256)
        value = dot(cols[...], weights[:, block])
        out[:, block] = value
        out_sums[0:1, block] = col_sum(value)
        out_sums[1:2, block] = col_sum(value * value)


def third_kernel(count, me, hidden, sums, norms, weights, act, out, out_sums):
    mean, scale = statistics(sums, count, slice(None))
    gain, shift = norms[0:1, :], norms[1:2, :]
    for step in range(hidden.shape[0] // CHUNK):
        part = slice(step * CHUNK, (step + 1) * CHUNK)
        value = (hidden[part, :] - mean) * scale * gain + shift
        act[part, :] = (value * sigmoid(value)).astype(BF16)
    for start in range(0, out.shape[1], 256):
        block = slice(start, start + 256)
        value = dot(act[...], weights[:, block])
        out[:, block] = value
        out_sums[0:1, block] = col_sum(value)
        out_sums[1:2, block] = col_sum(value * value)


def head_kernel(count, pixels, group, classes, me, hidden, sums, norms, row_weights, target, weights, *refs):
    *features, upper, out_sums, packed, loss = refs
    chan, rows = me[1], hidden.shape[0]
    width = features[0].shape[1]
    twice = 2 * group
    blocks = [pl.ds(pl.multiple_of((chan ^ k) * width, width), width) for k in range(len(features))]
    for k, cols in enumerate(blocks):
        mean, scale = statistics(sums, count, cols)
        gain = scale * norms[0:1, cols]
        shift = norms[1:2, cols] - mean * gain

        def forward(step, pool, k=k, cols=cols, gain=gain, shift=shift):
            part = rows_of(step)
            value = hidden[part, cols] * gain + shift + features[k][part, :].astype(F32)
            upper[part, cols] = value
            value = value * sigmoid(value)
            return pool + jnp.sum(value.reshape(CHUNK // twice, twice, width), axis=0)

        pool = lax.fori_loop(0, rows // CHUNK, forward, jnp.zeros((twice, width), F32))
        pool = (pool + pltpu.roll(pool, group, 0)) / pixels
        packed[:, cols] = pool.astype(BF16)
    depth, space = weights.shape
    pooled = packed[:, 0:depth]
    logits = dot(pooled, weights[...])
    column = lax.broadcasted_iota(jnp.int32, logits.shape, 1)
    valid = lax.rem(column, space // len(features)) < classes
    top = jnp.max(jnp.where(valid, logits, -jnp.inf), axis=1, keepdims=True)
    grown = jnp.where(valid, jnp.exp(logits - top), 0.0)
    spread = top + jnp.log(jnp.sum(grown, axis=1, keepdims=True))
    wanted = target[...]
    picked = jnp.sum(wanted * logits, axis=1, keepdims=True)
    weight, share = row_weights[:, 0:1], row_weights[:, 1:2]
    loss[...] = 0.5 * jnp.sum(weight * (spread - picked), axis=0, keepdims=True)
    down = share * (jnp.where(valid, jnp.exp(logits - spread), 0.0) - wanted)
    packed[:, depth:] = down.astype(BF16)
    low_down = down.astype(BF16)
    for k, cols in enumerate(blocks):
        mean, scale = statistics(sums, count, cols)
        back = dot(low_down, weights[cols, :], ((1,), (1,))) / pixels
        back = jnp.broadcast_to(back[None], (CHUNK // twice, twice, width)).reshape(CHUNK, width)

        def backward(step, so_far, cols=cols, mean=mean, scale=scale, back=back):
            part = rows_of(step)
            value = back * silu_grad(upper[part, cols])
            normed = (hidden[part, cols] - mean) * scale
            upper[part, cols] = value
            return (so_far[0] + col_sum(value), so_far[1] + col_sum(value * normed))

        zero = jnp.zeros((1, width), F32)
        first, second = lax.fori_loop(0, rows // CHUNK, backward, (zero, zero))
        out_sums[0:1, cols] = first
        out_sums[1:2, cols] = second
    out_sums[2:3, :] = jnp.broadcast_to(loss[...], (1, out_sums.shape[1]))


def lower(upper, hidden, sums, back_sums, norms, count, part, cols):
    mean, scale = statistics(sums, count, cols)
    normed = (hidden[part, cols] - mean) * scale
    slope = scale * norms[0:1, cols]
    return slope * (
        upper[part, cols] - back_sums[0:1, cols] / count - normed * (back_sums[1:2, cols] / count)
    )


def back_three_kernel(
    count, me, upper, hidden, sums, norms, back_sums, weights, hidden_two, sums_two, norms_two, down, out, out_sums
):
    rows, wide = upper.shape
    for start in range(0, wide, 512):
        cols = slice(start, start + 512)
        for step in range(rows // CHUNK):
            part = slice(step * CHUNK, (step + 1) * CHUNK)
            down[part, cols] = lower(
                upper, hidden, sums, back_sums, norms, count, part, cols
            ).astype(BF16)
    for start in range(0, out.shape[1], 256):
        cols = slice(start, start + 256)
        value = dot(down[...], weights[cols, :], ((1,), (1,)))
        finish(value, hidden_two, sums_two, norms_two, count, cols, out, out_sums)


def finish(value, hidden, sums, norms, count, cols, out, out_sums):
    mean, scale = statistics(sums, count, cols)
    normed = (hidden[:, cols] - mean) * scale
    value = value * silu_grad(normed * norms[0:1, cols] + norms[1:2, cols])
    out[:, cols] = value
    out_sums[0:1, cols] = col_sum(value)
    out_sums[1:2, cols] = col_sum(value * normed)


def back_two_kernel(
    count, size, group, me, upper, hidden, sums, norms, back_sums, weights, hidden_one, sums_one, norms_one,
    down, out, out_sums, pad, cols,
):
    rows, width = upper.shape
    line = size * group
    pad[1, 0:line, :] = jnp.zeros((line, width), F32)
    pad[1, line + rows :, :] = jnp.zeros((line, width), F32)
    for step in range(rows // CHUNK):
        part = slice(step * CHUNK, (step + 1) * CHUNK)
        value = lower(upper, hidden, sums, back_sums, norms, count, part, slice(None)).astype(BF16)
        down[part, :] = value
        pad[1, line + step * CHUNK : line + (step + 1) * CHUNK, :] = value.astype(F32)
    fill(pad, size, group)
    windows(pad, cols, size, group)
    for start in range(0, out.shape[1], 256):
        block = slice(start, start + 256)
        value = None
        for tap in range(9):
            base = (8 - tap) * out.shape[1] + start
            term = dot(
                cols[:, tap * width : (tap + 1) * width],
                weights[base : base + 256, :],
                ((1,), (1,)),
            )
            value = term if value is None else value + term
        finish(value, hidden_one, sums_one, norms_one, count, block, out, out_sums)


def spread_blocks(number, c, outs, block):
    for k, out in enumerate(outs):
        for a in range(out.shape[0]):
            other = number ^ (8 * a + k)
            out[a] = block(lax.div(other, c), lax.rem(other, c))


def at(index, size):
    return pl.ds(pl.multiple_of(index * size, size), size)


def grad_out_kernel(c, me, act, down, *refs):
    *outs, whole = refs
    for start in range(0, whole.shape[1], 512):
        cols = slice(start, start + 512)
        whole[:, cols] = dot(act[...], down[:, cols], ((0,), (0,))).astype(BF16)
    rows, width = outs[0].shape[1:]
    spread_blocks(
        me[0] * c + me[1], c, outs, lambda i, j: whole[at(j, rows), at(i, width)]
    )


def grad_mid_kernel(c, me, cols, down, *refs):
    *outs, whole = refs
    depth = whole.shape[1]
    for tap in range(9):
        whole[tap] = dot(
            cols[:, tap * depth : (tap + 1) * depth], down[...], ((0,), (0,))
        ).astype(BF16)
    rows, width = outs[0].shape[2:]
    spread_blocks(
        me[0] * c + me[1], c, outs, lambda i, j: whole[:, at(i, rows), at(j, width)]
    )


def grad_in_kernel(count, c, me, upper, hidden, sums, norms, back_sums, *refs):
    features, outs, whole, down = refs[:c], refs[c:-2], refs[-2], refs[-1]
    rows = upper.shape[0]
    for step in range(rows // CHUNK):
        part = slice(step * CHUNK, (step + 1) * CHUNK)
        down[part, :] = lower(
            upper, hidden, sums, back_sums, norms, count, part, slice(None)
        ).astype(BF16)
    depth = features[0].shape[1]
    for k, part in enumerate(features):
        whole[at(me[1] ^ k, depth), :] = dot(part[...], down[...], ((0,), (0,))).astype(BF16)
    height, width = outs[0].shape[1:]
    spread_blocks(
        me[0] * c + me[1], c, outs, lambda i, j: whole[at(i, height), at(j, width)]
    )


def call_with_scratch(kernel, outs, scratch, *inputs, flops=0):
    moved = sum(x.size * x.dtype.itemsize for x in inputs)
    shapes = [jax.ShapeDtypeStruct(*out) for out in outs]
    moved += sum(s.size * s.dtype.itemsize for s in shapes)
    return pl.pallas_call(
        kernel,
        out_shape=shapes,
        in_specs=[pl.BlockSpec(memory_space=pltpu.SMEM)]
        + [pl.BlockSpec(memory_space=pltpu.VMEM)] * (len(inputs) - 1),
        out_specs=[pl.BlockSpec(memory_space=pltpu.VMEM)] * len(outs),
        scratch_shapes=[pltpu.VMEM(*one) for one in scratch],
        compiler_params=pltpu.CompilerParams(vmem_limit_bytes=56 * 2**20),
        cost_estimate=pl.CostEstimate(flops=flops, bytes_accessed=moved, transcendentals=0),
    )(*inputs)


def advance(weight, grad, momentum, average, rate):
    fresh = MOMENTUM * momentum + grad
    weight_new = weight - rate * (grad + MOMENTUM * fresh)
    return (weight_new, fresh, AVERAGE * average + (1.0 - AVERAGE) * weight_new)


def ordered(parts, number, n):
    stacked = jnp.stack(parts, axis=1)
    stacked = stacked.reshape((n,) + parts[0].shape[1:])
    return jnp.take(stacked, jnp.arange(n) ^ number, axis=0)


def relative(blocks, number, n):
    blocks = jnp.take(blocks, jnp.arange(n) ^ number, axis=0)
    blocks = blocks.reshape((n // 8, 8) + blocks.shape[1:])
    return [blocks[:, k] for k in range(8)]


def shards(
    d,
    c,
    features,
    labels,
    class_weights,
    conv_in,
    conv_mid,
    conv_out,
    classifier,
    norms,
    momentum_in,
    momentum_mid,
    momentum_out,
    momentum_head,
    momentum_norms,
    average_in,
    average_mid,
    average_out,
    average_head,
    average_norms,
):
    n = d * c
    dp, chan = lax.axis_index("dp"), lax.axis_index("chan")
    number = dp * c + chan
    me = jnp.stack([dp, chan]).astype(jnp.int32)
    images, size = features.shape[0], features.shape[1]
    group = images // c
    pixels = size * size
    count = float(images * pixels * d)
    rows = pixels * group
    deep = features.shape[3]
    mid, wide = conv_in.shape[1] * c, deep * c
    aligned = conv_out.shape[1] % LANES == 0

    laid = features.transpose(1, 2, 0, 3).reshape(pixels, c, group, deep)
    laid = laid.transpose(1, 0, 2, 3).reshape(c, rows, deep)
    pieces = [lax.dynamic_index_in_dim(laid, chan ^ k, 0, keepdims=False) for k in range(c)]
    pieces = [pieces[0]] + [swap(pieces[k], k, n) for k in range(1, c)]

    low_in = gather(conv_in.astype(BF16), n)
    fan_in, fan_out = conv_mid.shape[2:]
    low_mid = gather(conv_mid.astype(BF16).reshape(9, fan_in, fan_out), n)
    low_out = gather(conv_out.astype(BF16), n)
    classes = classifier.shape[1]
    space = -(-classes // LANES) * LANES
    low_head = gather(jnp.pad(classifier.astype(BF16), ((0, 0), (0, space - classes))), n)

    table = norms[:, 0]
    tables = jnp.stack([table] + [swap(table, k, n) for k in range(1, c)])
    tables = jnp.take(tables, jnp.arange(c) ^ chan, axis=0).transpose(1, 0, 2)
    narrow = conv_in.shape[1]
    norms_one = tables[:, :, :narrow].reshape(2, mid)
    norms_two = tables[:, :, narrow : 2 * narrow].reshape(2, mid)
    norms_three = tables[:, :, 2 * narrow :].reshape(2, wide)

    own = lax.dynamic_index_in_dim(labels.reshape(c, group), chan, 0, keepdims=False)
    own = jnp.concatenate([own, own])
    catalog = lax.broadcasted_iota(jnp.int32, (2 * group, class_weights.shape[0]), 1)
    chosen = catalog == own[:, None]
    weight_row = jnp.sum(jnp.where(chosen, class_weights[None, :], 0), axis=1).astype(F32)
    target = jnp.pad(
        chosen.astype(F32).reshape(2 * group, c, classes), ((0, 0), (0, 0), (0, space - classes))
    ).reshape(2 * group, c * space)
    own_weight = (0.5 * jnp.sum(weight_row)).reshape(1, 1)

    def assembled(parts, shape, kernel):
        if aligned:
            return call(functools.partial(kernel, c), [(shape, BF16)], me, *parts)[0]
        blocks = ordered(parts, number, n)
        blocks = blocks.reshape((d, c) + blocks.shape[1:])
        if kernel is assemble_out_kernel:
            return blocks.transpose(1, 2, 0, 3).reshape(shape)
        if len(shape) == 3:
            return blocks.transpose(2, 0, 3, 1, 4).reshape(shape)
        return blocks.transpose(0, 2, 1, 3).reshape(shape)

    whole_in = assembled(low_in, (wide, mid), assemble_kernel)
    hidden_one, sums_one = call(
        first_kernel, [((rows, mid), F32), ((3, mid), F32)], me, own_weight, *pieces, whole_in,
        flops=2 * rows * wide * mid,
    )
    sums_one = total(sums_one, n)
    weight_sum = sums_one[2, 0]

    whole_mid = assembled(low_mid, (9, mid, mid), assemble_kernel).reshape(9 * mid, mid)
    line = size * group
    padded = ((3, rows + 2 * line, mid), F32)
    cols, hidden_two, sums_two = call_with_scratch(
        functools.partial(second_kernel, count, size, group),
        [((rows, 9 * mid), BF16), ((rows, mid), F32), ((2, mid), F32)],
        [padded],
        me, hidden_one, sums_one, norms_one, whole_mid,
        flops=18 * rows * mid * mid,
    )
    sums_two = total(sums_two, n)

    whole_out = assembled(low_out, (mid, wide), assemble_out_kernel)
    act_two, hidden_three, sums_three = call(
        functools.partial(third_kernel, count),
        [((rows, mid), BF16), ((rows, wide), F32), ((2, wide), F32)],
        me, hidden_two, sums_two, norms_two, whole_out,
        flops=2 * rows * mid * wide,
    )
    sums_three = total(sums_three, n)

    whole_head = assembled(low_head, (wide, c * space), assemble_kernel)
    row_weights = jnp.stack([weight_row, weight_row / weight_sum], axis=1)
    upper_three, back_three, packed, _ = call(
        functools.partial(head_kernel, count, pixels, group, classes),
        [((rows, wide), F32), ((3, wide), F32), ((2 * group, wide + c * space), BF16), ((1, 1), F32)],
        me, hidden_three, sums_three, norms_three, row_weights, target, whole_head, *pieces,
        flops=4 * 8 * wide * c * space,
    )
    everything = lax.all_gather(packed[:group], AXES, axis=0, tiled=True)
    back_three = total(back_three, n)
    loss_sum = back_three[2, 0]

    down_three, upper_two, back_two = call(
        functools.partial(back_three_kernel, count),
        [((rows, wide), BF16), ((rows, mid), F32), ((2, mid), F32)],
        me, upper_three, hidden_three, sums_three, norms_three, back_three, whole_out,
        hidden_two, sums_two, norms_two,
        flops=2 * rows * mid * wide,
    )
    back_two = total(back_two, n)

    def blocks_of(shape):
        return [((n // 8,) + shape, BF16)] * 8

    if aligned:
        parts_out = call_with_scratch(
            functools.partial(grad_out_kernel, c), blocks_of(conv_out.shape), [((mid, wide), BF16)],
            me, act_two, down_three, flops=2 * rows * mid * wide,
        )
    else:
        whole = dot(act_two, down_three, ((0,), (0,))).astype(BF16)
        whole = whole.reshape((c, conv_out.shape[0], d, conv_out.shape[1])).transpose(2, 0, 1, 3)
        parts_out = relative(whole.reshape((n,) + conv_out.shape), number, n)
    grad_out = scatter_sum(parts_out, n)

    down_two, upper_one, back_one = call_with_scratch(
        functools.partial(back_two_kernel, count, size, group),
        [((rows, mid), BF16), ((rows, mid), F32), ((2, mid), F32)],
        [padded, ((rows, 9 * mid), BF16)],
        me, upper_two, hidden_two, sums_two, norms_two, back_two, whole_mid,
        hidden_one, sums_one, norms_one,
        flops=18 * rows * mid * mid,
    )
    back_one = total(back_one, n)

    shard_mid = (9, fan_in, fan_out)
    parts_mid = call_with_scratch(
        functools.partial(grad_mid_kernel, c), blocks_of(shard_mid), [((9, mid, mid), BF16)],
        me, cols, down_two, flops=18 * rows * mid * mid,
    )
    grad_mid = scatter_sum(parts_mid, n).reshape(conv_mid.shape)

    parts_in = call_with_scratch(
        functools.partial(grad_in_kernel, count, c), blocks_of(conv_in.shape),
        [((wide, mid), BF16), ((rows, mid), BF16)],
        me, upper_one, hidden_one, sums_one, norms_one, back_one, *pieces,
        flops=2 * rows * mid * wide,
    )
    grad_in = scatter_sum(parts_in, n)

    height = classifier.shape[0]
    pooled = lax.dynamic_slice_in_dim(everything, dp * height, height, axis=1)
    upper_logits = lax.dynamic_slice_in_dim(everything, wide + chan * space, space, axis=1)
    grad_head = dot(pooled, upper_logits, ((0,), (0,)))[:, :classes]

    def mine(sums, width):
        return lax.dynamic_slice_in_dim(sums[:2], chan * width, width, axis=1)[::-1]

    grad_norms = jnp.concatenate(
        [mine(back_one, narrow), mine(back_two, narrow), mine(back_three, deep)], axis=1
    )[:, None, :]
    params = (conv_in, conv_mid, conv_out, classifier, norms)
    grads = (grad_in, grad_mid, grad_out, grad_head, grad_norms)
    moments = (momentum_in, momentum_mid, momentum_out, momentum_head, momentum_norms)
    averages = (average_in, average_mid, average_out, average_head, average_norms)
    rates = (RATE_MATRIX, RATE_MATRIX, RATE_MATRIX, RATE_MATRIX, RATE_NORM)
    results = [
        advance(p, g, m, a, r) for p, g, m, a, r in zip(params, grads, moments, averages, rates)
    ]
    news = [item[0] for item in results]
    freshs = [item[1] for item in results]
    means = [item[2] for item in results]
    copies = [item.astype(BF16) for item in news]
    return (loss_sum, weight_sum, *news, *freshs, *means, *copies)


def solution(mesh):
    matrices = (P("dp", "chan"), P(None, None, "dp", "chan"), P("chan", "dp"), P("dp", "chan"), P(None, "chan", None))
    return jax.shard_map(
        functools.partial(shards, mesh.shape["dp"], mesh.shape["chan"]),
        mesh=mesh,
        in_specs=(P("dp", None, None, "chan"), P("dp"), P()) + matrices * 3,
        out_specs=(P(), P()) + matrices * 4,
        check_vma=False,
    )
```

time: 712 us -> 391 us (0.55); the launches traced: 702 us -> 390 us
  blocking collectives: 262 us -> 42 us
  waiting for transfers between devices: 251 us -> 118 us
  starting transfers between devices: 0.92 us -> 113 us
  Pallas kernels: 0 us -> 71.4 us
  local copies, waits for them, and re-layouts: 74.2 us -> 18 us
  matrix products: 56.3 us -> 1.01 us
  other arithmetic: 42.4 us -> 24 us
  between operations: 15.7 us -> 2.5 us
    reduce_scatter x6 -> x0, waiting for transfers between devices: 158 us -> none  [the longest x1 61.4 us: shards(): lax.psum_scatter(grad_in.astype(jnp.bfloat16), 'dp', scatter_dimension=0,...]
    psum x7 -> x0, blocking collectives: 148 us -> none  [the longest x3 64.9 us: norm_forward(): lax.psum((jnp.sum(hidden, axis=(0, 1, 2)), jnp.sum(hidden * hidden, axis=...]
    ppermute x0 -> x118, waiting for transfers between devices: none -> 118 us  [swap(): return lax.ppermute(array, AXES, [(d, d ^ mask) for d in range(n)])]
    ppermute x0 -> x118, starting transfers between devices: none -> 113 us  [swap(): return lax.ppermute(array, AXES, [(d, d ^ mask) for d in range(n)])]
    pallas_call x0 -> x13, Pallas kernels: none -> 71.4 us  [the longest x8 42.7 us: call(): pl.pallas_call(kernel, out_shape=shapes, in_specs=[pl.BlockSpec(memory_sp...]
    all_gather x4 -> x1, blocking collectives: 107 us -> 42 us  [shards(): everything = lax.all_gather(packed[:group], AXES, axis=0, tiled=True)]
    all_gather x4 -> x0, waiting for transfers between devices: 62.3 us -> none  [the longest x1 39.9 us: shards(): sent = lax.all_gather(low_three, 'chan', axis=3, tiled=True)]
    unnamed x132 -> x152, local copies, waits for them, and re-layouts: 65.6 us -> 6.47 us
  transfers between devices with their start and end apart: 11 -> 118, of which waited for: 9 -> 41; matrix products, arithmetic and copies ran while one was open for 16% -> 9% of each run, Pallas kernels for 0% -> 12%
where the time goes in v1:
time: 391 us; the launch traced here: 390 us
  waiting for transfers between devices  118 us (30%)
  starting transfers between devices  113 us (29%)
  Pallas kernels  71.4 us (18%)
  blocking collectives  42 us (11%)
  other arithmetic  24 us (6%)
  local copies, waits for them, and re-layouts  18 us (5%)
    ppermute x118, waiting for transfers between devices, swap(): return lax.ppermute(array, AXES, [(d, d ^ mask) for d in range(n)])  118 us
    ppermute x118, starting transfers between devices, swap(): return lax.ppermute(array, AXES, [(d, d ^ mask) for d in range(n)])  113 us
    pallas_call x8, Pallas kernels, call(): pl.pallas_call(kernel, out_shape=shapes, in_specs=[pl.BlockSpec(memory_sp...  42.7 us
    all_gather x1, blocking collectives, shards(): everything = lax.all_gather(packed[:group], AXES, axis=0, tiled=True)  42 us
    pallas_call x5, Pallas kernels, call_with_scratch(): pl.pallas_call(kernel, out_shape=shapes, in_specs=[pl.BlockSpec(memory_sp...  28.7 us
  transfers between devices with their start and end apart: 118, of which 41 were waited for; matrix products, arithmetic and copies ran while one was open for 9% of the time, Pallas kernels for 12%

profile of v1, /device:TPU:0, one launch (start us, length us, event | category | flops | bytes accessed | tf_op | source)
XLA Modules:
  0.0 389.8 jit_solution(17111346948397533941)
XLA Ops:
  1.6 4.0 %collective-permute-start.4 = (bf16[256,128]{1,0:T(8,128)(2,1)S(1)}, bf16[256,128]{1,0:T(8,128)(2,1)S(1)}, u32[]{:S(2)}, u32[]{:S(2)}) collective-permute-start(bf16[256,128]{1,0:T(8,128)(2,1)S(1)} %convert_element_type.249), channel_id=1, source_target_pairs={{0,16},{1,17},{2,18},{3,19},{4,20},{5,21},{6,22},{7,23},{8,24},{9,... | collective-permute-start | bytes 196616 | tf_op jit(solution)/shard_map/ppermute | solution.py:23
  8.8 3.8 collective-permute-start.25
  15.9 2.5 collective-permute-start.11
  18.5 3.0 reshape.139
  38.6 3.3 shard_map.345.refs_4_
  42.5 7.3 %collective-permute-done.1.refs_2_ = bf16[400,512]{1,0:T(8,128)(2,1)S(1)} collective-permute-done((bf16[400,512]{1,0:T(8,128)(2,1)}, bf16[400,512]{1,0:T(8,128)(2,1)S(1)}, u32[]{:S(2)}, u32[]{:S(2)}) %collective-permute-start.1) | collective-permute-done | bytes 409632 | tf_op jit(solution)/shard_map/ppermute | solution.py:23
  50.8 4.1 %shard_map.346 = (f32[400,512]{1,0:T(8,128)}, f32[3,512]{1,0:T(4,128)}) custom-call(s32[2]{0:T(128)} %pad_add_fusion.refs_0_.me, f32[1,1]{1,0:T(1,128)} %bitcast.3.weight_sum, bf16[400,512]{1,0:T(8,128)(2,1)} %get-tuple-element.209.refs_0_, bf16[400,512]{1,0:T(8,128)(2,1)} %copy-done.2, bf16[400,512]{1,0:T(8,128)(2,1)} %copy-done.1, ...), custom_call_target="tpu_custom_call" | custom-call | flops 838860800 | bytes 4560908 | tf_op jit(solution)/shard_map/pallas_call | solution.py:65
  58.6 2.9 collective-permute-start.41
  61.5 13.8 %collective-permute-done.22 = f32[2,768]{1,0:T(2,128)S(1)} collective-permute-done((f32[2,768]{1,0:T(2,128)S(1)}, f32[2,768]{1,0:T(2,128)S(1)}, u32[]{:S(2)}, u32[]{:S(2)}) %collective-permute-start.22) | collective-permute-done | bytes 6176 | tf_op jit(solution)/shard_map/ppermute | solution.py:23
  77.5 2.4 collective-permute-done.16
  83.6 2.4 collective-permute-start.42
  86.0 3.6 collective-permute-done.42
  89.6 2.5 collective-permute-start.19
  92.8 2.3 collective-permute-done.19
  95.7 3.9 %collective-permute-done.18 = f32[3,512]{1,0:T(4,128)S(1)} collective-permute-done((f32[3,512]{1,0:T(4,128)S(1)}, f32[3,512]{1,0:T(4,128)S(1)}, u32[]{:S(2)}, u32[]{:S(2)}) %collective-permute-start.18) | collective-permute-done | bytes 6176 | tf_op jit(solution)/shard_map/ppermute | solution.py:23
  100.6 2.8 collective-permute-done.17
  110.6 5.4 %shard_map.347 = bf16[9,512,512]{2,1,0:T(8,128)(2,1)} custom-call(s32[2]{0:T(128)} %pad_add_fusion.refs_0_.me, bf16[4,9,64,128]{3,2,1,0:T(8,128)(2,1)} %copy-done.3, bf16[4,9,64,128]{3,2,1,0:T(8,128)(2,1)} %copy-done.15, bf16[4,9,64,128]{3,2,1,0:T(8,128)(2,1)} %collective-permute-done.27.refs_3_, bf16[4,9,64,128]{3,2,1,0:T(8,128)(2,1)} %copy-done.18, ...), custom_call_target="tpu_custom_call" | custom-call | bytes 9437192 | tf_op jit(solution)/shard_map/pallas_call | solution.py:65
  116.0 6.2 %shard_map.348 = (bf16[400,4608]{1,0:T(8,128)(2,1)}, f32[400,512]{1,0:T(8,128)}, f32[2,512]{1,0:T(2,128)}) custom-call(s32[2]{0:T(128)} %pad_add_fusion.refs_0_.me, f32[400,512]{1,0:T(8,128)} %get-tuple-element.63.hidden.hidden_one, f32[3,512]{1,0:T(4,128)} %add_add_fusion.4.sums.sums_one, f32[2,512]{1,0:T(2,128)} %get-tuple-element.222.norms.norms_one, ...), custom_call_target="tpu_custom_call" | custom-call | flops 1887436800 | bytes 10057736 | tf_op jit(solution)/shard_map/pallas_call | solution.py:394
  133.2 4.8 %collective-permute-done.59 = bf16[256,256]{1,0:T(8,128)(2,1)S(1)} collective-permute-done((bf16[256,256]{1,0:T(8,128)(2,1)S(1)}, bf16[256,256]{1,0:T(8,128)(2,1)S(1)}, u32[]{:S(2)}, u32[]{:S(2)}) %collective-permute-start.59) | collective-permute-done | bytes 131104 | tf_op jit(solution)/shard_map/ppermute | solution.py:23
  146.1 3.0 shard_map.349.weights
  149.8 4.7 %shard_map.350 = (bf16[400,512]{1,0:T(8,128)(2,1)}, f32[400,2048]{1,0:T(8,128)}, f32[2,2048]{1,0:T(2,128)}) custom-call(s32[2]{0:T(128)} %pad_add_fusion.refs_0_.me, f32[400,512]{1,0:T(8,128)} %get-tuple-element.65.hidden.hidden_two, f32[2,512]{1,0:T(2,128)} %add_add_fusion.10.sums.sums_two, f32[2,512]{1,0:T(2,128)} %get-tuple-element.221.norms.norms_two, ...), custom_call_target="tpu_custom_call" | custom-call | flops 838860800 | bytes 6627336 | tf_op jit(solution)/shard_map/pallas_call | solution.py:65
  159.3 4.6 %collective-permute-done.63.refs_5_ = bf16[4,256,256]{2,1,0:T(8,128)(2,1)S(1)} collective-permute-done((bf16[4,256,256]{2,1,0:T(8,128)(2,1)S(1)}, bf16[4,256,256]{2,1,0:T(8,128)(2,1)S(1)}, u32[]{:S(2)}, u32[]{:S(2)}) %collective-permute-start.63) | collective-permute-done | bytes 524320 | tf_op jit(solution)/shard_map/ppermute | solution.py:23
  168.1 2.8 collective-permute-start.56
  174.1 4.8 %shard_map.351.weights = bf16[2048,1024]{1,0:T(8,128)(2,1)} custom-call(s32[2]{0:T(128)} %pad_add_fusion.refs_0_.me, bf16[4,256,256]{2,1,0:T(8,128)(2,1)} %copy-done.4, bf16[4,256,256]{2,1,0:T(8,128)(2,1)} %copy-done.26, bf16[4,256,256]{2,1,0:T(8,128)(2,1)} %copy-done.25, bf16[4,256,256]{2,1,0:T(8,128)(2,1)} %collective-permute-done.62.refs_4_, ...), custom_call_target="tpu_custom_call" | custom-call | bytes 8388616 | tf_op jit(solution)/shard_map/pallas_call | solution.py:65
  179.5 11.2 %shard_map.352 = (f32[400,2048]{1,0:T(8,128)}, f32[3,2048]{1,0:T(4,128)}, bf16[8,3072]{1,0:T(8,128)(2,1)}, f32[1,1]{1,0:T(1,128)}) custom-call(s32[2]{0:T(128)} %pad_add_fusion.refs_0_.me, f32[400,2048]{1,0:T(8,128)} %get-tuple-element.67.hidden, f32[2,2048]{1,0:T(2,128)} %add_add_fusion.2.sums, f32[2,2048]{1,0:T(2,128)} %bitcast.124, ...), custom_call_target="tpu_custom_call" | custom-call | flops 67108864 | bytes 12525644 | tf_op jit(solution)/shard_map/pallas_call | solution.py:65
  199.8 2.5 collective-permute-start.73
  204.3 42.0 %all-gather = bf16[32,4,3072]{2,1,0:T(4,128)(2,1)S(1)} all-gather(bf16[1,4,3072]{2,1,0:T(4,128)(2,1)S(1)} %slice_bitcast_fusion.12), channel_id=1, replica_groups=mesh['dp'=8,'chan'=4] {'dp','chan'}, dimensions={0}, use_global_device_ids=true | all-gather | bytes 811008 | tf_op jit(solution)/shard_map/all_gather | solution.py:538
  247.1 6.3 %shard_map.353 = (bf16[400,2048]{1,0:T(8,128)(2,1)}, f32[400,512]{1,0:T(8,128)}, f32[2,512]{1,0:T(2,128)}) custom-call(s32[2]{0:T(128)} %pad_add_fusion.refs_0_.me, f32[400,2048]{1,0:T(8,128)} %get-tuple-element.70.upper, f32[400,2048]{1,0:T(8,128)} %get-tuple-element.67.hidden, f32[2,2048]{1,0:T(2,128)} %add_add_fusion.2.sums, f32[2,2048]{1,0:T(2,128)} %bitcast.125, ...), custom_call_target="tpu_custom_call" | custom-call | flops 838860800 | bytes 11997192 | tf_op jit(solution)/shard_map/pallas_call | solution.py:65
  255.0 3.4 collective-permute-start.75
  260.2 4.3 %collective-permute-start.78 = (f32[2,512]{1,0:T(2,128)S(1)}, f32[2,512]{1,0:T(2,128)S(1)}, u32[]{:S(2)}, u32[]{:S(2)}) collective-permute-start(f32[2,512]{1,0:T(2,128)S(1)} %add_add_fusion.9), channel_id=1, source_target_pairs={{0,8},{1,9},{2,10},{3,11},{4,12},{5,13},{6,14},{7,15},{8,0},{9,1},... | collective-permute-start | bytes 12296 | tf_op jit(solution)/shard_map/ppermute | solution.py:23
  266.7 6.4 %shard_map.354 = (bf16[400,512]{1,0:T(8,128)(2,1)}, f32[400,512]{1,0:T(8,128)}, f32[2,512]{1,0:T(2,128)}) custom-call(s32[2]{0:T(128)} %pad_add_fusion.refs_0_.me, f32[400,512]{1,0:T(8,128)} %get-tuple-element.71.upper, f32[400,512]{1,0:T(8,128)} %get-tuple-element.65.hidden.hidden_two, f32[2,512]{1,0:T(2,128)} %add_add_fusion.10.sums.sums_two, ...), custom_call_target="tpu_custom_call" | custom-call | flops 1887436800 | bytes 8431624 | tf_op jit(solution)/shard_map/pallas_call | solution.py:394
  273.1 4.2 %shard_map.357 = (bf16[4,128,256]{2,1,0:T(8,128)(2,1)}, bf16[4,128,256]{2,1,0:T(8,128)(2,1)}, bf16[4,128,256]{2,1,0:T(8,128)(2,1)}, bf16[4,128,256]{2,1,0:T(8,12...) custom-call(s32[2]{0:T(128)} %pad_add_fusion.refs_0_.me, ...), custom_call_target="tpu_custom_call" | custom-call | flops 838860800 | bytes 4145160 | tf_op jit(solution)/shard_map/pallas_call | solution.py:394
  282.1 7.1 %shard_map.356 = (bf16[4,9,64,128]{3,2,1,0:T(8,128)(2,1)}, bf16[4,9,64,128]{3,2,1,0:T(8,128)(2,1)}, bf16[4,9,64,128]{3,2,1,0:T(8,128)(2,1)}, bf16[4,9,64,128]{3,...) custom-call(s32[2]{0:T(128)} %pad_add_fusion.refs_0_.me, ...), custom_call_target="tpu_custom_call" | custom-call | flops 1887436800 | bytes 8814600 | tf_op jit(solution)/shard_map/pallas_call | solution.py:394
  289.3 2.4 collective-permute-start.87
  297.1 4.7 %shard_map.355 = (bf16[4,256,128]{2,1,0:T(8,128)(2,1)}, bf16[4,256,128]{2,1,0:T(8,128)(2,1)}, bf16[4,256,128]{2,1,0:T(8,128)(2,1)}, bf16[4,256,128]{2,1,0:T(8,12...) custom-call(s32[2]{0:T(128)} %pad_add_fusion.refs_0_.me, ...), custom_call_target="tpu_custom_call" | custom-call | flops 838860800 | bytes 5388296 | tf_op jit(solution)/shard_map/pallas_call | solution.py:394
  309.9 4.0 %collective-permute-done.110 = bf16[4,128,256]{2,1,0:T(8,128)(2,1)S(1)} collective-permute-done((bf16[4,128,256]{2,1,0:T(8,128)(2,1)S(1)}, bf16[4,128,256]{2,1,0:T(8,128)(2,1)S(1)}, u32[]{:S(2)}, u32[]{:S(2)}) %collective-permute-start.110) | collective-permute-done | bytes 262176 | tf_op jit(solution)/shard_map/ppermute | solution.py:23
  315.9 4.8 %collective-permute-done.112 = bf16[4,128,256]{2,1,0:T(8,128)(2,1)S(1)} collective-permute-done((bf16[4,128,256]{2,1,0:T(8,128)(2,1)S(1)}, bf16[4,128,256]{2,1,0:T(8,128)(2,1)S(1)}, u32[]{:S(2)}, u32[]{:S(2)}) %collective-permute-start.112) | collective-permute-done | bytes 262176 | tf_op jit(solution)/shard_map/ppermute | solution.py:23
  325.2 8.5 %collective-permute-done.92 = bf16[4,256,128]{2,1,0:T(8,128)(2,1)S(1)} collective-permute-done((bf16[4,256,128]{2,1,0:T(8,128)(2,1)S(1)}, bf16[4,256,128]{2,1,0:T(8,128)(2,1)S(1)}, u32[]{:S(2)}, u32[]{:S(2)}) %collective-permute-start.92) | collective-permute-done | bytes 262176 | tf_op jit(solution)/shard_map/ppermute | solution.py:23
  335.1 2.4 collective-permute-start.117
  340.5 2.4 collective-permute-start.97
  344.3 3.4 collective-permute-start.104
  349.2 4.5 %collective-permute-done.96 = bf16[256,128]{1,0:T(8,128)(2,1)S(1)} collective-permute-done((bf16[256,128]{1,0:T(8,128)(2,1)S(1)}, bf16[256,128]{1,0:T(8,128)(2,1)S(1)}, u32[]{:S(2)}, u32[]{:S(2)}) %collective-permute-start.96) | collective-permute-done | bytes 65568 | tf_op jit(solution)/shard_map/ppermute | solution.py:23
  354.4 4.7 %collective-permute-done.100 = bf16[4,9,64,128]{3,2,1,0:T(8,128)(2,1)S(1)} collective-permute-done((bf16[4,9,64,128]{3,2,1,0:T(8,128)(2,1)S(1)}, bf16[4,9,64,128]{3,2,1,0:T(8,128)(2,1)S(1)}, u32[]{:S(2)}, u32[]{:S(2)}) %collective-permute-start.100) | collective-permute-done | bytes 589856 | tf_op jit(solution)/shard_map/ppermute | solution.py:23
  359.1 12.7 %collective-permute-done.102 = bf16[4,9,64,128]{3,2,1,0:T(8,128)(2,1)S(1)} collective-permute-done((bf16[4,9,64,128]{3,2,1,0:T(8,128)(2,1)S(1)}, bf16[4,9,64,128]{3,2,1,0:T(8,128)(2,1)S(1)}, u32[]{:S(2)}, u32[]{:S(2)}) %collective-permute-start.102) | collective-permute-done | bytes 589856 | tf_op jit(solution)/shard_map/ppermute | solution.py:23
  372.6 2.4 collective-permute-start.107
  376.7 3.2 collective-permute-done.105
  379.9 2.8 collective-permute-done.107
  382.7 5.3 %collective-permute-done.106 = bf16[9,64,128]{2,1,0:T(8,128)(2,1)S(1)} collective-permute-done((bf16[9,64,128]{2,1,0:T(8,128)(2,1)S(1)}, bf16[9,64,128]{2,1,0:T(8,128)(2,1)S(1)}, u32[]{:S(2)}, u32[]{:S(2)}) %collective-permute-start.106) | collective-permute-done | bytes 147488 | tf_op jit(solution)/shard_map/ppermute | solution.py:23
  (444 shorter events, 130.7 us)
Async XLA Ops:
  1.6 14.3 %collective-permute-start.4 = (bf16[256,128]{1,0:T(8,128)(2,1)S(1)}, bf16[256,128]{1,0:T(8,128)(2,1)S(1)}, u32[]{:S(2)}, u32[]{:S(2)}) collective-permute-start(bf16[256,128]{1,0:T(8,128)(2,1)S(1)} %convert_element_type.249), channel_id=1, source_target_pairs={{0,16},{1,17},{2,18},{3,19},{4,20},{5,21},{6,22},{7,23},{8,24},{9,... | collective-permute-start | bytes 196616 | tf_op jit(solution)/shard_map/ppermute | solution.py:23
  5.6 10.2 %collective-permute-start.3 = (bf16[256,128]{1,0:T(8,128)(2,1)S(1)}, bf16[256,128]{1,0:T(8,128)(2,1)S(1)}, u32[]{:S(2)}, u32[]{:S(2)}) collective-permute-start(bf16[256,128]{1,0:T(8,128)(2,1)S(1)} %convert_element_type.249), channel_id=1, source_target_pairs={{0,8},{1,9},{2,10},{3,11},{4,12},{5,13},{6,14},{7,15},{8,0},{9,1},... | collective-permute-start | bytes 196616 | tf_op jit(solution)/shard_map/ppermute | solution.py:23
  8.8 15.0 %collective-permute-start.25 = (bf16[9,64,128]{2,1,0:T(8,128)(2,1)}, bf16[9,64,128]{2,1,0:T(8,128)(2,1)}, u32[]{:S(2)}, u32[]{:S(2)}) collective-permute-start(bf16[9,64,128]{2,1,0:T(8,128)(2,1)} %bitcast.21), channel_id=1, source_target_pairs={{0,24},{1,25},{2,26},{3,27},{4,28},{5,29},{6,30},{7,31},{8,16},{9,... | collective-permute-start | bytes 442376 | tf_op jit(solution)/shard_map/ppermute | solution.py:23
  12.7 12.9 %collective-permute-start.24 = (bf16[9,64,128]{2,1,0:T(8,128)(2,1)}, bf16[9,64,128]{2,1,0:T(8,128)(2,1)}, u32[]{:S(2)}, u32[]{:S(2)}) collective-permute-start(bf16[9,64,128]{2,1,0:T(8,128)(2,1)} %bitcast.21), channel_id=1, source_target_pairs={{0,16},{1,17},{2,18},{3,19},{4,20},{5,21},{6,22},{7,23},{8,24},{9,... | collective-permute-start | bytes 442376 | tf_op jit(solution)/shard_map/ppermute | solution.py:23
  15.9 9.7 %collective-permute-start.11 = (bf16[4,256,128]{2,1,0:T(8,128)(2,1)S(1)}, bf16[4,256,128]{2,1,0:T(8,128)(2,1)}, u32[]{:S(2)}, u32[]{:S(2)}) collective-permute-start(bf16[4,256,128]{2,1,0:T(8,128)(2,1)S(1)} %pad_maximum_fusion.2.refs_1_), channel_id=1, source_target_pairs={{0,6},{1,7},{2,4},{3,5},{4,2},{5,3},{6,0},{7,1},{8,14},{9,15},{10,... | collective-permute-start | bytes 786440 | tf_op jit(solution)/shard_map/ppermute | solution.py:23
  29.3 12.7 %collective-permute-start.2 = (bf16[400,512]{1,0:T(8,128)(2,1)S(1)}, bf16[400,512]{1,0:T(8,128)(2,1)S(1)}, u32[]{:S(2)}, u32[]{:S(2)}) collective-permute-start(bf16[400,512]{1,0:T(8,128)(2,1)S(1)} %get-tuple-element.206), channel_id=1, source_target_pairs={{0,3},{1,2},{2,1},{3,0},{4,7},{5,6},{6,5},{7,4},{8,11},{9,10},{10,... | collective-permute-start | bytes 1228808 | tf_op jit(solution)/shard_map/ppermute | solution.py:23
  29.4 20.4 %collective-permute-start.1 = (bf16[400,512]{1,0:T(8,128)(2,1)}, bf16[400,512]{1,0:T(8,128)(2,1)S(1)}, u32[]{:S(2)}, u32[]{:S(2)}) collective-permute-start(bf16[400,512]{1,0:T(8,128)(2,1)} %get-tuple-element.207), channel_id=1, source_target_pairs={{0,2},{1,3},{2,0},{3,1},{4,6},{5,7},{6,4},{7,5},{8,10},{9,11},{10,... | collective-permute-start | bytes 1228808 | tf_op jit(solution)/shard_map/ppermute | solution.py:23
  30.9 18.9 %collective-permute-start = (bf16[400,512]{1,0:T(8,128)(2,1)}, bf16[400,512]{1,0:T(8,128)(2,1)S(1)}, u32[]{:S(2)}, u32[]{:S(2)}) collective-permute-start(bf16[400,512]{1,0:T(8,128)(2,1)} %get-tuple-element.208), channel_id=1, source_target_pairs={{0,1},{1,0},{2,3},{3,2},{4,5},{5,4},{6,7},{7,6},{8,9},{9,8},{10,11... | collective-permute-start | bytes 1228808 | tf_op jit(solution)/shard_map/ppermute | solution.py:23
  35.5 20.5 %collective-permute-start.21 = (f32[2,768]{1,0:T(2,128)S(1)}, f32[2,768]{1,0:T(2,128)S(1)}, u32[]{:S(2)}, u32[]{:S(2)}) collective-permute-start(f32[2,768]{1,0:T(2,128)S(1)} %bitcast.137), channel_id=1, source_target_pairs={{0,2},{1,3},{2,0},{3,1},{4,6},{5,7},{6,4},{7,5},{8,10},{9,11},{10,... | collective-permute-start | bytes 18440 | tf_op jit(solution)/shard_map/ppermute | solution.py:23
  37.1 55.0 %collective-permute-start.31 = (bf16[4,9,64,128]{3,2,1,0:T(8,128)(2,1)S(1)}, bf16[4,9,64,128]{3,2,1,0:T(8,128)(2,1)S(1)}, u32[]{:S(2)}, u32[]{:S(2)}) collective-permute-start(bf16[4,9,64,128]{3,2,1,0:T(8,128)(2,1)S(1)} %pad_maximum_fusion.refs_1_), channel_id=1, source_target_pairs={{0,6},{1,7},{2,4},{3,5},{4,2},{5,3},{6,0},{7,1},{8,14},{9,15},{10,... | collective-permute-start | bytes 1769480 | tf_op jit(solution)/shard_map/ppermute | solution.py:23
  42.0 50.2 %collective-permute-start.29 = (bf16[4,9,64,128]{3,2,1,0:T(8,128)(2,1)S(1)}, bf16[4,9,64,128]{3,2,1,0:T(8,128)(2,1)S(1)}, u32[]{:S(2)}, u32[]{:S(2)}) collective-permute-start(bf16[4,9,64,128]{3,2,1,0:T(8,128)(2,1)S(1)} %pad_maximum_fusion.refs_1_), channel_id=1, source_target_pairs={{0,4},{1,5},{2,6},{3,7},{4,0},{5,1},{6,2},{7,3},{8,12},{9,13},{10,... | collective-permute-start | bytes 1769480 | tf_op jit(solution)/shard_map/ppermute | solution.py:23
  49.9 42.8 %collective-permute-start.27 = (bf16[4,9,64,128]{3,2,1,0:T(8,128)(2,1)S(1)}, bf16[4,9,64,128]{3,2,1,0:T(8,128)(2,1)}, u32[]{:S(2)}, u32[]{:S(2)}) collective-permute-start(bf16[4,9,64,128]{3,2,1,0:T(8,128)(2,1)S(1)} %pad_maximum_fusion.refs_1_), channel_id=1, source_target_pairs={{0,2},{1,3},{2,0},{3,1},{4,6},{5,7},{6,4},{7,5},{8,10},{9,11},{10,... | collective-permute-start | bytes 1769480 | tf_op jit(solution)/shard_map/ppermute | solution.py:23
  57.0 18.4 %collective-permute-start.22 = (f32[2,768]{1,0:T(2,128)S(1)}, f32[2,768]{1,0:T(2,128)S(1)}, u32[]{:S(2)}, u32[]{:S(2)}) collective-permute-start(f32[2,768]{1,0:T(2,128)S(1)} %bitcast.139), channel_id=1, source_target_pairs={{0,3},{1,2},{2,1},{3,0},{4,7},{5,6},{6,5},{7,4},{8,11},{9,10},{10,... | collective-permute-start | bytes 18440 | tf_op jit(solution)/shard_map/ppermute | solution.py:23
  58.6 18.3 %collective-permute-start.41 = (bf16[128,256]{1,0:T(8,128)(2,1)S(1)}, bf16[128,256]{1,0:T(8,128)(2,1)S(1)}, u32[]{:S(2)}, u32[]{:S(2)}) collective-permute-start(bf16[128,256]{1,0:T(8,128)(2,1)S(1)} %convert_element_type.251), channel_id=1, source_target_pairs={{0,16},{1,17},{2,18},{3,19},{4,20},{5,21},{6,22},{7,23},{8,24},{9,... | collective-permute-start | bytes 196616 | tf_op jit(solution)/shard_map/ppermute | solution.py:23
  86.0 19.0 %collective-permute-start.26 = (bf16[4,9,64,128]{3,2,1,0:T(8,128)(2,1)S(1)}, bf16[4,9,64,128]{3,2,1,0:T(8,128)(2,1)S(1)}, u32[]{:S(2)}, u32[]{:S(2)}) collective-permute-start(bf16[4,9,64,128]{3,2,1,0:T(8,128)(2,1)S(1)} %pad_maximum_fusion.refs_1_), channel_id=1, source_target_pairs={{0,1},{1,0},{2,3},{3,2},{4,5},{5,4},{6,7},{7,6},{8,9},{9,8},{10,11... | collective-permute-start | bytes 1769480 | tf_op jit(solution)/shard_map/ppermute | solution.py:23
  92.1 14.8 %collective-permute-start.32 = (bf16[4,9,64,128]{3,2,1,0:T(8,128)(2,1)S(1)}, bf16[4,9,64,128]{3,2,1,0:T(8,128)(2,1)S(1)}, u32[]{:S(2)}, u32[]{:S(2)}) collective-permute-start(bf16[4,9,64,128]{3,2,1,0:T(8,128)(2,1)S(1)} %collective-permute-done.31.refs_7_), channel_id=1, source_target_pairs={{0,1},{1,0},{2,3},{3,2},{4,5},{5,4},{6,7},{7,6},{8,9},{9,8},{10,11... | collective-permute-start | bytes 1769480 | tf_op jit(solution)/shard_map/ppermute | solution.py:23
  92.1 16.7 %collective-permute-start.30 = (bf16[4,9,64,128]{3,2,1,0:T(8,128)(2,1)S(1)}, bf16[4,9,64,128]{3,2,1,0:T(8,128)(2,1)S(1)}, u32[]{:S(2)}, u32[]{:S(2)}) collective-permute-start(bf16[4,9,64,128]{3,2,1,0:T(8,128)(2,1)S(1)} %collective-permute-done.29.refs_5_), channel_id=1, source_target_pairs={{0,1},{1,0},{2,3},{3,2},{4,5},{5,4},{6,7},{7,6},{8,9},{9,8},{10,11... | collective-permute-start | bytes 1769480 | tf_op jit(solution)/shard_map/ppermute | solution.py:23
  92.6 16.3 %collective-permute-start.28 = (bf16[4,9,64,128]{3,2,1,0:T(8,128)(2,1)}, bf16[4,9,64,128]{3,2,1,0:T(8,128)(2,1)S(1)}, u32[]{:S(2)}, u32[]{:S(2)}) collective-permute-start(bf16[4,9,64,128]{3,2,1,0:T(8,128)(2,1)} %collective-permute-done.27.refs_3_), channel_id=1, source_target_pairs={{0,1},{1,0},{2,3},{3,2},{4,5},{5,4},{6,7},{7,6},{8,9},{9,8},{10,11... | collective-permute-start | bytes 1769480 | tf_op jit(solution)/shard_map/ppermute | solution.py:23
  103.4 22.0 %collective-permute-start.58 = (bf16[256,256]{1,0:T(8,128)(2,1)}, bf16[256,256]{1,0:T(8,128)(2,1)S(1)}, u32[]{:S(2)}, u32[]{:S(2)}) collective-permute-start(bf16[256,256]{1,0:T(8,128)(2,1)} %get-tuple-element.220), channel_id=1, source_target_pairs={{0,16},{1,17},{2,18},{3,19},{4,20},{5,21},{6,22},{7,23},{8,24},{9,... | collective-permute-start | bytes 393224 | tf_op jit(solution)/shard_map/ppermute | solution.py:23
  105.0 21.5 %collective-permute-start.57 = (bf16[256,256]{1,0:T(8,128)(2,1)}, bf16[256,256]{1,0:T(8,128)(2,1)S(1)}, u32[]{:S(2)}, u32[]{:S(2)}) collective-permute-start(bf16[256,256]{1,0:T(8,128)(2,1)} %get-tuple-element.220), channel_id=1, source_target_pairs={{0,8},{1,9},{2,10},{3,11},{4,12},{5,13},{6,14},{7,15},{8,0},{9,1},... | collective-permute-start | bytes 393224 | tf_op jit(solution)/shard_map/ppermute | solution.py:23
  107.0 20.9 %collective-permute-start.48 = (bf16[4,128,256]{2,1,0:T(8,128)(2,1)S(1)}, bf16[4,128,256]{2,1,0:T(8,128)(2,1)S(1)}, u32[]{:S(2)}, u32[]{:S(2)}) collective-permute-start(bf16[4,128,256]{2,1,0:T(8,128)(2,1)S(1)} %pad_maximum_fusion.3.refs_1_), channel_id=1, source_target_pairs={{0,6},{1,7},{2,4},{3,5},{4,2},{5,3},{6,0},{7,1},{8,14},{9,15},{10,... | collective-permute-start | bytes 786440 | tf_op jit(solution)/shard_map/ppermute | solution.py:23
  132.8 10.0 %collective-permute-start.45 = (bf16[4,128,256]{2,1,0:T(8,128)(2,1)S(1)}, bf16[4,128,256]{2,1,0:T(8,128)(2,1)S(1)}, u32[]{:S(2)}, u32[]{:S(2)}) collective-permute-start(bf16[4,128,256]{2,1,0:T(8,128)(2,1)S(1)} %collective-permute-done.44.refs_3_), channel_id=1, source_target_pairs={{0,1},{1,0},{2,3},{3,2},{4,5},{5,4},{6,7},{7,6},{8,9},{9,8},{10,11... | collective-permute-start | bytes 786440 | tf_op jit(solution)/shard_map/ppermute | solution.py:23
  139.2 18.2 %collective-permute-start.65 = (bf16[4,256,256]{2,1,0:T(8,128)(2,1)S(1)}, bf16[4,256,256]{2,1,0:T(8,128)(2,1)S(1)}, u32[]{:S(2)}, u32[]{:S(2)}) collective-permute-start(bf16[4,256,256]{2,1,0:T(8,128)(2,1)S(1)} %pad_maximum_fusion.1.refs_1_), channel_id=1, source_target_pairs={{0,6},{1,7},{2,4},{3,5},{4,2},{5,3},{6,0},{7,1},{8,14},{9,15},{10,... | collective-permute-start | bytes 1572872 | tf_op jit(solution)/shard_map/ppermute | solution.py:23
  140.6 23.3 %collective-permute-start.63 = (bf16[4,256,256]{2,1,0:T(8,128)(2,1)S(1)}, bf16[4,256,256]{2,1,0:T(8,128)(2,1)S(1)}, u32[]{:S(2)}, u32[]{:S(2)}) collective-permute-start(bf16[4,256,256]{2,1,0:T(8,128)(2,1)S(1)} %pad_maximum_fusion.1.refs_1_), channel_id=1, source_target_pairs={{0,4},{1,5},{2,6},{3,7},{4,0},{5,1},{6,2},{7,3},{8,12},{9,13},{10,... | collective-permute-start | bytes 1572872 | tf_op jit(solution)/shard_map/ppermute | solution.py:23
  142.1 22.2 %collective-permute-start.61 = (bf16[4,256,256]{2,1,0:T(8,128)(2,1)S(1)}, bf16[4,256,256]{2,1,0:T(8,128)(2,1)S(1)}, u32[]{:S(2)}, u32[]{:S(2)}) collective-permute-start(bf16[4,256,256]{2,1,0:T(8,128)(2,1)S(1)} %pad_maximum_fusion.1.refs_1_), channel_id=1, source_target_pairs={{0,2},{1,3},{2,0},{3,1},{4,6},{5,7},{6,4},{7,5},{8,10},{9,11},{10,... | collective-permute-start | bytes 1572872 | tf_op jit(solution)/shard_map/ppermute | solution.py:23
  155.7 15.3 %collective-permute-start.60 = (bf16[4,256,256]{2,1,0:T(8,128)(2,1)S(1)}, bf16[4,256,256]{2,1,0:T(8,128)(2,1)S(1)}, u32[]{:S(2)}, u32[]{:S(2)}) collective-permute-start(bf16[4,256,256]{2,1,0:T(8,128)(2,1)S(1)} %pad_maximum_fusion.1.refs_1_), channel_id=1, source_target_pairs={{0,1},{1,0},{2,3},{3,2},{4,5},{5,4},{6,7},{7,6},{8,9},{9,8},{10,11... | collective-permute-start | bytes 1572872 | tf_op jit(solution)/shard_map/ppermute | solution.py:23
  157.4 13.6 %collective-permute-start.66 = (bf16[4,256,256]{2,1,0:T(8,128)(2,1)S(1)}, bf16[4,256,256]{2,1,0:T(8,128)(2,1)S(1)}, u32[]{:S(2)}, u32[]{:S(2)}) collective-permute-start(bf16[4,256,256]{2,1,0:T(8,128)(2,1)S(1)} %collective-permute-done.65.refs_7_), channel_id=1, source_target_pairs={{0,1},{1,0},{2,3},{3,2},{4,5},{5,4},{6,7},{7,6},{8,9},{9,8},{10,11... | collective-permute-start | bytes 1572872 | tf_op jit(solution)/shard_map/ppermute | solution.py:23
  168.1 10.7 %collective-permute-start.56 = (f32[2,2048]{1,0:T(2,128)S(1)}, f32[2,2048]{1,0:T(2,128)S(1)}, u32[]{:S(2)}, u32[]{:S(2)}) collective-permute-start(f32[2,2048]{1,0:T(2,128)S(1)} %add_add_fusion.3), channel_id=1, source_target_pairs={{0,24},{1,25},{2,26},{3,27},{4,28},{5,29},{6,30},{7,31},{8,16},{9,... | collective-permute-start | bytes 49160 | tf_op jit(solution)/shard_map/ppermute | solution.py:23
  199.8 46.6 %collective-permute-start.73 = (f32[3,2048]{1,0:T(4,128)S(1)}, f32[3,2048]{1,0:T(4,128)S(1)}, u32[]{:S(2)}, u32[]{:S(2)}) collective-permute-start(f32[3,2048]{1,0:T(4,128)S(1)} %add_add_fusion.1), channel_id=1, source_target_pairs={{0,24},{1,25},{2,26},{3,27},{4,28},{5,29},{6,30},{7,31},{8,16},{9,... | collective-permute-start | bytes 73736 | tf_op jit(solution)/shard_map/ppermute | solution.py:23
  202.3 44.2 %collective-permute-start.72 = (f32[3,2048]{1,0:T(4,128)S(1)}, f32[3,2048]{1,0:T(4,128)S(1)}, u32[]{:S(2)}, u32[]{:S(2)}) collective-permute-start(f32[3,2048]{1,0:T(4,128)S(1)} %add_add_fusion.1), channel_id=1, source_target_pairs={{0,16},{1,17},{2,18},{3,19},{4,20},{5,21},{6,22},{7,23},{8,24},{9,... | collective-permute-start | bytes 73736 | tf_op jit(solution)/shard_map/ppermute | solution.py:23
  202.3 44.2 %collective-permute-start.71 = (f32[3,2048]{1,0:T(4,128)S(1)}, f32[3,2048]{1,0:T(4,128)S(1)}, u32[]{:S(2)}, u32[]{:S(2)}) collective-permute-start(f32[3,2048]{1,0:T(4,128)S(1)} %add_add_fusion.1), channel_id=1, source_target_pairs={{0,8},{1,9},{2,10},{3,11},{4,12},{5,13},{6,14},{7,15},{8,0},{9,1},... | collective-permute-start | bytes 73736 | tf_op jit(solution)/shard_map/ppermute | solution.py:23
  277.9 31.5 %collective-permute-start.108 = (bf16[4,128,256]{2,1,0:T(8,128)(2,1)}, bf16[4,128,256]{2,1,0:T(8,128)(2,1)S(1)}, u32[]{:S(2)}, u32[]{:S(2)}) collective-permute-start(bf16[4,128,256]{2,1,0:T(8,128)(2,1)} %get-tuple-element.96), channel_id=1, source_target_pairs={{0,1},{1,0},{2,3},{3,2},{4,5},{5,4},{6,7},{7,6},{8,9},{9,8},{10,11... | collective-permute-start | bytes 786440 | tf_op jit(solution)/shard_map/ppermute | solution.py:23
  278.4 25.5 %collective-permute-start.109 = (bf16[4,128,256]{2,1,0:T(8,128)(2,1)}, bf16[4,128,256]{2,1,0:T(8,128)(2,1)S(1)}, u32[]{:S(2)}, u32[]{:S(2)}) collective-permute-start(bf16[4,128,256]{2,1,0:T(8,128)(2,1)} %get-tuple-element.98), channel_id=1, source_target_pairs={{0,1},{1,0},{2,3},{3,2},{4,5},{5,4},{6,7},{7,6},{8,9},{9,8},{10,11... | collective-permute-start | bytes 786440 | tf_op jit(solution)/shard_map/ppermute | solution.py:23
  278.5 10.7 %collective-permute-start.84 = (f32[2,512]{1,0:T(2,128)S(1)}, f32[2,512]{1,0:T(2,128)S(1)}, u32[]{:S(2)}, u32[]{:S(2)}) collective-permute-start(f32[2,512]{1,0:T(2,128)S(1)} %add.361), channel_id=1, source_target_pairs={{0,6},{1,7},{2,4},{3,5},{4,2},{5,3},{6,0},{7,1},{8,14},{9,15},{10,... | collective-permute-start | bytes 12296 | tf_op jit(solution)/shard_map/ppermute | solution.py:23
  306.9 13.8 %collective-permute-start.112 = (bf16[4,128,256]{2,1,0:T(8,128)(2,1)S(1)}, bf16[4,128,256]{2,1,0:T(8,128)(2,1)S(1)}, u32[]{:S(2)}, u32[]{:S(2)}) collective-permute-start(bf16[4,128,256]{2,1,0:T(8,128)(2,1)S(1)} %add_convert_fusion.7), channel_id=1, source_target_pairs={{0,4},{1,5},{2,6},{3,7},{4,0},{5,1},{6,2},{7,3},{8,12},{9,13},{10,... | collective-permute-start | bytes 786440 | tf_op jit(solution)/shard_map/ppermute | solution.py:23
  307.1 13.9 %collective-permute-start.114 = (bf16[4,128,256]{2,1,0:T(8,128)(2,1)S(1)}, bf16[4,128,256]{2,1,0:T(8,128)(2,1)S(1)}, u32[]{:S(2)}, u32[]{:S(2)}) collective-permute-start(bf16[4,128,256]{2,1,0:T(8,128)(2,1)S(1)} %add_convert_fusion.6), channel_id=1, source_target_pairs={{0,6},{1,7},{2,4},{3,5},{4,2},{5,3},{6,0},{7,1},{8,14},{9,15},{10,... | collective-permute-start | bytes 786440 | tf_op jit(solution)/shard_map/ppermute | solution.py:23
  309.2 25.9 %collective-permute-start.99 = (bf16[4,9,64,128]{3,2,1,0:T(8,128)(2,1)S(1)}, bf16[4,9,64,128]{3,2,1,0:T(8,128)(2,1)S(1)}, u32[]{:S(2)}, u32[]{:S(2)}) collective-permute-start(bf16[4,9,64,128]{3,2,1,0:T(8,128)(2,1)S(1)} %copy-done.69), channel_id=1, source_target_pairs={{0,1},{1,0},{2,3},{3,2},{4,5},{5,4},{6,7},{7,6},{8,9},{9,8},{10,11... | collective-permute-start | bytes 1769480 | tf_op jit(solution)/shard_map/ppermute | solution.py:23
  309.4 13.8 %collective-permute-start.88 = (bf16[4,256,128]{2,1,0:T(8,128)(2,1)S(1)}, bf16[4,256,128]{2,1,0:T(8,128)(2,1)S(1)}, u32[]{:S(2)}, u32[]{:S(2)}) collective-permute-start(bf16[4,256,128]{2,1,0:T(8,128)(2,1)S(1)} %copy-done.72), channel_id=1, source_target_pairs={{0,1},{1,0},{2,3},{3,2},{4,5},{5,4},{6,7},{7,6},{8,9},{9,8},{10,11... | collective-permute-start | bytes 786440 | tf_op jit(solution)/shard_map/ppermute | solution.py:23
  313.9 11.3 %collective-permute-start.90 = (bf16[4,256,128]{2,1,0:T(8,128)(2,1)S(1)}, bf16[4,256,128]{2,1,0:T(8,128)(2,1)S(1)}, u32[]{:S(2)}, u32[]{:S(2)}) collective-permute-start(bf16[4,256,128]{2,1,0:T(8,128)(2,1)S(1)} %add_convert_fusion.13), channel_id=1, source_target_pairs={{0,2},{1,3},{2,0},{3,1},{4,6},{5,7},{6,4},{7,5},{8,10},{9,11},{10,... | collective-permute-start | bytes 786440 | tf_op jit(solution)/shard_map/ppermute | solution.py:23
  320.7 12.9 %collective-permute-start.92 = (bf16[4,256,128]{2,1,0:T(8,128)(2,1)S(1)}, bf16[4,256,128]{2,1,0:T(8,128)(2,1)S(1)}, u32[]{:S(2)}, u32[]{:S(2)}) collective-permute-start(bf16[4,256,128]{2,1,0:T(8,128)(2,1)S(1)} %add_convert_fusion.12), channel_id=1, source_target_pairs={{0,4},{1,5},{2,6},{3,7},{4,0},{5,1},{6,2},{7,3},{8,12},{9,13},{10,... | collective-permute-start | bytes 786440 | tf_op jit(solution)/shard_map/ppermute | solution.py:23
  321.0 12.6 %collective-permute-start.94 = (bf16[4,256,128]{2,1,0:T(8,128)(2,1)S(1)}, bf16[4,256,128]{2,1,0:T(8,128)(2,1)S(1)}, u32[]{:S(2)}, u32[]{:S(2)}) collective-permute-start(bf16[4,256,128]{2,1,0:T(8,128)(2,1)S(1)} %add_convert_fusion.11), channel_id=1, source_target_pairs={{0,6},{1,7},{2,4},{3,5},{4,2},{5,3},{6,0},{7,1},{8,14},{9,15},{10,... | collective-permute-start | bytes 786440 | tf_op jit(solution)/shard_map/ppermute | solution.py:23
  323.3 31.2 %collective-permute-start.98 = (bf16[4,9,64,128]{3,2,1,0:T(8,128)(2,1)S(1)}, bf16[4,9,64,128]{3,2,1,0:T(8,128)(2,1)S(1)}, u32[]{:S(2)}, u32[]{:S(2)}) collective-permute-start(bf16[4,9,64,128]{3,2,1,0:T(8,128)(2,1)S(1)} %copy-done.66), channel_id=1, source_target_pairs={{0,1},{1,0},{2,3},{3,2},{4,5},{5,4},{6,7},{7,6},{8,9},{9,8},{10,11... | collective-permute-start | bytes 1769480 | tf_op jit(solution)/shard_map/ppermute | solution.py:23
  325.2 12.6 %collective-permute-start.101 = (bf16[4,9,64,128]{3,2,1,0:T(8,128)(2,1)S(1)}, bf16[4,9,64,128]{3,2,1,0:T(8,128)(2,1)S(1)}, u32[]{:S(2)}, u32[]{:S(2)}) collective-permute-start(bf16[4,9,64,128]{3,2,1,0:T(8,128)(2,1)S(1)} %copy-done.68), channel_id=1, source_target_pairs={{0,1},{1,0},{2,3},{3,2},{4,5},{5,4},{6,7},{7,6},{8,9},{9,8},{10,11... | collective-permute-start | bytes 1769480 | tf_op jit(solution)/shard_map/ppermute | solution.py:23
  342.9 16.3 %collective-permute-start.100 = (bf16[4,9,64,128]{3,2,1,0:T(8,128)(2,1)S(1)}, bf16[4,9,64,128]{3,2,1,0:T(8,128)(2,1)S(1)}, u32[]{:S(2)}, u32[]{:S(2)}) collective-permute-start(bf16[4,9,64,128]{3,2,1,0:T(8,128)(2,1)S(1)} %add_convert_fusion.3), channel_id=1, source_target_pairs={{0,2},{1,3},{2,0},{3,1},{4,6},{5,7},{6,4},{7,5},{8,10},{9,11},{10,... | collective-permute-start | bytes 1769480 | tf_op jit(solution)/shard_map/ppermute | solution.py:23
  344.0 27.8 %collective-permute-start.102 = (bf16[4,9,64,128]{3,2,1,0:T(8,128)(2,1)S(1)}, bf16[4,9,64,128]{3,2,1,0:T(8,128)(2,1)S(1)}, u32[]{:S(2)}, u32[]{:S(2)}) collective-permute-start(bf16[4,9,64,128]{3,2,1,0:T(8,128)(2,1)S(1)} %add_convert_fusion.2), channel_id=1, source_target_pairs={{0,4},{1,5},{2,6},{3,7},{4,0},{5,1},{6,2},{7,3},{8,12},{9,13},{10,... | collective-permute-start | bytes 1769480 | tf_op jit(solution)/shard_map/ppermute | solution.py:23
  344.3 27.5 %collective-permute-start.104 = (bf16[4,9,64,128]{3,2,1,0:T(8,128)(2,1)S(1)}, bf16[4,9,64,128]{3,2,1,0:T(8,128)(2,1)S(1)}, u32[]{:S(2)}, u32[]{:S(2)}) collective-permute-start(bf16[4,9,64,128]{3,2,1,0:T(8,128)(2,1)S(1)} %add_convert_fusion.1), channel_id=1, source_target_pairs={{0,6},{1,7},{2,4},{3,5},{4,2},{5,3},{6,0},{7,1},{8,14},{9,15},{10,... | collective-permute-start | bytes 1769480 | tf_op jit(solution)/shard_map/ppermute | solution.py:23
  372.6 10.2 %collective-permute-start.107 = (bf16[9,64,128]{2,1,0:T(8,128)(2,1)S(1)}, bf16[9,64,128]{2,1,0:T(8,128)(2,1)S(1)}, u32[]{:S(2)}, u32[]{:S(2)}) collective-permute-start(bf16[9,64,128]{2,1,0:T(8,128)(2,1)S(1)} %get-tuple-element.211), channel_id=1, source_target_pairs={{0,24},{1,25},{2,26},{3,27},{4,28},{5,29},{6,30},{7,31},{8,16},{9,... | collective-permute-start | bytes 442376 | tf_op jit(solution)/shard_map/ppermute | solution.py:23
  375.0 13.0 %collective-permute-start.106 = (bf16[9,64,128]{2,1,0:T(8,128)(2,1)S(1)}, bf16[9,64,128]{2,1,0:T(8,128)(2,1)S(1)}, u32[]{:S(2)}, u32[]{:S(2)}) collective-permute-start(bf16[9,64,128]{2,1,0:T(8,128)(2,1)S(1)} %get-tuple-element.212), channel_id=1, source_target_pairs={{0,16},{1,17},{2,18},{3,19},{4,20},{5,21},{6,22},{7,23},{8,24},{9,... | collective-permute-start | bytes 442376 | tf_op jit(solution)/shard_map/ppermute | solution.py:23
  (144 other events, 1153.3 us)

commit v2 on v1

--- a/solution.py
+++ b/solution.py
@@ -1,4 +1,5 @@
 import functools
+import math
 
 import jax
 import jax.numpy as jnp
@@ -33,42 +34,73 @@
     return [8 * k for k in range(n // 8)]
 
 
-def total(array, n):
-    array = array + swap(array, 1, n)
-    array = tree_sum([array] + [swap(array, mask, n) for mask in (2, 4, 6)])
-    return tree_sum([array] + [swap(array, mask, n) for mask in high_masks(n)[1:]])
-
-
-def gather(shard, n):
-    stack = jnp.stack([shard] + [swap(shard, mask, n) for mask in high_masks(n)[1:]])
-    even = [stack] + [swap(stack, mask, n) for mask in (2, 4, 6)]
-    odd = [swap(part, 1, n) for part in even]
-    return [even[0], odd[0], even[1], odd[1], even[2], odd[2], even[3], odd[3]]
-
-
-def scatter_sum(parts, n):
-    arrived = [swap(parts[k], 1, n) for k in (3, 5, 7, 1)]
-    merged = [
-        (own.astype(F32) + other.astype(F32)).astype(BF16)
-        for own, other in zip((parts[2], parts[4], parts[6], parts[0]), arrived)
-    ]
-    across = [swap(merged[k], 2 * k + 2, n) for k in range(3)]
-    both = tree_sum([part.astype(F32) for part in [merged[3]] + across]).astype(BF16)
-    last = [both[0]] + [swap(both[a], mask, n) for a, mask in enumerate(high_masks(n)) if a]
-    return tree_sum([part.astype(F32) for part in last])
-
-
-def call(kernel, outs, *inputs, flops=0):
+def total(array, n, early=None, late=None):
+    pair = following(array + swap(array, 1, n), early)
+    array = tree_sum([pair] + [swap(pair, mask, n) for mask in (2, 4, 6)])
+    array = following(array, late)
+    return tree_sum([array] + [swap(array, mask, n) for mask in high_masks(n)[1:]]), array, pair
+
+
+def following(value, earlier):
+    return value if earlier is None else lax.optimization_barrier((value, earlier))[0]
+
+
+def gather_high(shard, n):
+    return [shard] + [swap(shard, mask, n) for mask in high_masks(n)[1:]]
+
+
+def gather_low(parts, halves, n, after=None):
+    stack, masks = following(jnp.stack(parts), after), high_masks(n)
+    near, side = swap(stack, 2, n), swap(stack, 4, n)
+    half = len(masks) // 2
+    pairs = [(stack, masks), (side, [m ^ 4 for m in masks]), (near, [m ^ 2 for m in masks])]
+    if halves:
+        pairs.append((swap(near[:half], 4, n), [m ^ 6 for m in masks[:half]]))
+        pairs.append((swap(side[half:], 2, n), [m ^ 6 for m in masks[half:]]))
+    else:
+        pairs.append((swap(stack, 6, n), [m ^ 6 for m in masks]))
+    pairs += [(swap(array, 1, n), [m ^ 1 for m in row]) for array, row in pairs]
+    return pairs, side
+
+
+def slot_masks(n):
+    return [[core ^ low ^ high for low in (0, 2, 4, 6) for high in high_masks(n)] for core in (0, 1)]
+
+
+def scatter_start(own, other, n):
+    outs = [((n // 8,) + own.shape[1:], BF16)] * 4
+    return call(add_first_kernel, outs, swap(other, 1, n), own, anywhere=True)
+
+
+def scatter_next(kept, arrived, n):
+    shape = kept.shape[1:]
+    outs = [(shape, F32)] + [(shape, BF16)] * (n // 8 - 1)
+    return call(add_next_kernel, outs, kept, *arrived, anywhere=True)
+
+
+def scatter_last(sums, n):
+    return [sums[0]] + [swap(part, mask, n) for part, mask in zip(sums[1:], high_masks(n)[1:])]
+
+
+def added(parts):
+    return tree_sum([part.astype(F32) for part in parts])
+
+
+def call(kernel, outs, *inputs, flops=0, anywhere=False, scratch=(), semaphores=(), space=pltpu.VMEM):
     moved = sum(x.size * x.dtype.itemsize for x in inputs)
     shapes = [jax.ShapeDtypeStruct(*out) for out in outs]
     moved += sum(s.size * s.dtype.itemsize for s in shapes)
+    held = sum(math.prod(shape) * dtype(0).itemsize for shape, dtype in scratch)
+    specs = [pl.BlockSpec(memory_space=space)] * len(inputs)
+    if not anywhere:
+        specs[0] = pl.BlockSpec(memory_space=pltpu.SMEM)
     return pl.pallas_call(
         kernel,
         out_shape=shapes,
-        in_specs=[pl.BlockSpec(memory_space=pltpu.SMEM)]
-        + [pl.BlockSpec(memory_space=pltpu.VMEM)] * (len(inputs) - 1),
+        in_specs=specs,
         out_specs=[pl.BlockSpec(memory_space=pltpu.VMEM)] * len(outs),
-        compiler_params=pltpu.CompilerParams(vmem_limit_bytes=56 * 2**20),
+        scratch_shapes=[pltpu.VMEM(*one) for one in scratch] + list(semaphores),
+        compiler_params=pltpu.CompilerParams(vmem_limit_bytes=max(moved // 2, 8 * 2**20) + held + 4 * 2**20),
         cost_estimate=pl.CostEstimate(flops=flops, bytes_accessed=moved, transcendentals=0),
     )(*inputs)
 
@@ -96,47 +128,82 @@
     return jnp.sum(value, axis=0, keepdims=True)
 
 
+def octet_sum(value):
+    return jnp.sum(value.reshape(value.shape[0] // 8, 8, value.shape[1]), axis=0)
+
+
 def rows_of(step):
     return pl.ds(pl.multiple_of(step * CHUNK, CHUNK), CHUNK)
 
 
-def assemble_kernel(c, *refs):
-    me, *parts, out = refs
+def at(index, size):
+    if isinstance(index, int):
+        return pl.ds(index * size, size)
+    return pl.ds(pl.multiple_of(index * size, size), size)
+
+
+def assemble_kernel(c, plan, tall, me, *refs):
+    *parts, out = refs
     number = me[0] * c + me[1]
-    for k, part in enumerate(parts):
-        for a in range(part.shape[0]):
-            other = number ^ (8 * a + k)
+    for part, masks in zip(parts, plan):
+        for a, mask in enumerate(masks):
+            other = number ^ mask
             i, j = lax.div(other, c), lax.rem(other, c)
+            rows, cols = part.shape[-2:]
             if len(out.shape) == 3:
-                rows, cols = part.shape[2:]
-                out[
-                    :,
-                    pl.ds(pl.multiple_of(i * rows, rows), rows),
-                    pl.ds(pl.multiple_of(j * cols, cols), cols),
-                ] = part[a]
+                out[:, at(i, rows), at(j, cols)] = part[a]
+            elif tall:
+                out[at(i, rows), at(j, cols)] = part[a]
             else:
-                rows, cols = part.shape[1:]
-                out[
-                    pl.ds(pl.multiple_of(i * rows, rows), rows),
-                    pl.ds(pl.multiple_of(j * cols, cols), cols),
-                ] = part[a]
-
-
-def assemble_out_kernel(c, *refs):
-    me, *parts, out = refs
-    number = me[0] * c + me[1]
-    for k, part in enumerate(parts):
-        for a in range(part.shape[0]):
-            other = number ^ (8 * a + k)
-            i, j = lax.div(other, c), lax.rem(other, c)
-            rows, cols = part.shape[1:]
-            out[
-                pl.ds(pl.multiple_of(j * rows, rows), rows),
-                pl.ds(pl.multiple_of(i * cols, cols), cols),
-            ] = part[a]
-
-
-def first_kernel(me, weight_sum, *refs):
+                out[at(j, rows), at(i, cols)] = part[a]
+
+
+def assemble_head_kernel(c, me, rest, out):
+    n = rest.shape[0]
+    rows, cols = out.shape[0] // (n // c), out.shape[1] // c
+    for a in range(n):
+        for k in range(cols // LANES):
+            part = rest[a, k * rows : (k + 1) * rows, :]
+            out[at(a // c, rows), a % c * cols + k * LANES : a % c * cols + (k + 1) * LANES] = part
+
+
+def prepare_kernel(c, me, *refs):
+    sources, outs, held, arrived = refs[:5], refs[5:-6], refs[-6:-1], refs[-1]
+    pieces, (low_in, low_mid, low_out, low_head) = outs[:c], outs[c:]
+    features, conv_in, conv_mid, conv_out, classifier = held
+    order = (1, 0, 2, 3, 4)
+    copies = [pltpu.make_async_copy(sources[k], held[k], arrived.at[k]) for k in range(5)]
+    for k in order:
+        copies[k].start()
+    copies[1].wait()
+    low_in[...] = conv_in[...].astype(BF16)
+    copies[0].wait()
+    pixels, images, width = features.shape
+    group = images // c
+    for t in range(c):
+        part = features[:, t * group : (t + 1) * group, :].astype(F32)
+        part = part.reshape(pixels * group, width).astype(BF16)
+        for k in range(c):
+
+            @pl.when(me[1] == t ^ k)
+            def _(part=part, k=k):
+                pieces[k][...] = part
+
+    copies[2].wait()
+    low_mid[...] = conv_mid[...].astype(BF16)
+    copies[3].wait()
+    low_out[...] = conv_out[...].astype(BF16)
+    copies[4].wait()
+    tall, classes = classifier.shape
+    for k, start in enumerate(range(0, classes, LANES)):
+        stop = min(start + LANES, classes)
+        rows = slice(k * tall, (k + 1) * tall)
+        low_head[rows, 0 : stop - start] = classifier[:, start:stop].astype(BF16)
+        if stop - start < LANES:
+            low_head[rows, stop - start :] = jnp.zeros((tall, LANES - stop + start), BF16)
+
+
+def first_kernel(me, carried, *refs):
     *features, weights, hidden, sums = refs
     chan, depth = me[1], features[0].shape[1]
     width = hidden.shape[1]
@@ -150,7 +217,7 @@
         hidden[:, cols] = value
         sums[0:1, cols] = col_sum(value)
         sums[1:2, cols] = col_sum(value * value)
-    sums[2:3, :] = jnp.broadcast_to(weight_sum[...], (1, width))
+    sums[2:, :] = carried[...]
 
 
 def windows(pad, out, size, group):
@@ -230,8 +297,9 @@
         def forward(step, pool, k=k, cols=cols, gain=gain, shift=shift):
             part = rows_of(step)
             value = hidden[part, cols] * gain + shift + features[k][part, :].astype(F32)
-            upper[part, cols] = value
-            value = value * sigmoid(value)
+            sigma = sigmoid(value)
+            value = value * sigma
+            upper[part, cols] = sigma + value - value * sigma
             return pool + jnp.sum(value.reshape(CHUNK // twice, twice, width), axis=0)
 
         pool = lax.fori_loop(0, rows // CHUNK, forward, jnp.zeros((twice, width), F32))
@@ -257,17 +325,17 @@
         back = dot(low_down, weights[cols, :], ((1,), (1,))) / pixels
         back = jnp.broadcast_to(back[None], (CHUNK // twice, twice, width)).reshape(CHUNK, width)
 
-        def backward(step, so_far, cols=cols, mean=mean, scale=scale, back=back):
+        def backward(step, so_far, cols=cols, mean=mean, back=back):
             part = rows_of(step)
-            value = back * silu_grad(upper[part, cols])
-            normed = (hidden[part, cols] - mean) * scale
+            value = back * upper[part, cols]
+            moved = value * (hidden[part, cols] - mean)
             upper[part, cols] = value
-            return (so_far[0] + col_sum(value), so_far[1] + col_sum(value * normed))
-
-        zero = jnp.zeros((1, width), F32)
+            return (so_far[0] + octet_sum(value), so_far[1] + octet_sum(moved))
+
+        zero = jnp.zeros((8, width), F32)
         first, second = lax.fori_loop(0, rows // CHUNK, backward, (zero, zero))
-        out_sums[0:1, cols] = first
-        out_sums[1:2, cols] = second
+        out_sums[0:1, cols] = col_sum(first)
+        out_sums[1:2, cols] = col_sum(second) * scale
     out_sums[2:3, :] = jnp.broadcast_to(loss[...], (1, out_sums.shape[1]))
 
 
@@ -335,29 +403,25 @@
         finish(value, hidden_one, sums_one, norms_one, count, block, out, out_sums)
 
 
-def spread_blocks(number, c, outs, block):
-    for k, out in enumerate(outs):
-        for a in range(out.shape[0]):
-            other = number ^ (8 * a + k)
+def spread_blocks(number, c, outs, masks, block):
+    for out, row in zip(outs, masks):
+        for a, mask in enumerate(row):
+            other = number ^ mask
             out[a] = block(lax.div(other, c), lax.rem(other, c))
 
 
-def at(index, size):
-    return pl.ds(pl.multiple_of(index * size, size), size)
-
-
-def grad_out_kernel(c, me, act, down, *refs):
+def grad_out_kernel(c, masks, me, act, down, *refs):
     *outs, whole = refs
     for start in range(0, whole.shape[1], 512):
         cols = slice(start, start + 512)
         whole[:, cols] = dot(act[...], down[:, cols], ((0,), (0,))).astype(BF16)
     rows, width = outs[0].shape[1:]
     spread_blocks(
-        me[0] * c + me[1], c, outs, lambda i, j: whole[at(j, rows), at(i, width)]
-    )
-
-
-def grad_mid_kernel(c, me, cols, down, *refs):
+        me[0] * c + me[1], c, outs, masks, lambda i, j: whole[at(j, rows), at(i, width)]
+    )
+
+
+def grad_mid_kernel(c, masks, me, cols, down, *refs):
     *outs, whole = refs
     depth = whole.shape[1]
     for tap in range(9):
@@ -366,11 +430,11 @@
         ).astype(BF16)
     rows, width = outs[0].shape[2:]
     spread_blocks(
-        me[0] * c + me[1], c, outs, lambda i, j: whole[:, at(i, rows), at(j, width)]
-    )
-
-
-def grad_in_kernel(count, c, me, upper, hidden, sums, norms, back_sums, *refs):
+        me[0] * c + me[1], c, outs, masks, lambda i, j: whole[:, at(i, rows), at(j, width)]
+    )
+
+
+def grad_in_kernel(count, c, masks, me, upper, hidden, sums, norms, back_sums, *refs):
     features, outs, whole, down = refs[:c], refs[c:-2], refs[-2], refs[-1]
     rows = upper.shape[0]
     for step in range(rows // CHUNK):
@@ -383,42 +447,31 @@
         whole[at(me[1] ^ k, depth), :] = dot(part[...], down[...], ((0,), (0,))).astype(BF16)
     height, width = outs[0].shape[1:]
     spread_blocks(
-        me[0] * c + me[1], c, outs, lambda i, j: whole[at(i, height), at(j, width)]
-    )
-
-
-def call_with_scratch(kernel, outs, scratch, *inputs, flops=0):
-    moved = sum(x.size * x.dtype.itemsize for x in inputs)
-    shapes = [jax.ShapeDtypeStruct(*out) for out in outs]
-    moved += sum(s.size * s.dtype.itemsize for s in shapes)
-    return pl.pallas_call(
-        kernel,
-        out_shape=shapes,
-        in_specs=[pl.BlockSpec(memory_space=pltpu.SMEM)]
-        + [pl.BlockSpec(memory_space=pltpu.VMEM)] * (len(inputs) - 1),
-        out_specs=[pl.BlockSpec(memory_space=pltpu.VMEM)] * len(outs),
-        scratch_shapes=[pltpu.VMEM(*one) for one in scratch],
-        compiler_params=pltpu.CompilerParams(vmem_limit_bytes=56 * 2**20),
-        cost_estimate=pl.CostEstimate(flops=flops, bytes_accessed=moved, transcendentals=0),
-    )(*inputs)
+        me[0] * c + me[1], c, outs, masks, lambda i, j: whole[at(i, height), at(j, width)]
+    )
+
+
+def add_low(one, other):
+    return (one.astype(F32) + other.astype(F32)).astype(BF16)
+
+
+def add_first_kernel(arrived, own, *outs):
+    z = own.shape[0] // 4
+    for low, out in enumerate(outs):
+        for k in range(z):
+            out[k] = add_low(own[low * z + k], arrived[low * z + k])
+
+
+def add_next_kernel(kept, one, two, three, *outs):
+    for k, out in enumerate(outs):
+        pair = kept[k].astype(F32) + one[k].astype(F32)
+        out[...] = (pair + (two[k].astype(F32) + three[k].astype(F32))).astype(out.dtype)
 
 
 def advance(weight, grad, momentum, average, rate):
     fresh = MOMENTUM * momentum + grad
     weight_new = weight - rate * (grad + MOMENTUM * fresh)
     return (weight_new, fresh, AVERAGE * average + (1.0 - AVERAGE) * weight_new)
-
-
-def ordered(parts, number, n):
-    stacked = jnp.stack(parts, axis=1)
-    stacked = stacked.reshape((n,) + parts[0].shape[1:])
-    return jnp.take(stacked, jnp.arange(n) ^ number, axis=0)
-
-
-def relative(blocks, number, n):
-    blocks = jnp.take(blocks, jnp.arange(n) ^ number, axis=0)
-    blocks = blocks.reshape((n // 8, 8) + blocks.shape[1:])
-    return [blocks[:, k] for k in range(8)]
 
 
 def shards(
@@ -456,27 +509,32 @@
     mid, wide = conv_in.shape[1] * c, deep * c
     aligned = conv_out.shape[1] % LANES == 0
 
-    laid = features.transpose(1, 2, 0, 3).reshape(pixels, c, group, deep)
-    laid = laid.transpose(1, 0, 2, 3).reshape(c, rows, deep)
-    pieces = [lax.dynamic_index_in_dim(laid, chan ^ k, 0, keepdims=False) for k in range(c)]
-    pieces = [pieces[0]] + [swap(pieces[k], k, n) for k in range(1, c)]
-
-    low_in = gather(conv_in.astype(BF16), n)
     fan_in, fan_out = conv_mid.shape[2:]
-    low_mid = gather(conv_mid.astype(BF16).reshape(9, fan_in, fan_out), n)
-    low_out = gather(conv_out.astype(BF16), n)
     classes = classifier.shape[1]
     space = -(-classes // LANES) * LANES
-    low_head = gather(jnp.pad(classifier.astype(BF16), ((0, 0), (0, space - classes))), n)
-
-    table = norms[:, 0]
-    tables = jnp.stack([table] + [swap(table, k, n) for k in range(1, c)])
-    tables = jnp.take(tables, jnp.arange(c) ^ chan, axis=0).transpose(1, 0, 2)
+    tall = classifier.shape[0]
+    laid = features.transpose(1, 2, 0, 3).reshape(pixels, images, deep)
+    narrow_mid = conv_mid.reshape(9, fan_in, fan_out)
+    sources = (laid, conv_in, narrow_mid, conv_out, classifier)
+    own, mate, other, away, low_in, low_mid, low_out, low_head = call(
+        functools.partial(prepare_kernel, c),
+        [((rows, deep), BF16)] * c
+        + [(x.shape, BF16) for x in (conv_in, narrow_mid, conv_out)]
+        + [((tall * (space // LANES), LANES), BF16)],
+        me, *[pltpu.with_memory_space_constraint(x, pltpu.HBM) for x in sources], space=pltpu.HBM,
+        scratch=[(x.shape, jnp.dtype(x.dtype).type) for x in sources],
+        semaphores=[pltpu.SemaphoreType.DMA((5,))],
+    )
+    away, other = swap(away, 2, n), swap(other, 2, n)
+    high_in = gather_high(low_in, n)
+    low_head = lax.all_gather(low_head, AXES)
+    pieces = [own, swap(mate, 1, n), other, swap(away, 1, n)]
+    low_in, side_in = gather_low(high_in, False, n, (away, other))
+    high_mid = gather_high(following(low_mid, high_in[1]), n)
+    low_mid, _ = gather_low(high_mid, True, n, side_in)
+    high_out = gather_high(following(low_out, high_mid[1]), n)
+
     narrow = conv_in.shape[1]
-    norms_one = tables[:, :, :narrow].reshape(2, mid)
-    norms_two = tables[:, :, narrow : 2 * narrow].reshape(2, mid)
-    norms_three = tables[:, :, 2 * narrow :].reshape(2, wide)
-
     own = lax.dynamic_index_in_dim(labels.reshape(c, group), chan, 0, keepdims=False)
     own = jnp.concatenate([own, own])
     catalog = lax.broadcasted_iota(jnp.int32, (2 * group, class_weights.shape[0]), 1)
@@ -485,49 +543,59 @@
     target = jnp.pad(
         chosen.astype(F32).reshape(2 * group, c, classes), ((0, 0), (0, 0), (0, space - classes))
     ).reshape(2 * group, c * space)
-    own_weight = (0.5 * jnp.sum(weight_row)).reshape(1, 1)
-
-    def assembled(parts, shape, kernel):
-        if aligned:
-            return call(functools.partial(kernel, c), [(shape, BF16)], me, *parts)[0]
-        blocks = ordered(parts, number, n)
+    own_weight = jnp.broadcast_to(0.5 * jnp.sum(weight_row), (1, mid))
+    table = jnp.where(dp == 0, norms[:, 0], 0.0)
+    table = jnp.where((jnp.arange(c) == chan)[None, :, None], table[:, None, :], 0.0)
+    carried = table.reshape(-1, mid)
+    own_weight = jnp.concatenate([own_weight, carried])
+
+    def assembled(parts, shape, wide_rows):
+        if parts[0][0].shape[-1] % LANES == 0:
+            plan = [masks for _, masks in parts]
+            kernel = functools.partial(assemble_kernel, c, plan, wide_rows)
+            return call(kernel, [(shape, BF16)], me, *[array for array, _ in parts])[0]
+        blocks = jnp.concatenate([array for array, _ in parts], axis=0)
+        order = jnp.array([mask for _, masks in parts for mask in masks])
+        blocks = jnp.take(blocks, jnp.argsort(order ^ number), axis=0)
         blocks = blocks.reshape((d, c) + blocks.shape[1:])
-        if kernel is assemble_out_kernel:
-            return blocks.transpose(1, 2, 0, 3).reshape(shape)
-        if len(shape) == 3:
-            return blocks.transpose(2, 0, 3, 1, 4).reshape(shape)
-        return blocks.transpose(0, 2, 1, 3).reshape(shape)
-
-    whole_in = assembled(low_in, (wide, mid), assemble_kernel)
+        return blocks.transpose(1, 2, 0, 3).reshape(shape)
+
+    whole_in = assembled(low_in, (wide, mid), True)
     hidden_one, sums_one = call(
-        first_kernel, [((rows, mid), F32), ((3, mid), F32)], me, own_weight, *pieces, whole_in,
+        first_kernel, [((rows, mid), F32), ((2 + own_weight.shape[0], mid), F32)], me, own_weight, *pieces, whole_in,
         flops=2 * rows * wide * mid,
     )
-    sums_one = total(sums_one, n)
+    sums_one, half_way, _ = total(sums_one, n)
     weight_sum = sums_one[2, 0]
-
-    whole_mid = assembled(low_mid, (9, mid, mid), assemble_kernel).reshape(9 * mid, mid)
+    tables = sums_one[3:].reshape(2, c, -1)
+    norms_one = tables[:, :, :narrow].reshape(2, mid)
+    norms_two = tables[:, :, narrow : 2 * narrow].reshape(2, mid)
+    norms_three = tables[:, :, 2 * narrow :].reshape(2, wide)
+
+    low_out, _ = gather_low(high_out, False, n, half_way)
+    whole_mid = assembled(low_mid, (9, mid, mid), True).reshape(9 * mid, mid)
     line = size * group
-    padded = ((3, rows + 2 * line, mid), F32)
-    cols, hidden_two, sums_two = call_with_scratch(
+    padded = ((3, rows + 2 * line, mid), jnp.float32)
+    cols, hidden_two, sums_two = call(
         functools.partial(second_kernel, count, size, group),
         [((rows, 9 * mid), BF16), ((rows, mid), F32), ((2, mid), F32)],
-        [padded],
         me, hidden_one, sums_one, norms_one, whole_mid,
-        flops=18 * rows * mid * mid,
-    )
-    sums_two = total(sums_two, n)
-
-    whole_out = assembled(low_out, (mid, wide), assemble_out_kernel)
+        flops=18 * rows * mid * mid, scratch=[padded],
+    )
+    whole_head = call(
+        functools.partial(assemble_head_kernel, c), [((wide, c * space), BF16)], me, low_head
+    )[0]
+    sums_two, *_ = total(sums_two, n, None, whole_head)
+
+    whole_out = assembled(low_out, (mid, wide), False)
     act_two, hidden_three, sums_three = call(
         functools.partial(third_kernel, count),
         [((rows, mid), BF16), ((rows, wide), F32), ((2, wide), F32)],
         me, hidden_two, sums_two, norms_two, whole_out,
         flops=2 * rows * mid * wide,
     )
-    sums_three = total(sums_three, n)
-
-    whole_head = assembled(low_head, (wide, c * space), assemble_kernel)
+    sums_three, *_ = total(sums_three, n)
+
     row_weights = jnp.stack([weight_row, weight_row / weight_sum], axis=1)
     upper_three, back_three, packed, _ = call(
         functools.partial(head_kernel, count, pixels, group, classes),
@@ -535,8 +603,8 @@
         me, hidden_three, sums_three, norms_three, row_weights, target, whole_head, *pieces,
         flops=4 * 8 * wide * c * space,
     )
-    everything = lax.all_gather(packed[:group], AXES, axis=0, tiled=True)
-    back_three = total(back_three, n)
+    everything = lax.all_gather(packed, AXES, axis=0, tiled=True)
+    back_three, *_ = total(back_three, n)
     loss_sum = back_three[2, 0]
 
     down_three, upper_two, back_two = call(
@@ -546,51 +614,62 @@
         hidden_two, sums_two, norms_two,
         flops=2 * rows * mid * wide,
     )
-    back_two = total(back_two, n)
-
     def blocks_of(shape):
-        return [((n // 8,) + shape, BF16)] * 8
-
+        return [((n // 2,) + shape, BF16)] * 2
+
+    masks = slot_masks(n)
     if aligned:
-        parts_out = call_with_scratch(
-            functools.partial(grad_out_kernel, c), blocks_of(conv_out.shape), [((mid, wide), BF16)],
-            me, act_two, down_three, flops=2 * rows * mid * wide,
+        parts_out = call(
+            functools.partial(grad_out_kernel, c, masks), blocks_of(conv_out.shape),
+            me, act_two, down_three, flops=2 * rows * mid * wide, scratch=[((mid, wide), BF16)],
         )
     else:
         whole = dot(act_two, down_three, ((0,), (0,))).astype(BF16)
         whole = whole.reshape((c, conv_out.shape[0], d, conv_out.shape[1])).transpose(2, 0, 1, 3)
-        parts_out = relative(whole.reshape((n,) + conv_out.shape), number, n)
-    grad_out = scatter_sum(parts_out, n)
-
-    down_two, upper_one, back_one = call_with_scratch(
+        whole = whole.reshape((n,) + conv_out.shape)
+        parts_out = [jnp.take(whole, jnp.array(row) ^ number, axis=0) for row in masks]
+    back_two, half_way, _ = total(back_two, n, None, parts_out[0])
+    kept_out, *sends_out = scatter_start(*parts_out, n)
+    sends_out = following(sends_out, half_way)
+
+    down_two, upper_one, back_one = call(
         functools.partial(back_two_kernel, count, size, group),
         [((rows, mid), BF16), ((rows, mid), F32), ((2, mid), F32)],
-        [padded, ((rows, 9 * mid), BF16)],
         me, upper_two, hidden_two, sums_two, norms_two, back_two, whole_mid,
         hidden_one, sums_one, norms_one,
-        flops=18 * rows * mid * mid,
-    )
-    back_one = total(back_one, n)
-
-    shard_mid = (9, fan_in, fan_out)
-    parts_mid = call_with_scratch(
-        functools.partial(grad_mid_kernel, c), blocks_of(shard_mid), [((9, mid, mid), BF16)],
-        me, cols, down_two, flops=18 * rows * mid * mid,
-    )
-    grad_mid = scatter_sum(parts_mid, n).reshape(conv_mid.shape)
-
-    parts_in = call_with_scratch(
-        functools.partial(grad_in_kernel, count, c), blocks_of(conv_in.shape),
-        [((wide, mid), BF16), ((rows, mid), BF16)],
+        flops=18 * rows * mid * mid, scratch=[padded, ((rows, 9 * mid), BF16)],
+    )
+    arrived_out = [swap(send, mask, n) for send, mask in zip(sends_out, (2, 4, 6))]
+    parts_mid = call(
+        functools.partial(grad_mid_kernel, c, masks), blocks_of((9, fan_in, fan_out)),
+        me, cols, down_two, flops=18 * rows * mid * mid, scratch=[((9, mid, mid), BF16)],
+    )
+    kept_mid, *sends_mid = scatter_start(*parts_mid, n)
+    back_one, half_way, _ = total(back_one, n, None, sends_mid[2])
+    sends_mid = following(sends_mid, half_way)
+    far_mid = swap(sends_mid[2], 6, n)
+    sums_out = scatter_next(kept_out, arrived_out, n)
+    upper_one = following(upper_one, (far_mid, sums_out[0]))
+    parts_in = call(
+        functools.partial(grad_in_kernel, count, c, masks), blocks_of(conv_in.shape),
         me, upper_one, hidden_one, sums_one, norms_one, back_one, *pieces,
-        flops=2 * rows * mid * wide,
-    )
-    grad_in = scatter_sum(parts_in, n)
-
-    height = classifier.shape[0]
-    pooled = lax.dynamic_slice_in_dim(everything, dp * height, height, axis=1)
+        flops=2 * rows * mid * wide, scratch=[((wide, mid), BF16), ((rows, mid), BF16)],
+    )
+    last_out = scatter_last(sums_out, n)
+    arrived_mid = [swap(sends_mid[0], 2, n), swap(sends_mid[1], 4, n), far_mid]
+    kept_in, *sends_in = scatter_start(*parts_in, n)
+    arrived_in = [swap(send, mask, n) for send, mask in zip(sends_in, (2, 4, 6))]
+    last_mid = scatter_last(scatter_next(kept_mid, arrived_mid, n), n)
+    arrived_in, last_mid = lax.optimization_barrier((arrived_in, last_mid))
+    sums_in = scatter_next(kept_in, arrived_in, n)
+    last_mid = following(last_mid, sums_in[0])
+    grad_out = added(last_out)
+    grad_mid = added(last_mid).reshape(conv_mid.shape)
+    grad_in = added(scatter_last(sums_in, n))
+
+    pooled = lax.dynamic_slice_in_dim(everything, dp * tall, tall, axis=1)
     upper_logits = lax.dynamic_slice_in_dim(everything, wide + chan * space, space, axis=1)
-    grad_head = dot(pooled, upper_logits, ((0,), (0,)))[:, :classes]
+    grad_head = 0.5 * dot(pooled, upper_logits, ((0,), (0,)))[:, :classes]
 
     def mine(sums, width):
         return lax.dynamic_slice_in_dim(sums[:2], chan * width, width, axis=1)[::-1]

time: 391 us -> 316 us (0.81)
  blocking collectives: 42 us -> 0 us
  Pallas kernels: 71.4 us -> 46.5 us
  waiting for transfers between devices: 118 us -> 93.8 us
  local copies, waits for them, and re-layouts: 18 us -> 33.9 us
  between operations: 2.5 us -> 15.6 us
  other arithmetic: 24 us -> 14.3 us
  starting transfers between devices: 113 us -> 109 us
    all_gather x1 -> x0, blocking collectives: 42 us -> none  [shards(): everything = lax.all_gather(packed[:group], AXES, axis=0, tiled=True)]
    pallas_call x13 -> x20, Pallas kernels: 71.4 us -> 46.5 us  [call(): pl.pallas_call(kernel, out_shape=shapes, in_specs=specs, out_specs=[pl.Bl...]
    ppermute x118 -> x99, waiting for transfers between devices: 118 us -> 93.7 us  [swap(): return lax.ppermute(array, AXES, [(d, d ^ mask) for d in range(n)])]
    unnamed x152 -> x129, local copies, waits for them, and re-layouts: 6.47 us -> 29.5 us
    ppermute x118 -> x99, starting transfers between devices: 113 us -> 108 us  [swap(): return lax.ppermute(array, AXES, [(d, d ^ mask) for d in range(n)])]
    convert_element_type x16 -> x0, other arithmetic: 4.54 us -> none  [the longest x1 1.65 us: shards(): low_mid = gather(conv_mid.astype(BF16).reshape(9, fan_in, fan_out), n)]
    reshape x3 -> x1, local copies, waits for them, and re-layouts: 4 us -> 0.02 us  [shards(): tables = sums_one[3:].reshape(2, c, -1)]
  transfers between devices with their start and end apart: 118 -> 101, of which waited for: 41 -> 41; matrix products, arithmetic and copies ran while one was open for 9% -> 7% of each run, Pallas kernels for 12% -> 8%
where the time goes in v2:
time: 316 us; the launch traced here: 315 us
  starting transfers between devices  109 us (34%)
  waiting for transfers between devices  93.8 us (30%)
  Pallas kernels  46.5 us (15%)
  local copies, waits for them, and re-layouts  33.9 us (11%)
  between operations  15.6 us (5%)
  other arithmetic  14.3 us (5%)
    ppermute x99, starting transfers between devices, swap(): return lax.ppermute(array, AXES, [(d, d ^ mask) for d in range(n)])  108 us
    ppermute x99, waiting for transfers between devices, swap(): return lax.ppermute(array, AXES, [(d, d ^ mask) for d in range(n)])  93.7 us
    pallas_call x20, Pallas kernels, call(): pl.pallas_call(kernel, out_shape=shapes, in_specs=specs, out_specs=[pl.Bl...  46.5 us
    unnamed x129, local copies, waits for them, and re-layouts  29.5 us
  transfers between devices with their start and end apart: 101, of which 41 were waited for; matrix products, arithmetic and copies ran while one was open for 7% of the time, Pallas kernels for 8%

profile of v2, /device:TPU:0, one launch (start us, length us, event | category | flops | bytes accessed | tf_op | source)
XLA Modules:
  0.0 314.9 jit_solution(9762912312861487126)
XLA Ops:
  7.4 3.8 %shard_map.345 = (bf16[400,512]{1,0:T(8,128)(2,1)S(1)}, bf16[400,512]{1,0:T(8,128)(2,1)}, bf16[400,512]{1,0:T(8,128)(2,1)S(1)}, bf16[400,512]{1,0:T(8,128)(2,1)S...) custom-call(s32[2]{0:T(128)S(1)} %pad_add_fusion.me, ...), custom_call_target="tpu_custom_call" | custom-call | bytes 4499464 | tf_op jit(solution)/shard_map/pallas_call | solution.py:97
  11.2 3.0 collective-permute-start.1
  14.3 2.0 collective-permute-start.4
  16.4 2.6 collective-permute-start.5
  20.8 2.4 collective-permute-done.5
  25.9 7.5 %collective-permute-done.2 = bf16[400,512]{1,0:T(8,128)(2,1)S(1)} collective-permute-done((bf16[400,512]{1,0:T(8,128)(2,1)S(1)}, bf16[400,512]{1,0:T(8,128)(2,1)S(1)}, u32[]{:S(2)}, u32[]{:S(2)}) %collective-permute-start.2) | collective-permute-done | bytes 409632 | tf_op jit(solution)/shard_map/ppermute | solution.py:24
  37.5 3.7 %collective-permute-start.23 = (bf16[9,64,128]{2,1,0:T(8,128)(2,1)S(1)}, bf16[9,64,128]{2,1,0:T(8,128)(2,1)S(1)}, u32[]{:S(2)}, u32[]{:S(2)}) collective-permute-start(bf16[9,64,128]{2,1,0:T(8,128)(2,1)S(1)} %get-tuple-element.112), channel_id=1, source_target_pairs={{0,24},{1,25},{2,26},{3,27},{4,28},{5,29},{6,30},{7,31},{8,16},{9,... | collective-permute-start | bytes 442376 | tf_op jit(solution)/shard_map/ppermute | solution.py:24
  42.1 4.9 %collective-permute-done.8.refs_2_ = bf16[4,256,128]{2,1,0:T(8,128)(2,1)S(1)} collective-permute-done((bf16[4,256,128]{2,1,0:T(8,128)(2,1)S(1)}, bf16[4,256,128]{2,1,0:T(8,128)(2,1)S(1)}, u32[]{:S(2)}, u32[]{:S(2)}) %collective-permute-start.8) | collective-permute-done | bytes 262176 | tf_op jit(solution)/shard_map/ppermute | solution.py:24
  48.9 3.3 %collective-permute-done.9.refs_3_ = bf16[4,256,128]{2,1,0:T(8,128)(2,1)S(1)} collective-permute-done((bf16[4,256,128]{2,1,0:T(8,128)(2,1)S(1)}, bf16[4,256,128]{2,1,0:T(8,128)(2,1)S(1)}, u32[]{:S(2)}, u32[]{:S(2)}) %collective-permute-start.9) | collective-permute-done | bytes 262176 | tf_op jit(solution)/shard_map/ppermute | solution.py:24
  62.6 2.4 collective-permute-start.17
  65.0 8.4 %collective-permute-done.25.refs_2_ = bf16[4,9,64,128]{3,2,1,0:T(8,128)(2,1)} collective-permute-done((bf16[4,9,64,128]{3,2,1,0:T(8,128)(2,1)S(1)}, bf16[4,9,64,128]{3,2,1,0:T(8,128)(2,1)}, u32[]{:S(2)}, u32[]{:S(2)}) %collective-permute-start.25) | collective-permute-done | bytes 589856 | tf_op jit(solution)/shard_map/ppermute | solution.py:24
  76.5 3.0 collective-permute-start.41
  81.9 2.3 collective-permute-start.26
  85.3 3.1 collective-permute-start.19
  90.7 3.8 %collective-permute-done.20 = f32[15,512]{1,0:T(8,128)S(1)} collective-permute-done((f32[15,512]{1,0:T(8,128)S(1)}, f32[15,512]{1,0:T(8,128)S(1)}, u32[]{:S(2)}, u32[]{:S(2)}) %collective-permute-start.20) | collective-permute-done | bytes 30752 | tf_op jit(solution)/shard_map/ppermute | solution.py:24
  100.2 2.5 shard_map.348
  102.8 2.9 shard_map.349
  114.4 2.3 collective-permute-done.36
  116.8 2.2 copy-done.5
  120.7 2.1 copy-done.1
  128.5 2.6 collective-permute-done.39
  137.5 2.1 collective-permute-start.53
  142.2 2.3 collective-permute-start.55
  144.6 2.0 collective-permute-start.56
  146.9 3.2 %collective-permute-done.56 = f32[2,2048]{1,0:T(2,128)S(1)} collective-permute-done((f32[2,2048]{1,0:T(2,128)S(1)}, f32[2,2048]{1,0:T(2,128)S(1)}, u32[]{:S(2)}, u32[]{:S(2)}) %collective-permute-start.56) | collective-permute-done | bytes 16416 | tf_op jit(solution)/shard_map/ppermute | solution.py:24
  150.2 2.2 copy-done.2
  156.3 5.7 %shard_map.353 = (f32[400,2048]{1,0:T(8,128)S(1)}, f32[3,2048]{1,0:T(4,128)S(1)}, bf16[8,3072]{1,0:T(8,128)(2,1)}, f32[1,1]{1,0:T(1,128)}) custom-call(s32[2]{0:T(128)S(1)} %pad_add_fusion.me, f32[400,2048]{1,0:T(8,128)S(1)} %get-tuple-element.121.hidden, f32[2,2048]{1,0:T(2,128)S(1)} %add_add_fusion.7.sums, f32[2,2048]{1,0:T(2,128)S(1)} %bitcast.60, ...), custom_call_target="tpu_custom_call" | custom-call | flops 67108864 | bytes 12525644 | tf_op jit(solution)/shard_map/pallas_call | solution.py:97
  168.3 2.2 collective-permute-done.60
  170.6 3.0 collective-permute-start.62
  175.5 3.8 %collective-permute-done.63 = f32[3,2048]{1,0:T(4,128)S(1)} collective-permute-done((f32[3,2048]{1,0:T(4,128)S(1)}, f32[3,2048]{1,0:T(4,128)S(1)}, u32[]{:S(2)}, u32[]{:S(2)}) %collective-permute-start.63) | collective-permute-done | bytes 24608 | tf_op jit(solution)/shard_map/ppermute | solution.py:24
  179.3 2.0 shard_map.354
  184.0 2.1 collective-permute-start.67
  186.1 3.1 shard_map.355
  191.3 2.4 collective-permute-start.70
  193.9 2.8 collective-permute-done.70
  196.7 2.9 shard_map.356
  200.6 5.5 %shard_map.357 = (bf16[16,9,64,128]{3,2,1,0:T(8,128)(2,1)S(1)}, bf16[16,9,64,128]{3,2,1,0:T(8,128)(2,1)}) custom-call(s32[2]{0:T(128)S(1)} %pad_add_fusion.me, bf16[400,4608]{1,0:T(8,128)(2,1)S(1)} %copy-done.42, bf16[400,512]{1,0:T(8,128)(2,1)S(1)} %get-tuple-element.133.down), custom_call_target="tpu_custom_call" | custom-call | flops 1887436800 | bytes 8814600 | tf_op jit(solution)/shard_map/pallas_call | solution.py:97
  208.2 3.9 %collective-permute-done.72 = f32[2,512]{1,0:T(2,128)S(1)} collective-permute-done((f32[2,512]{1,0:T(2,128)S(1)}, f32[2,512]{1,0:T(2,128)S(1)}, u32[]{:S(2)}, u32[]{:S(2)}) %collective-permute-start.72) | collective-permute-done | bytes 4128 | tf_op jit(solution)/shard_map/ppermute | solution.py:24
  221.0 2.8 shard_map.358
  228.6 3.0 collective-permute-start.82
  234.7 13.2 %collective-permute-done.80.three = bf16[4,128,256]{2,1,0:T(8,128)(2,1)} collective-permute-done((bf16[4,128,256]{2,1,0:T(8,128)(2,1)}, bf16[4,128,256]{2,1,0:T(8,128)(2,1)}, u32[]{:S(2)}, u32[]{:S(2)}) %collective-permute-start.80) | collective-permute-done | bytes 262176 | tf_op jit(solution)/shard_map/ppermute | solution.py:24
  249.7 3.0 collective-permute-start.97
  256.1 3.3 %shard_map.361 = (bf16[16,256,128]{2,1,0:T(8,128)(2,1)S(1)}, bf16[16,256,128]{2,1,0:T(8,128)(2,1)}) custom-call(s32[2]{0:T(128)S(1)} %pad_add_fusion.me, f32[400,512]{1,0:T(8,128)S(1)} %copy-done.26, f32[400,512]{1,0:T(8,128)S(1)} %copy-done.19, f32[15,512]{1,0:T(8,128)S(1)} %add_add_fusion.5.sums.sums_one, f32[2,512]{1,0:T(2,128)S(1)} %bitcast.68, ...), custom_call_target="tpu_custom_call" | custom-call | flops 838860800 | bytes 5412872 | tf_op jit(solution)/shard_map/pallas_call | solution.py:97
  269.0 8.3 %collective-permute-done.88.one = bf16[4,9,64,128]{3,2,1,0:T(8,128)(2,1)S(1)} collective-permute-done((bf16[4,9,64,128]{3,2,1,0:T(8,128)(2,1)}, bf16[4,9,64,128]{3,2,1,0:T(8,128)(2,1)S(1)}, u32[]{:S(2)}, u32[]{:S(2)}) %collective-permute-start.88) | collective-permute-done | bytes 589856 | tf_op jit(solution)/shard_map/ppermute | solution.py:24
  281.9 2.9 collective-permute-start.91
  288.7 2.2 fusion.7
  294.2 4.0 %collective-permute-done.92 = bf16[9,64,128]{2,1,0:T(8,128)(2,1)S(1)} collective-permute-done((bf16[9,64,128]{2,1,0:T(8,128)(2,1)}, bf16[9,64,128]{2,1,0:T(8,128)(2,1)S(1)}, u32[]{:S(2)}, u32[]{:S(2)}) %collective-permute-start.92) | collective-permute-done | bytes 147488 | tf_op jit(solution)/shard_map/ppermute | solution.py:24
  300.5 2.6 collective-permute-start.95
  (369 shorter events, 132.0 us)
Async XLA Ops:
  7.2 109.6 %all-gather.6.cloned.1.call-start = ((), (), s32[]{:S(2)}) async-start(), calls=%async_computation.1 | async-start | bytes 4325376 | tf_op jit(solution)/shard_map/all_gather | solution.py:530
  11.2 277.5 %all-gather.4.cloned.1.call-start = ((), (), s32[]{:S(2)}) async-start(), calls=%async_computation | async-start | bytes 1622016 | tf_op jit(solution)/shard_map/all_gather | solution.py:606
  11.2 14.7 %collective-permute-start.1 = (bf16[400,512]{1,0:T(8,128)(2,1)S(1)}, bf16[400,512]{1,0:T(8,128)(2,1)S(1)}, u32[]{:S(2)}, u32[]{:S(2)}) collective-permute-start(bf16[400,512]{1,0:T(8,128)(2,1)S(1)} %get-tuple-element.105), channel_id=1, source_target_pairs={{0,2},{1,3},{2,0},{3,1},{4,6},{5,7},{6,4},{7,5},{8,10},{9,11},{10,... | collective-permute-start | bytes 1228808 | tf_op jit(solution)/shard_map/ppermute | solution.py:24
  14.2 19.2 %collective-permute-start.2 = (bf16[400,512]{1,0:T(8,128)(2,1)S(1)}, bf16[400,512]{1,0:T(8,128)(2,1)S(1)}, u32[]{:S(2)}, u32[]{:S(2)}) collective-permute-start(bf16[400,512]{1,0:T(8,128)(2,1)S(1)} %get-tuple-element.106), channel_id=1, source_target_pairs={{0,2},{1,3},{2,0},{3,1},{4,6},{5,7},{6,4},{7,5},{8,10},{9,11},{10,... | collective-permute-start | bytes 1228808 | tf_op jit(solution)/shard_map/ppermute | solution.py:24
  18.9 22.2 %collective-permute-start.21 = (bf16[9,64,128]{2,1,0:T(8,128)(2,1)S(1)}, bf16[9,64,128]{2,1,0:T(8,128)(2,1)S(1)}, u32[]{:S(2)}, u32[]{:S(2)}) collective-permute-start(bf16[9,64,128]{2,1,0:T(8,128)(2,1)S(1)} %get-tuple-element.112), channel_id=1, source_target_pairs={{0,8},{1,9},{2,10},{3,11},{4,12},{5,13},{6,14},{7,15},{8,0},{9,1},... | collective-permute-start | bytes 442376 | tf_op jit(solution)/shard_map/ppermute | solution.py:24
  23.2 18.5 %collective-permute-start.22 = (bf16[9,64,128]{2,1,0:T(8,128)(2,1)S(1)}, bf16[9,64,128]{2,1,0:T(8,128)(2,1)S(1)}, u32[]{:S(2)}, u32[]{:S(2)}) collective-permute-start(bf16[9,64,128]{2,1,0:T(8,128)(2,1)S(1)} %get-tuple-element.112), channel_id=1, source_target_pairs={{0,16},{1,17},{2,18},{3,19},{4,20},{5,21},{6,22},{7,23},{8,24},{9,... | collective-permute-start | bytes 442376 | tf_op jit(solution)/shard_map/ppermute | solution.py:24
  35.9 11.1 %collective-permute-start.8 = (bf16[4,256,128]{2,1,0:T(8,128)(2,1)S(1)}, bf16[4,256,128]{2,1,0:T(8,128)(2,1)S(1)}, u32[]{:S(2)}, u32[]{:S(2)}) collective-permute-start(bf16[4,256,128]{2,1,0:T(8,128)(2,1)S(1)} %pad_maximum_fusion.1.refs_0_), channel_id=1, source_target_pairs={{0,2},{1,3},{2,0},{3,1},{4,6},{5,7},{6,4},{7,5},{8,10},{9,11},{10,... | collective-permute-start | bytes 786440 | tf_op jit(solution)/shard_map/ppermute | solution.py:24
  37.5 9.7 %collective-permute-start.23 = (bf16[9,64,128]{2,1,0:T(8,128)(2,1)S(1)}, bf16[9,64,128]{2,1,0:T(8,128)(2,1)S(1)}, u32[]{:S(2)}, u32[]{:S(2)}) collective-permute-start(bf16[9,64,128]{2,1,0:T(8,128)(2,1)S(1)} %get-tuple-element.112), channel_id=1, source_target_pairs={{0,24},{1,25},{2,26},{3,27},{4,28},{5,29},{6,30},{7,31},{8,16},{9,... | collective-permute-start | bytes 442376 | tf_op jit(solution)/shard_map/ppermute | solution.py:24
  41.1 11.0 %collective-permute-start.9 = (bf16[4,256,128]{2,1,0:T(8,128)(2,1)S(1)}, bf16[4,256,128]{2,1,0:T(8,128)(2,1)S(1)}, u32[]{:S(2)}, u32[]{:S(2)}) collective-permute-start(bf16[4,256,128]{2,1,0:T(8,128)(2,1)S(1)} %pad_maximum_fusion.1.refs_0_), channel_id=1, source_target_pairs={{0,6},{1,7},{2,4},{3,5},{4,2},{5,3},{6,0},{7,1},{8,14},{9,15},{10,... | collective-permute-start | bytes 786440 | tf_op jit(solution)/shard_map/ppermute | solution.py:24
  41.6 10.5 %collective-permute-start.10 = (bf16[4,256,128]{2,1,0:T(8,128)(2,1)S(1)}, bf16[4,256,128]{2,1,0:T(8,128)(2,1)}, u32[]{:S(2)}, u32[]{:S(2)}) collective-permute-start(bf16[4,256,128]{2,1,0:T(8,128)(2,1)S(1)} %pad_maximum_fusion.1.refs_0_), channel_id=1, source_target_pairs={{0,1},{1,0},{2,3},{3,2},{4,5},{5,4},{6,7},{7,6},{8,9},{9,8},{10,11... | collective-permute-start | bytes 786440 | tf_op jit(solution)/shard_map/ppermute | solution.py:24
  41.7 11.9 %collective-permute-start.11 = (bf16[4,256,128]{2,1,0:T(8,128)(2,1)S(1)}, bf16[4,256,128]{2,1,0:T(8,128)(2,1)}, u32[]{:S(2)}, u32[]{:S(2)}) collective-permute-start(bf16[4,256,128]{2,1,0:T(8,128)(2,1)S(1)} %collective-permute-done.7.refs_1_), channel_id=1, source_target_pairs={{0,1},{1,0},{2,3},{3,2},{4,5},{5,4},{6,7},{7,6},{8,9},{9,8},{10,11... | collective-permute-start | bytes 786440 | tf_op jit(solution)/shard_map/ppermute | solution.py:24
  47.2 11.2 %collective-permute-start = (bf16[400,512]{1,0:T(8,128)(2,1)}, bf16[400,512]{1,0:T(8,128)(2,1)S(1)}, u32[]{:S(2)}, u32[]{:S(2)}) collective-permute-start(bf16[400,512]{1,0:T(8,128)(2,1)} %get-tuple-element.104), channel_id=1, source_target_pairs={{0,1},{1,0},{2,3},{3,2},{4,5},{5,4},{6,7},{7,6},{8,9},{9,8},{10,11... | collective-permute-start | bytes 1228808 | tf_op jit(solution)/shard_map/ppermute | solution.py:24
  52.2 21.2 %collective-permute-start.25 = (bf16[4,9,64,128]{3,2,1,0:T(8,128)(2,1)S(1)}, bf16[4,9,64,128]{3,2,1,0:T(8,128)(2,1)}, u32[]{:S(2)}, u32[]{:S(2)}) collective-permute-start(bf16[4,9,64,128]{3,2,1,0:T(8,128)(2,1)S(1)} %pad_maximum_fusion.refs_0_), channel_id=1, source_target_pairs={{0,2},{1,3},{2,0},{3,1},{4,6},{5,7},{6,4},{7,5},{8,10},{9,11},{10,... | collective-permute-start | bytes 1769480 | tf_op jit(solution)/shard_map/ppermute | solution.py:24
  53.6 23.0 %collective-permute-start.24 = (bf16[4,9,64,128]{3,2,1,0:T(8,128)(2,1)S(1)}, bf16[4,9,64,128]{3,2,1,0:T(8,128)(2,1)}, u32[]{:S(2)}, u32[]{:S(2)}) collective-permute-start(bf16[4,9,64,128]{3,2,1,0:T(8,128)(2,1)S(1)} %pad_maximum_fusion.refs_0_), channel_id=1, source_target_pairs={{0,4},{1,5},{2,6},{3,7},{4,0},{5,1},{6,2},{7,3},{8,12},{9,13},{10,... | collective-permute-start | bytes 1769480 | tf_op jit(solution)/shard_map/ppermute | solution.py:24
  61.5 19.1 %collective-permute-start.15 = (f32[15,512]{1,0:T(8,128)S(1)}, f32[15,512]{1,0:T(8,128)S(1)}, u32[]{:S(2)}, u32[]{:S(2)}) collective-permute-start(f32[15,512]{1,0:T(8,128)S(1)} %add.232), channel_id=1, source_target_pairs={{0,2},{1,3},{2,0},{3,1},{4,6},{5,7},{6,4},{7,5},{8,10},{9,11},{10,... | collective-permute-start | bytes 92168 | tf_op jit(solution)/shard_map/ppermute | solution.py:24
  62.0 19.9 %collective-permute-start.16 = (f32[15,512]{1,0:T(8,128)S(1)}, f32[15,512]{1,0:T(8,128)S(1)}, u32[]{:S(2)}, u32[]{:S(2)}) collective-permute-start(f32[15,512]{1,0:T(8,128)S(1)} %add.232), channel_id=1, source_target_pairs={{0,4},{1,5},{2,6},{3,7},{4,0},{5,1},{6,2},{7,3},{8,12},{9,13},{10,... | collective-permute-start | bytes 92168 | tf_op jit(solution)/shard_map/ppermute | solution.py:24
  62.6 21.6 %collective-permute-start.17 = (f32[15,512]{1,0:T(8,128)S(1)}, f32[15,512]{1,0:T(8,128)S(1)}, u32[]{:S(2)}, u32[]{:S(2)}) collective-permute-start(f32[15,512]{1,0:T(8,128)S(1)} %add.232), channel_id=1, source_target_pairs={{0,6},{1,7},{2,4},{3,5},{4,2},{5,3},{6,0},{7,1},{8,14},{9,15},{10,... | collective-permute-start | bytes 92168 | tf_op jit(solution)/shard_map/ppermute | solution.py:24
  73.4 10.8 %collective-permute-start.40 = (bf16[128,256]{1,0:T(8,128)(2,1)S(1)}, bf16[128,256]{1,0:T(8,128)(2,1)S(1)}, u32[]{:S(2)}, u32[]{:S(2)}) collective-permute-start(bf16[128,256]{1,0:T(8,128)(2,1)S(1)} %get-tuple-element.119), channel_id=1, source_target_pairs={{0,8},{1,9},{2,10},{3,11},{4,12},{5,13},{6,14},{7,15},{8,0},{9,1},... | collective-permute-start | bytes 196616 | tf_op jit(solution)/shard_map/ppermute | solution.py:24
  76.5 8.8 %collective-permute-start.41 = (bf16[128,256]{1,0:T(8,128)(2,1)S(1)}, bf16[128,256]{1,0:T(8,128)(2,1)S(1)}, u32[]{:S(2)}, u32[]{:S(2)}) collective-permute-start(bf16[128,256]{1,0:T(8,128)(2,1)S(1)} %get-tuple-element.119), channel_id=1, source_target_pairs={{0,16},{1,17},{2,18},{3,19},{4,20},{5,21},{6,22},{7,23},{8,24},{9,... | collective-permute-start | bytes 196616 | tf_op jit(solution)/shard_map/ppermute | solution.py:24
  80.5 8.2 %collective-permute-start.42 = (bf16[128,256]{1,0:T(8,128)(2,1)S(1)}, bf16[128,256]{1,0:T(8,128)(2,1)S(1)}, u32[]{:S(2)}, u32[]{:S(2)}) collective-permute-start(bf16[128,256]{1,0:T(8,128)(2,1)S(1)} %get-tuple-element.119), channel_id=1, source_target_pairs={{0,24},{1,25},{2,26},{3,27},{4,28},{5,29},{6,30},{7,31},{8,16},{9,... | collective-permute-start | bytes 196616 | tf_op jit(solution)/shard_map/ppermute | solution.py:24
  81.9 12.7 %collective-permute-start.26 = (bf16[2,9,64,128]{3,2,1,0:T(8,128)(2,1)S(1)}, bf16[2,9,64,128]{3,2,1,0:T(8,128)(2,1)S(1)}, u32[]{:S(2)}, u32[]{:S(2)}) collective-permute-start(bf16[2,9,64,128]{3,2,1,0:T(8,128)(2,1)S(1)} %slice.43), channel_id=1, source_target_pairs={{0,4},{1,5},{2,6},{3,7},{4,0},{5,1},{6,2},{7,3},{8,12},{9,13},{10,... | collective-permute-start | bytes 884744 | tf_op jit(solution)/shard_map/ppermute | solution.py:24
  84.1 11.0 %collective-permute-start.27 = (bf16[2,9,64,128]{3,2,1,0:T(8,128)(2,1)S(1)}, bf16[2,9,64,128]{3,2,1,0:T(8,128)(2,1)}, u32[]{:S(2)}, u32[]{:S(2)}) collective-permute-start(bf16[2,9,64,128]{3,2,1,0:T(8,128)(2,1)S(1)} %slice.44), channel_id=1, source_target_pairs={{0,2},{1,3},{2,0},{3,1},{4,6},{5,7},{6,4},{7,5},{8,10},{9,11},{10,... | collective-permute-start | bytes 884744 | tf_op jit(solution)/shard_map/ppermute | solution.py:24
  90.7 9.5 %collective-permute-start.29 = (bf16[4,9,64,128]{3,2,1,0:T(8,128)(2,1)}, bf16[4,9,64,128]{3,2,1,0:T(8,128)(2,1)S(1)}, u32[]{:S(2)}, u32[]{:S(2)}) collective-permute-start(bf16[4,9,64,128]{3,2,1,0:T(8,128)(2,1)} %collective-permute-done.24.refs_1_), channel_id=1, source_target_pairs={{0,1},{1,0},{2,3},{3,2},{4,5},{5,4},{6,7},{7,6},{8,9},{9,8},{10,11... | collective-permute-start | bytes 1769480 | tf_op jit(solution)/shard_map/ppermute | solution.py:24
  95.3 13.7 %collective-permute-start.43 = (bf16[4,128,256]{2,1,0:T(8,128)(2,1)S(1)}, bf16[4,128,256]{2,1,0:T(8,128)(2,1)}, u32[]{:S(2)}, u32[]{:S(2)}) collective-permute-start(bf16[4,128,256]{2,1,0:T(8,128)(2,1)S(1)} %pad_maximum_fusion.2.refs_0_), channel_id=1, source_target_pairs={{0,4},{1,5},{2,6},{3,7},{4,0},{5,1},{6,2},{7,3},{8,12},{9,13},{10,... | collective-permute-start | bytes 786440 | tf_op jit(solution)/shard_map/ppermute | solution.py:24
  97.5 13.3 %collective-permute-start.44 = (bf16[4,128,256]{2,1,0:T(8,128)(2,1)S(1)}, bf16[4,128,256]{2,1,0:T(8,128)(2,1)}, u32[]{:S(2)}, u32[]{:S(2)}) collective-permute-start(bf16[4,128,256]{2,1,0:T(8,128)(2,1)S(1)} %pad_maximum_fusion.2.refs_0_), channel_id=1, source_target_pairs={{0,2},{1,3},{2,0},{3,1},{4,6},{5,7},{6,4},{7,5},{8,10},{9,11},{10,... | collective-permute-start | bytes 786440 | tf_op jit(solution)/shard_map/ppermute | solution.py:24
  98.5 13.8 %collective-permute-start.45 = (bf16[4,128,256]{2,1,0:T(8,128)(2,1)S(1)}, bf16[4,128,256]{2,1,0:T(8,128)(2,1)}, u32[]{:S(2)}, u32[]{:S(2)}) collective-permute-start(bf16[4,128,256]{2,1,0:T(8,128)(2,1)S(1)} %pad_maximum_fusion.2.refs_0_), channel_id=1, source_target_pairs={{0,6},{1,7},{2,4},{3,5},{4,2},{5,3},{6,0},{7,1},{8,14},{9,15},{10,... | collective-permute-start | bytes 786440 | tf_op jit(solution)/shard_map/ppermute | solution.py:24
  108.5 15.4 %collective-permute-start.46 = (bf16[4,128,256]{2,1,0:T(8,128)(2,1)S(1)}, bf16[4,128,256]{2,1,0:T(8,128)(2,1)S(1)}, u32[]{:S(2)}, u32[]{:S(2)}) collective-permute-start(bf16[4,128,256]{2,1,0:T(8,128)(2,1)S(1)} %pad_maximum_fusion.2.refs_0_), channel_id=1, source_target_pairs={{0,1},{1,0},{2,3},{3,2},{4,5},{5,4},{6,7},{7,6},{8,9},{9,8},{10,11... | collective-permute-start | bytes 786440 | tf_op jit(solution)/shard_map/ppermute | solution.py:24
  109.0 16.7 %collective-permute-start.47 = (bf16[4,128,256]{2,1,0:T(8,128)(2,1)}, bf16[4,128,256]{2,1,0:T(8,128)(2,1)S(1)}, u32[]{:S(2)}, u32[]{:S(2)}) collective-permute-start(bf16[4,128,256]{2,1,0:T(8,128)(2,1)} %collective-permute-done.43.refs_1_), channel_id=1, source_target_pairs={{0,1},{1,0},{2,3},{3,2},{4,5},{5,4},{6,7},{7,6},{8,9},{9,8},{10,11... | collective-permute-start | bytes 786440 | tf_op jit(solution)/shard_map/ppermute | solution.py:24
  113.5 13.7 %collective-permute-start.48 = (bf16[4,128,256]{2,1,0:T(8,128)(2,1)}, bf16[4,128,256]{2,1,0:T(8,128)(2,1)S(1)}, u32[]{:S(2)}, u32[]{:S(2)}) collective-permute-start(bf16[4,128,256]{2,1,0:T(8,128)(2,1)} %collective-permute-done.44.refs_2_), channel_id=1, source_target_pairs={{0,1},{1,0},{2,3},{3,2},{4,5},{5,4},{6,7},{7,6},{8,9},{9,8},{10,11... | collective-permute-start | bytes 786440 | tf_op jit(solution)/shard_map/ppermute | solution.py:24
  114.4 12.7 %collective-permute-start.49 = (bf16[4,128,256]{2,1,0:T(8,128)(2,1)}, bf16[4,128,256]{2,1,0:T(8,128)(2,1)S(1)}, u32[]{:S(2)}, u32[]{:S(2)}) collective-permute-start(bf16[4,128,256]{2,1,0:T(8,128)(2,1)} %collective-permute-done.45.refs_3_), channel_id=1, source_target_pairs={{0,1},{1,0},{2,3},{3,2},{4,5},{5,4},{6,7},{7,6},{8,9},{9,8},{10,11... | collective-permute-start | bytes 786440 | tf_op jit(solution)/shard_map/ppermute | solution.py:24
  207.6 11.7 %collective-permute-start.71 = (bf16[16,9,64,128]{3,2,1,0:T(8,128)(2,1)}, bf16[16,9,64,128]{3,2,1,0:T(8,128)(2,1)}, u32[]{:S(2)}, u32[]{:S(2)}) collective-permute-start(bf16[16,9,64,128]{3,2,1,0:T(8,128)(2,1)} %get-tuple-element.134), channel_id=1, source_target_pairs={{0,1},{1,0},{2,3},{3,2},{4,5},{5,4},{6,7},{7,6},{8,9},{9,8},{10,11... | collective-permute-start | bytes 7077896 | tf_op jit(solution)/shard_map/ppermute | solution.py:24
  217.3 11.3 %collective-permute-start.78 = (bf16[4,128,256]{2,1,0:T(8,128)(2,1)}, bf16[4,128,256]{2,1,0:T(8,128)(2,1)}, u32[]{:S(2)}, u32[]{:S(2)}) collective-permute-start(bf16[4,128,256]{2,1,0:T(8,128)(2,1)} %get-tuple-element.147), channel_id=1, source_target_pairs={{0,2},{1,3},{2,0},{3,1},{4,6},{5,7},{6,4},{7,5},{8,10},{9,11},{10,... | collective-permute-start | bytes 786440 | tf_op jit(solution)/shard_map/ppermute | solution.py:24
  218.5 13.0 %collective-permute-start.79 = (bf16[4,128,256]{2,1,0:T(8,128)(2,1)}, bf16[4,128,256]{2,1,0:T(8,128)(2,1)}, u32[]{:S(2)}, u32[]{:S(2)}) collective-permute-start(bf16[4,128,256]{2,1,0:T(8,128)(2,1)} %get-tuple-element.148), channel_id=1, source_target_pairs={{0,4},{1,5},{2,6},{3,7},{4,0},{5,1},{6,2},{7,3},{8,12},{9,13},{10,... | collective-permute-start | bytes 786440 | tf_op jit(solution)/shard_map/ppermute | solution.py:24
  225.6 28.5 %collective-permute-start.76 = (bf16[4,9,64,128]{3,2,1,0:T(8,128)(2,1)}, bf16[4,9,64,128]{3,2,1,0:T(8,128)(2,1)S(1)}, u32[]{:S(2)}, u32[]{:S(2)}) collective-permute-start(bf16[4,9,64,128]{3,2,1,0:T(8,128)(2,1)} %get-tuple-element.141), channel_id=1, source_target_pairs={{0,6},{1,7},{2,4},{3,5},{4,2},{5,3},{6,0},{7,1},{8,14},{9,15},{10,... | collective-permute-start | bytes 1769480 | tf_op jit(solution)/shard_map/ppermute | solution.py:24
  227.2 20.7 %collective-permute-start.80 = (bf16[4,128,256]{2,1,0:T(8,128)(2,1)}, bf16[4,128,256]{2,1,0:T(8,128)(2,1)}, u32[]{:S(2)}, u32[]{:S(2)}) collective-permute-start(bf16[4,128,256]{2,1,0:T(8,128)(2,1)} %get-tuple-element.149), channel_id=1, source_target_pairs={{0,6},{1,7},{2,4},{3,5},{4,2},{5,3},{6,0},{7,1},{8,14},{9,15},{10,... | collective-permute-start | bytes 786440 | tf_op jit(solution)/shard_map/ppermute | solution.py:24
  228.6 21.1 %collective-permute-start.81 = (f32[2,512]{1,0:T(2,128)S(1)}, f32[2,512]{1,0:T(2,128)S(1)}, u32[]{:S(2)}, u32[]{:S(2)}) collective-permute-start(f32[2,512]{1,0:T(2,128)S(1)} %add_add_fusion.10), channel_id=1, source_target_pairs={{0,8},{1,9},{2,10},{3,11},{4,12},{5,13},{6,14},{7,15},{8,0},{9,1},... | collective-permute-start | bytes 12296 | tf_op jit(solution)/shard_map/ppermute | solution.py:24
  228.6 24.1 %collective-permute-start.82 = (f32[2,512]{1,0:T(2,128)S(1)}, f32[2,512]{1,0:T(2,128)S(1)}, u32[]{:S(2)}, u32[]{:S(2)}) collective-permute-start(f32[2,512]{1,0:T(2,128)S(1)} %add_add_fusion.10), channel_id=1, source_target_pairs={{0,16},{1,17},{2,18},{3,19},{4,20},{5,21},{6,22},{7,23},{8,24},{9,... | collective-permute-start | bytes 12296 | tf_op jit(solution)/shard_map/ppermute | solution.py:24
  231.5 22.5 %collective-permute-start.83 = (f32[2,512]{1,0:T(2,128)S(1)}, f32[2,512]{1,0:T(2,128)S(1)}, u32[]{:S(2)}, u32[]{:S(2)}) collective-permute-start(f32[2,512]{1,0:T(2,128)S(1)} %add_add_fusion.10), channel_id=1, source_target_pairs={{0,24},{1,25},{2,26},{3,27},{4,28},{5,29},{6,30},{7,31},{8,16},{9,... | collective-permute-start | bytes 12296 | tf_op jit(solution)/shard_map/ppermute | solution.py:24
  249.7 9.8 %collective-permute-start.96 = (bf16[128,256]{1,0:T(8,128)(2,1)}, bf16[128,256]{1,0:T(8,128)(2,1)}, u32[]{:S(2)}, u32[]{:S(2)}) collective-permute-start(bf16[128,256]{1,0:T(8,128)(2,1)} %get-tuple-element.180), channel_id=1, source_target_pairs={{0,8},{1,9},{2,10},{3,11},{4,12},{5,13},{6,14},{7,15},{8,0},{9,1},... | collective-permute-start | bytes 196616 | tf_op jit(solution)/shard_map/ppermute | solution.py:24
  249.7 9.8 %collective-permute-start.97 = (bf16[128,256]{1,0:T(8,128)(2,1)}, bf16[128,256]{1,0:T(8,128)(2,1)}, u32[]{:S(2)}, u32[]{:S(2)}) collective-permute-start(bf16[128,256]{1,0:T(8,128)(2,1)} %get-tuple-element.181), channel_id=1, source_target_pairs={{0,16},{1,17},{2,18},{3,19},{4,20},{5,21},{6,22},{7,23},{8,24},{9,... | collective-permute-start | bytes 196616 | tf_op jit(solution)/shard_map/ppermute | solution.py:24
  259.4 25.4 %collective-permute-start.84 = (bf16[16,256,128]{2,1,0:T(8,128)(2,1)}, bf16[16,256,128]{2,1,0:T(8,128)(2,1)S(1)}, u32[]{:S(2)}, u32[]{:S(2)}) collective-permute-start(bf16[16,256,128]{2,1,0:T(8,128)(2,1)} %get-tuple-element.152), channel_id=1, source_target_pairs={{0,1},{1,0},{2,3},{3,2},{4,5},{5,4},{6,7},{7,6},{8,9},{9,8},{10,11... | collective-permute-start | bytes 3145736 | tf_op jit(solution)/shard_map/ppermute | solution.py:24
  261.5 15.7 %collective-permute-start.88 = (bf16[4,9,64,128]{3,2,1,0:T(8,128)(2,1)}, bf16[4,9,64,128]{3,2,1,0:T(8,128)(2,1)S(1)}, u32[]{:S(2)}, u32[]{:S(2)}) collective-permute-start(bf16[4,9,64,128]{3,2,1,0:T(8,128)(2,1)} %copy-done.37), channel_id=1, source_target_pairs={{0,2},{1,3},{2,0},{3,1},{4,6},{5,7},{6,4},{7,5},{8,10},{9,11},{10,... | collective-permute-start | bytes 1769480 | tf_op jit(solution)/shard_map/ppermute | solution.py:24
  263.1 15.1 %collective-permute-start.89 = (bf16[4,9,64,128]{3,2,1,0:T(8,128)(2,1)}, bf16[4,9,64,128]{3,2,1,0:T(8,128)(2,1)S(1)}, u32[]{:S(2)}, u32[]{:S(2)}) collective-permute-start(bf16[4,9,64,128]{3,2,1,0:T(8,128)(2,1)} %copy-done.36), channel_id=1, source_target_pairs={{0,4},{1,5},{2,6},{3,7},{4,0},{5,1},{6,2},{7,3},{8,12},{9,13},{10,... | collective-permute-start | bytes 1769480 | tf_op jit(solution)/shard_map/ppermute | solution.py:24
  281.9 9.0 %collective-permute-start.90 = (bf16[9,64,128]{2,1,0:T(8,128)(2,1)}, bf16[9,64,128]{2,1,0:T(8,128)(2,1)}, u32[]{:S(2)}, u32[]{:S(2)}) collective-permute-start(bf16[9,64,128]{2,1,0:T(8,128)(2,1)} %get-tuple-element.162), channel_id=1, source_target_pairs={{0,8},{1,9},{2,10},{3,11},{4,12},{5,13},{6,14},{7,15},{8,0},{9,1},... | collective-permute-start | bytes 442376 | tf_op jit(solution)/shard_map/ppermute | solution.py:24
  281.9 12.2 %collective-permute-start.91 = (bf16[9,64,128]{2,1,0:T(8,128)(2,1)}, bf16[9,64,128]{2,1,0:T(8,128)(2,1)}, u32[]{:S(2)}, u32[]{:S(2)}) collective-permute-start(bf16[9,64,128]{2,1,0:T(8,128)(2,1)} %get-tuple-element.163), channel_id=1, source_target_pairs={{0,16},{1,17},{2,18},{3,19},{4,20},{5,21},{6,22},{7,23},{8,24},{9,... | collective-permute-start | bytes 442376 | tf_op jit(solution)/shard_map/ppermute | solution.py:24
  285.1 13.1 %collective-permute-start.85 = (bf16[4,256,128]{2,1,0:T(8,128)(2,1)S(1)}, bf16[4,256,128]{2,1,0:T(8,128)(2,1)S(1)}, u32[]{:S(2)}, u32[]{:S(2)}) collective-permute-start(bf16[4,256,128]{2,1,0:T(8,128)(2,1)S(1)} %get-tuple-element.155), channel_id=1, source_target_pairs={{0,2},{1,3},{2,0},{3,1},{4,6},{5,7},{6,4},{7,5},{8,10},{9,11},{10,... | collective-permute-start | bytes 786440 | tf_op jit(solution)/shard_map/ppermute | solution.py:24
  286.1 12.4 %collective-permute-start.86 = (bf16[4,256,128]{2,1,0:T(8,128)(2,1)S(1)}, bf16[4,256,128]{2,1,0:T(8,128)(2,1)S(1)}, u32[]{:S(2)}, u32[]{:S(2)}) collective-permute-start(bf16[4,256,128]{2,1,0:T(8,128)(2,1)S(1)} %get-tuple-element.156), channel_id=1, source_target_pairs={{0,4},{1,5},{2,6},{3,7},{4,0},{5,1},{6,2},{7,3},{8,12},{9,13},{10,... | collective-permute-start | bytes 786440 | tf_op jit(solution)/shard_map/ppermute | solution.py:24
  287.3 11.2 %collective-permute-start.87 = (bf16[4,256,128]{2,1,0:T(8,128)(2,1)S(1)}, bf16[4,256,128]{2,1,0:T(8,128)(2,1)S(1)}, u32[]{:S(2)}, u32[]{:S(2)}) collective-permute-start(bf16[4,256,128]{2,1,0:T(8,128)(2,1)S(1)} %get-tuple-element.157), channel_id=1, source_target_pairs={{0,6},{1,7},{2,4},{3,5},{4,2},{5,3},{6,0},{7,1},{8,14},{9,15},{10,... | collective-permute-start | bytes 786440 | tf_op jit(solution)/shard_map/ppermute | solution.py:24
  (113 other events, 1005.6 us)
Sparse Core Ops, SparseCore 0:
  11.5 80.6 all-gather.5
  208.2 55.1 all-gather.3

commit v3 on v2

--- a/solution.py
+++ b/solution.py
@@ -34,11 +34,11 @@
     return [8 * k for k in range(n // 8)]
 
 
-def total(array, n, early=None, late=None):
-    pair = following(array + swap(array, 1, n), early)
+def total(array, n, late=None, paired=False):
+    pair = array if paired else array + swap(array, 1, n)
     array = tree_sum([pair] + [swap(pair, mask, n) for mask in (2, 4, 6)])
     array = following(array, late)
-    return tree_sum([array] + [swap(array, mask, n) for mask in high_masks(n)[1:]]), array, pair
+    return tree_sum([array] + [swap(array, mask, n) for mask in high_masks(n)[1:]]), array
 
 
 def following(value, earlier):
@@ -69,7 +69,7 @@
 
 def scatter_start(own, other, n):
     outs = [((n // 8,) + own.shape[1:], BF16)] * 4
-    return call(add_first_kernel, outs, swap(other, 1, n), own, anywhere=True)
+    return call(add_quarters_kernel, outs, swap(other, 1, n), own, anywhere=True)
 
 
 def scatter_next(kept, arrived, n):
@@ -78,6 +78,25 @@
     return call(add_next_kernel, outs, kept, *arrived, anywhere=True)
 
 
+def split_start(own, other, plan, n):
+    shape = own.shape[1:]
+    halves = [((n // 4, stop - start) + shape[1:], BF16) for start, stop, _ in plan for _ in (0, 1)]
+    outs = call(functools.partial(add_first_kernel, plan), halves, swap(other, 1, n), own, anywhere=True)
+    return outs[0::2], outs[1::2]
+
+
+def split_second(arrived, keeps, n):
+    quarters = [((n // 8,) + keep.shape[1:], BF16) for keep in keeps for _ in (0, 1)]
+    outs = call(add_second_kernel, quarters, *arrived, *keeps, anywhere=True)
+    return outs[0::2], outs[1::2]
+
+
+def split_third(arrived, keeps, plan, n):
+    shape = (plan[-1][1],) + keeps[0].shape[2:]
+    outs = [(shape, F32)] + [(shape, BF16)] * (n // 8 - 1)
+    return call(functools.partial(add_third_kernel, plan), outs, *arrived, *keeps, anywhere=True)
+
+
 def scatter_last(sums, n):
     return [sums[0]] + [swap(part, mask, n) for part, mask in zip(sums[1:], high_masks(n)[1:])]
 
@@ -86,12 +105,14 @@
     return tree_sum([part.astype(F32) for part in parts])
 
 
-def call(kernel, outs, *inputs, flops=0, anywhere=False, scratch=(), semaphores=(), space=pltpu.VMEM):
+def call(kernel, outs, *inputs, flops=0, anywhere=False, scratch=(), semaphores=(), remain=0):
+    first = len(inputs) - remain
+    inputs = [pltpu.with_memory_space_constraint(x, pltpu.HBM) if k >= first else x for k, x in enumerate(inputs)]
     moved = sum(x.size * x.dtype.itemsize for x in inputs)
     shapes = [jax.ShapeDtypeStruct(*out) for out in outs]
     moved += sum(s.size * s.dtype.itemsize for s in shapes)
     held = sum(math.prod(shape) * dtype(0).itemsize for shape, dtype in scratch)
-    specs = [pl.BlockSpec(memory_space=space)] * len(inputs)
+    specs = [pl.BlockSpec(memory_space=pltpu.VMEM if k < first else pltpu.HBM) for k in range(len(inputs))]
     if not anywhere:
         specs[0] = pl.BlockSpec(memory_space=pltpu.SMEM)
     return pl.pallas_call(
@@ -142,34 +163,34 @@
     return pl.ds(pl.multiple_of(index * size, size), size)
 
 
-def assemble_kernel(c, plan, tall, me, *refs):
+def assemble_kernel(c, plan, me, *refs):
     *parts, out = refs
     number = me[0] * c + me[1]
     for part, masks in zip(parts, plan):
         for a, mask in enumerate(masks):
             other = number ^ mask
             i, j = lax.div(other, c), lax.rem(other, c)
-            rows, cols = part.shape[-2:]
-            if len(out.shape) == 3:
-                out[:, at(i, rows), at(j, cols)] = part[a]
-            elif tall:
-                out[at(i, rows), at(j, cols)] = part[a]
-            else:
-                out[at(j, rows), at(i, cols)] = part[a]
-
-
-def assemble_head_kernel(c, me, rest, out):
-    n = rest.shape[0]
-    rows, cols = out.shape[0] // (n // c), out.shape[1] // c
-    for a in range(n):
-        for k in range(cols // LANES):
-            part = rest[a, k * rows : (k + 1) * rows, :]
-            out[at(a // c, rows), a % c * cols + k * LANES : a % c * cols + (k + 1) * LANES] = part
+            rows, cols = part.shape[1:]
+            out[at(i, rows), at(j, cols)] = part[a]
+
+
+def assemble_mid_kernel(c, plan, me, *refs):
+    parts, outs = refs[: len(plan)], refs[len(plan) :]
+    number = me[0] * c + me[1]
+    for part, masks in zip(parts, plan):
+        for a, mask in enumerate(masks):
+            other = number ^ mask
+            i, j = lax.div(other, c), lax.rem(other, c)
+            rows, cols = part.shape[2:]
+            outs[0][:, at(i, rows), at(j, cols)] = part[a, 0:9]
+            if len(outs) > 1:
+                for k in range(4):
+                    outs[1][at(2 * j + k // 2, rows), at(2 * i + k % 2, cols)] = part[a, 9 + k]
 
 
 def prepare_kernel(c, me, *refs):
     sources, outs, held, arrived = refs[:5], refs[5:-6], refs[-6:-1], refs[-1]
-    pieces, (low_in, low_mid, low_out, low_head) = outs[:c], outs[c:]
+    pieces, (low_in, low_mid, low_head) = outs[:c], outs[c:]
     features, conv_in, conv_mid, conv_out, classifier = held
     order = (1, 0, 2, 3, 4)
     copies = [pltpu.make_async_copy(sources[k], held[k], arrived.at[k]) for k in range(5)]
@@ -190,9 +211,13 @@
                 pieces[k][...] = part
 
     copies[2].wait()
-    low_mid[...] = conv_mid[...].astype(BF16)
+    low_mid[0:9] = conv_mid[...].astype(BF16)
     copies[3].wait()
-    low_out[...] = conv_out[...].astype(BF16)
+    if low_mid.shape[0] > 9:
+        rows, cols = low_mid.shape[1:]
+        for k in range(4):
+            part = conv_out[k // 2 * rows : (k // 2 + 1) * rows, k % 2 * cols : (k % 2 + 1) * cols]
+            low_mid[9 + k] = part.astype(BF16)
     copies[4].wait()
     tall, classes = classifier.shape
     for k, start in enumerate(range(0, classes, LANES)):
@@ -203,16 +228,26 @@
             low_head[rows, stop - start :] = jnp.zeros((tall, LANES - stop + start), BF16)
 
 
-def first_kernel(me, carried, *refs):
-    *features, weights, hidden, sums = refs
+def fetch(sources, places, arrived, start=0):
+    copies = [pltpu.make_async_copy(x, y, arrived.at[start + k]) for k, (x, y) in enumerate(zip(sources, places))]
+    for copy in copies:
+        copy.start()
+    return copies
+
+
+def first_kernel(c, me, carried, weights, *refs):
+    features, (hidden, sums, held, arrived) = refs[:c], refs[c:]
     chan, depth = me[1], features[0].shape[1]
     width = hidden.shape[1]
+    copies = fetch(features, [held.at[k] for k in range(c)], arrived)
     for start in range(0, width, 256):
         cols = slice(start, start + 256)
         value = None
-        for k, part in enumerate(features):
+        for k in range(c):
+            if start == 0:
+                copies[k].wait()
             rows = pl.ds(pl.multiple_of((chan ^ k) * depth, depth), depth)
-            term = dot(part[...], weights[rows, cols])
+            term = dot(held[k], weights[rows, cols])
             value = term if value is None else value + term
         hidden[:, cols] = value
         sums[0:1, cols] = col_sum(value)
@@ -246,7 +281,7 @@
         pad[j, line + rows :, :] = empty
 
 
-def second_kernel(count, size, group, me, hidden, sums, norms, weights, cols, out, out_sums, pad):
+def second_kernel(count, size, group, me, hidden, sums, norms, weights, low_act, out, out_sums, pad, cols):
     rows, width = hidden.shape
     line = size * group
     mean, scale = statistics(sums, count, slice(None))
@@ -256,8 +291,9 @@
     for step in range(rows // CHUNK):
         part = slice(step * CHUNK, (step + 1) * CHUNK)
         value = (hidden[part, :] - mean) * scale * gain + shift
-        act = (value * sigmoid(value)).astype(BF16).astype(F32)
-        pad[1, line + step * CHUNK : line + (step + 1) * CHUNK, :] = act
+        act = (value * sigmoid(value)).astype(BF16)
+        low_act[part, :] = act
+        pad[1, line + step * CHUNK : line + (step + 1) * CHUNK, :] = act.astype(F32)
     fill(pad, size, group)
     windows(pad, cols, size, group)
     for start in range(0, out.shape[1], 256):
@@ -283,20 +319,34 @@
         out_sums[1:2, block] = col_sum(value * value)
 
 
-def head_kernel(count, pixels, group, classes, me, hidden, sums, norms, row_weights, target, weights, *refs):
-    *features, upper, out_sums, packed, loss = refs
+def head_kernel(count, pixels, group, classes, c, me, hidden, sums, norms, row_weights, target, shards, *refs):
+    sources, (upper, out_sums, packed, loss, features, weights, arrived) = refs[:c], refs[c:]
     chan, rows = me[1], hidden.shape[0]
-    width = features[0].shape[1]
+    width = features.shape[2]
     twice = 2 * group
-    blocks = [pl.ds(pl.multiple_of((chan ^ k) * width, width), width) for k in range(len(features))]
+    copies = fetch(sources, [features.at[k] for k in range(c)], arrived)
+    devices, tall = shards.shape[0], weights.shape[0] * c // shards.shape[0]
+    halves = weights.shape[1] // (c * LANES)
+    copies += fetch(
+        [shards.at[a, pl.ds(k * tall, tall), :] for a in range(devices) for k in range(halves)],
+        [
+            weights.at[pl.ds(a // c * tall, tall), pl.ds((a % c * halves + k) * LANES, LANES)]
+            for a in range(devices)
+            for k in range(halves)
+        ],
+        arrived,
+        c,
+    )
+    blocks = [pl.ds(pl.multiple_of((chan ^ k) * width, width), width) for k in range(c)]
     for k, cols in enumerate(blocks):
         mean, scale = statistics(sums, count, cols)
         gain = scale * norms[0:1, cols]
         shift = norms[1:2, cols] - mean * gain
+        copies[k].wait()
 
         def forward(step, pool, k=k, cols=cols, gain=gain, shift=shift):
             part = rows_of(step)
-            value = hidden[part, cols] * gain + shift + features[k][part, :].astype(F32)
+            value = hidden[part, cols] * gain + shift + features[k, part, :].astype(F32)
             sigma = sigmoid(value)
             value = value * sigma
             upper[part, cols] = sigma + value - value * sigma
@@ -306,10 +356,12 @@
         pool = (pool + pltpu.roll(pool, group, 0)) / pixels
         packed[:, cols] = pool.astype(BF16)
     depth, space = weights.shape
+    for copy in copies[c:]:
+        copy.wait()
     pooled = packed[:, 0:depth]
     logits = dot(pooled, weights[...])
     column = lax.broadcasted_iota(jnp.int32, logits.shape, 1)
-    valid = lax.rem(column, space // len(features)) < classes
+    valid = lax.rem(column, space // c) < classes
     top = jnp.max(jnp.where(valid, logits, -jnp.inf), axis=1, keepdims=True)
     grown = jnp.where(valid, jnp.exp(logits - top), 0.0)
     spread = top + jnp.log(jnp.sum(grown, axis=1, keepdims=True))
@@ -336,7 +388,8 @@
         first, second = lax.fori_loop(0, rows // CHUNK, backward, (zero, zero))
         out_sums[0:1, cols] = col_sum(first)
         out_sums[1:2, cols] = col_sum(second) * scale
-    out_sums[2:3, :] = jnp.broadcast_to(loss[...], (1, out_sums.shape[1]))
+    wide = hidden.shape[1]
+    out_sums[:, wide:] = jnp.broadcast_to(loss[...], (2, out_sums.shape[1] - wide))
 
 
 def lower(upper, hidden, sums, back_sums, norms, count, part, cols):
@@ -410,41 +463,51 @@
             out[a] = block(lax.div(other, c), lax.rem(other, c))
 
 
-def grad_out_kernel(c, masks, me, act, down, *refs):
-    *outs, whole = refs
-    for start in range(0, whole.shape[1], 512):
-        cols = slice(start, start + 512)
-        whole[:, cols] = dot(act[...], down[:, cols], ((0,), (0,))).astype(BF16)
-    rows, width = outs[0].shape[1:]
-    spread_blocks(
-        me[0] * c + me[1], c, outs, masks, lambda i, j: whole[at(j, rows), at(i, width)]
-    )
-
-
-def grad_mid_kernel(c, masks, me, cols, down, *refs):
-    *outs, whole = refs
-    depth = whole.shape[1]
+def turned(value):
+    return value.astype(F32).T.astype(BF16)
+
+
+def grad_mid_kernel(c, masks, size, group, me, act, down, act_two, down_three, *refs):
+    *outs, whole, pad, cols, whole_out = refs
+    rows, depth = act.shape
+    line = size * group
+    pad[1, 0:line, :] = jnp.zeros((line, depth), F32)
+    pad[1, line + rows :, :] = jnp.zeros((line, depth), F32)
+    pad[1, line : line + rows, :] = down[...].astype(F32)
+    fill(pad, size, group)
+    windows(pad, cols, size, group)
+    left = turned(act[...])
     for tap in range(9):
-        whole[tap] = dot(
-            cols[:, tap * depth : (tap + 1) * depth], down[...], ((0,), (0,))
-        ).astype(BF16)
-    rows, width = outs[0].shape[2:]
-    spread_blocks(
-        me[0] * c + me[1], c, outs, masks, lambda i, j: whole[:, at(i, rows), at(j, width)]
-    )
+        whole[tap] = dot(left, cols[:, (8 - tap) * depth : (9 - tap) * depth]).astype(BF16)
+    left = turned(act_two[...])
+    wide = whole_out.shape[1]
+    for start in range(0, wide, 512):
+        part = slice(start, start + 512)
+        whole_out[:, part] = dot(left, down_three[:, part]).astype(BF16)
+    height, width = outs[0].shape[2:]
+    number = me[0] * c + me[1]
+    for out, row in zip(outs, masks):
+        for a, mask in enumerate(row):
+            other = number ^ mask
+            i, j = lax.div(other, c), lax.rem(other, c)
+            out[a, 0:9] = whole[:, at(i, height), at(j, width)]
+            for k in range(4):
+                out[a, 9 + k] = whole_out[at(2 * j + k // 2, height), at(2 * i + k % 2, width)]
 
 
 def grad_in_kernel(count, c, masks, me, upper, hidden, sums, norms, back_sums, *refs):
-    features, outs, whole, down = refs[:c], refs[c:-2], refs[-2], refs[-1]
+    sources, outs, (whole, down, features, arrived) = refs[:c], refs[c:-4], refs[-4:]
+    copies = fetch(sources, [features.at[k] for k in range(c)], arrived)
     rows = upper.shape[0]
     for step in range(rows // CHUNK):
         part = slice(step * CHUNK, (step + 1) * CHUNK)
         down[part, :] = lower(
             upper, hidden, sums, back_sums, norms, count, part, slice(None)
         ).astype(BF16)
-    depth = features[0].shape[1]
-    for k, part in enumerate(features):
-        whole[at(me[1] ^ k, depth), :] = dot(part[...], down[...], ((0,), (0,))).astype(BF16)
+    depth = features.shape[2]
+    for k in range(c):
+        copies[k].wait()
+        whole[at(me[1] ^ k, depth), :] = dot(features[k], down[...], ((0,), (0,))).astype(BF16)
     height, width = outs[0].shape[1:]
     spread_blocks(
         me[0] * c + me[1], c, outs, masks, lambda i, j: whole[at(i, height), at(j, width)]
@@ -455,11 +518,41 @@
     return (one.astype(F32) + other.astype(F32)).astype(BF16)
 
 
-def add_first_kernel(arrived, own, *outs):
+def add_quarters_kernel(arrived, own, *outs):
     z = own.shape[0] // 4
     for low, out in enumerate(outs):
         for k in range(z):
             out[k] = add_low(own[low * z + k], arrived[low * z + k])
+
+
+def add_first_kernel(plan, arrived, own, *outs):
+    z = own.shape[0] // 4
+    for (start, stop, order), send, keep in zip(plan, outs[0::2], outs[1::2]):
+        for low in range(4):
+            inside = low // 2 if order[0] == 2 else low % 2
+            out = send if low & (order[0] // 2) else keep
+            for k in range(z):
+                entry = low * z + k
+                out[inside * z + k] = add_low(own[entry, start:stop], arrived[entry, start:stop])
+
+
+def add_second_kernel(*refs):
+    parts = len(refs) // 4
+    arrived, keeps, outs = refs[:parts], refs[parts : 2 * parts], refs[2 * parts :]
+    for one, other, send, keep in zip(arrived, keeps, outs[0::2], outs[1::2]):
+        z = send.shape[0]
+        for k in range(z):
+            keep[k] = add_low(one[k], other[k])
+            send[k] = add_low(one[z + k], other[z + k])
+
+
+def add_third_kernel(plan, *refs):
+    parts = len(plan)
+    arrived, keeps, outs = refs[:parts], refs[parts : 2 * parts], refs[2 * parts :]
+    for (start, stop, _), one, other in zip(plan, arrived, keeps):
+        for k, out in enumerate(outs):
+            value = one[k].astype(F32) + other[k].astype(F32)
+            out[start:stop] = value if k == 0 else value.astype(BF16)
 
 
 def add_next_kernel(kept, one, two, three, *outs):
@@ -516,15 +609,17 @@
     laid = features.transpose(1, 2, 0, 3).reshape(pixels, images, deep)
     narrow_mid = conv_mid.reshape(9, fan_in, fan_out)
     sources = (laid, conv_in, narrow_mid, conv_out, classifier)
-    own, mate, other, away, low_in, low_mid, low_out, low_head = call(
+    own, mate, other, away, low_in, low_mid, low_head = call(
         functools.partial(prepare_kernel, c),
         [((rows, deep), BF16)] * c
-        + [(x.shape, BF16) for x in (conv_in, narrow_mid, conv_out)]
+        + [(conv_in.shape, BF16), ((13 if aligned else 9, fan_in, fan_out), BF16)]
         + [((tall * (space // LANES), LANES), BF16)],
-        me, *[pltpu.with_memory_space_constraint(x, pltpu.HBM) for x in sources], space=pltpu.HBM,
+        me, *sources, remain=5,
         scratch=[(x.shape, jnp.dtype(x.dtype).type) for x in sources],
         semaphores=[pltpu.SemaphoreType.DMA((5,))],
     )
+    if not aligned:
+        low_mid = jnp.concatenate([low_mid, conv_out.astype(BF16).reshape(4, fan_in, fan_out)])
     away, other = swap(away, 2, n), swap(other, 2, n)
     high_in = gather_high(low_in, n)
     low_head = lax.all_gather(low_head, AXES)
@@ -532,7 +627,6 @@
     low_in, side_in = gather_low(high_in, False, n, (away, other))
     high_mid = gather_high(following(low_mid, high_in[1]), n)
     low_mid, _ = gather_low(high_mid, True, n, side_in)
-    high_out = gather_high(following(low_out, high_mid[1]), n)
 
     narrow = conv_in.shape[1]
     own = lax.dynamic_index_in_dim(labels.reshape(c, group), chan, 0, keepdims=False)
@@ -549,45 +643,46 @@
     carried = table.reshape(-1, mid)
     own_weight = jnp.concatenate([own_weight, carried])
 
-    def assembled(parts, shape, wide_rows):
-        if parts[0][0].shape[-1] % LANES == 0:
-            plan = [masks for _, masks in parts]
-            kernel = functools.partial(assemble_kernel, c, plan, wide_rows)
-            return call(kernel, [(shape, BF16)], me, *[array for array, _ in parts])[0]
-        blocks = jnp.concatenate([array for array, _ in parts], axis=0)
-        order = jnp.array([mask for _, masks in parts for mask in masks])
-        blocks = jnp.take(blocks, jnp.argsort(order ^ number), axis=0)
-        blocks = blocks.reshape((d, c) + blocks.shape[1:])
-        return blocks.transpose(1, 2, 0, 3).reshape(shape)
-
-    whole_in = assembled(low_in, (wide, mid), True)
+    def assembled(kernel, parts, *shapes):
+        kernel = functools.partial(kernel, c, [masks for _, masks in parts])
+        return call(kernel, [(shape, BF16) for shape in shapes], me, *[array for array, _ in parts])
+
+    (whole_in,) = assembled(assemble_kernel, low_in, (wide, mid))
+    feature_space = [((c, rows, deep), jnp.bfloat16)]
+    feature_ends = [pltpu.SemaphoreType.DMA((c,))]
     hidden_one, sums_one = call(
-        first_kernel, [((rows, mid), F32), ((2 + own_weight.shape[0], mid), F32)], me, own_weight, *pieces, whole_in,
-        flops=2 * rows * wide * mid,
-    )
-    sums_one, half_way, _ = total(sums_one, n)
+        functools.partial(first_kernel, c),
+        [((rows, mid), F32), ((2 + own_weight.shape[0], mid), F32)], me, own_weight, whole_in, *pieces,
+        flops=2 * rows * wide * mid, scratch=feature_space, semaphores=feature_ends, remain=c,
+    )
+    sums_one, *_ = total(sums_one, n)
     weight_sum = sums_one[2, 0]
     tables = sums_one[3:].reshape(2, c, -1)
     norms_one = tables[:, :, :narrow].reshape(2, mid)
     norms_two = tables[:, :, narrow : 2 * narrow].reshape(2, mid)
     norms_three = tables[:, :, 2 * narrow :].reshape(2, wide)
 
-    low_out, _ = gather_low(high_out, False, n, half_way)
-    whole_mid = assembled(low_mid, (9, mid, mid), True).reshape(9 * mid, mid)
+    if aligned:
+        whole_mid, whole_out = assembled(assemble_mid_kernel, low_mid, (9, mid, mid), (mid, wide))
+    else:
+        (whole_mid,) = assembled(assemble_mid_kernel, low_mid, (9, mid, mid))
+        blocks = jnp.concatenate([array[:, 9:] for array, _ in low_mid])
+        order = jnp.array([mask for _, masks in low_mid for mask in masks])
+        blocks = jnp.take(blocks, jnp.argsort(order ^ number), axis=0)
+        blocks = blocks.reshape((d, c) + conv_out.shape)
+        whole_out = blocks.transpose(1, 2, 0, 3).reshape(mid, wide)
+    whole_mid = whole_mid.reshape(9 * mid, mid)
     line = size * group
     padded = ((3, rows + 2 * line, mid), jnp.float32)
-    cols, hidden_two, sums_two = call(
+    many = ((rows, 9 * mid), jnp.bfloat16)
+    act_one, hidden_two, sums_two = call(
         functools.partial(second_kernel, count, size, group),
-        [((rows, 9 * mid), BF16), ((rows, mid), F32), ((2, mid), F32)],
+        [((rows, mid), BF16), ((rows, mid), F32), ((2, mid), F32)],
         me, hidden_one, sums_one, norms_one, whole_mid,
-        flops=18 * rows * mid * mid, scratch=[padded],
-    )
-    whole_head = call(
-        functools.partial(assemble_head_kernel, c), [((wide, c * space), BF16)], me, low_head
-    )[0]
-    sums_two, *_ = total(sums_two, n, None, whole_head)
-
-    whole_out = assembled(low_out, (mid, wide), False)
+        flops=18 * rows * mid * mid, scratch=[padded, many],
+    )
+    sums_two, *_ = total(sums_two, n)
+
     act_two, hidden_three, sums_three = call(
         functools.partial(third_kernel, count),
         [((rows, mid), BF16), ((rows, wide), F32), ((2, wide), F32)],
@@ -598,14 +693,16 @@
 
     row_weights = jnp.stack([weight_row, weight_row / weight_sum], axis=1)
     upper_three, back_three, packed, _ = call(
-        functools.partial(head_kernel, count, pixels, group, classes),
-        [((rows, wide), F32), ((3, wide), F32), ((2 * group, wide + c * space), BF16), ((1, 1), F32)],
-        me, hidden_three, sums_three, norms_three, row_weights, target, whole_head, *pieces,
-        flops=4 * 8 * wide * c * space,
+        functools.partial(head_kernel, count, pixels, group, classes, c),
+        [((rows, wide), F32), ((2, wide + LANES), F32), ((2 * group, wide + c * space), BF16), ((1, 1), F32)],
+        me, hidden_three, sums_three, norms_three, row_weights, target, low_head, *pieces,
+        flops=4 * 8 * wide * c * space, remain=1 + c,
+        scratch=feature_space + [((wide, c * space), jnp.bfloat16)],
+        semaphores=[pltpu.SemaphoreType.DMA((c + n * (space // LANES),))],
     )
     everything = lax.all_gather(packed, AXES, axis=0, tiled=True)
     back_three, *_ = total(back_three, n)
-    loss_sum = back_three[2, 0]
+    loss_sum = back_three[0, wide]
 
     down_three, upper_two, back_two = call(
         functools.partial(back_three_kernel, count),
@@ -618,55 +715,65 @@
         return [((n // 2,) + shape, BF16)] * 2
 
     masks = slot_masks(n)
-    if aligned:
-        parts_out = call(
-            functools.partial(grad_out_kernel, c, masks), blocks_of(conv_out.shape),
-            me, act_two, down_three, flops=2 * rows * mid * wide, scratch=[((mid, wide), BF16)],
-        )
-    else:
-        whole = dot(act_two, down_three, ((0,), (0,))).astype(BF16)
-        whole = whole.reshape((c, conv_out.shape[0], d, conv_out.shape[1])).transpose(2, 0, 1, 3)
-        whole = whole.reshape((n,) + conv_out.shape)
-        parts_out = [jnp.take(whole, jnp.array(row) ^ number, axis=0) for row in masks]
-    back_two, half_way, _ = total(back_two, n, None, parts_out[0])
-    kept_out, *sends_out = scatter_start(*parts_out, n)
-    sends_out = following(sends_out, half_way)
+    back_two, *_ = total(back_two, n)
 
     down_two, upper_one, back_one = call(
         functools.partial(back_two_kernel, count, size, group),
         [((rows, mid), BF16), ((rows, mid), F32), ((2, mid), F32)],
         me, upper_two, hidden_two, sums_two, norms_two, back_two, whole_mid,
         hidden_one, sums_one, norms_one,
-        flops=18 * rows * mid * mid, scratch=[padded, ((rows, 9 * mid), BF16)],
-    )
-    arrived_out = [swap(send, mask, n) for send, mask in zip(sends_out, (2, 4, 6))]
-    parts_mid = call(
-        functools.partial(grad_mid_kernel, c, masks), blocks_of((9, fan_in, fan_out)),
-        me, cols, down_two, flops=18 * rows * mid * mid, scratch=[((9, mid, mid), BF16)],
-    )
-    kept_mid, *sends_mid = scatter_start(*parts_mid, n)
-    back_one, half_way, _ = total(back_one, n, None, sends_mid[2])
-    sends_mid = following(sends_mid, half_way)
-    far_mid = swap(sends_mid[2], 6, n)
-    sums_out = scatter_next(kept_out, arrived_out, n)
-    upper_one = following(upper_one, (far_mid, sums_out[0]))
+        flops=18 * rows * mid * mid, scratch=[padded, many],
+    )
+
+    back_one = back_one + swap(back_one, 1, n)
+    down_two = following(down_two, back_one)
+    if aligned:
+        parts_mid = call(
+            functools.partial(grad_mid_kernel, c, masks, size, group), blocks_of((13, fan_in, fan_out)),
+            me, act_one, down_two, act_two, down_three, flops=18 * rows * mid * mid,
+            scratch=[((9, mid, mid), jnp.bfloat16), padded, many, ((mid, wide), jnp.bfloat16)],
+        )
+    else:
+        pad = jnp.pad(act_one.reshape(size, size, group, mid), ((1, 1), (1, 1), (0, 0), (0, 0)))
+        whole = [
+            dot(pad[i : i + size, j : j + size].reshape(rows, mid), down_two, ((0,), (0,))).astype(BF16)
+            for i in range(3)
+            for j in range(3)
+        ]
+        whole = jnp.stack(whole).reshape(9, d, fan_in, c, fan_out).transpose(1, 3, 0, 2, 4)
+        whole_two = dot(act_two, down_three, ((0,), (0,))).astype(BF16)
+        whole_two = whole_two.reshape((c, conv_out.shape[0], d, conv_out.shape[1])).transpose(2, 0, 1, 3)
+        whole_two = whole_two.reshape(d, c, 4, fan_in, fan_out)
+        whole = jnp.concatenate([whole, whole_two], axis=2).reshape(n, 13, fan_in, fan_out)
+        parts_mid = [jnp.take(whole, jnp.array(row) ^ number, axis=0) for row in masks]
+    plan = [(0, 7, (4, 2)), (7, 13, (2, 4))]
+    sends, keeps = split_start(*parts_mid, plan, n)
+    back_one, half_way = total(back_one, n, sends[0], True)
+    sends = following(sends, half_way)
+    arrived = [swap(send, order[0], n) for send, (_, _, order) in zip(sends, plan)]
+    sends, keeps = split_second(arrived, keeps, n)
+    upper_one = following(upper_one, sends)
     parts_in = call(
         functools.partial(grad_in_kernel, count, c, masks), blocks_of(conv_in.shape),
         me, upper_one, hidden_one, sums_one, norms_one, back_one, *pieces,
-        flops=2 * rows * mid * wide, scratch=[((wide, mid), BF16), ((rows, mid), BF16)],
-    )
-    last_out = scatter_last(sums_out, n)
-    arrived_mid = [swap(sends_mid[0], 2, n), swap(sends_mid[1], 4, n), far_mid]
+        flops=2 * rows * mid * wide, remain=c, semaphores=feature_ends,
+        scratch=[((wide, mid), jnp.bfloat16), ((rows, mid), jnp.bfloat16)] + feature_space,
+    )
+    arrived = [swap(send, order[1], n) for send, (_, _, order) in zip(sends, plan)]
     kept_in, *sends_in = scatter_start(*parts_in, n)
+    last_mid = scatter_last(split_third(arrived, keeps, plan, n), n)
     arrived_in = [swap(send, mask, n) for send, mask in zip(sends_in, (2, 4, 6))]
-    last_mid = scatter_last(scatter_next(kept_mid, arrived_mid, n), n)
     arrived_in, last_mid = lax.optimization_barrier((arrived_in, last_mid))
     sums_in = scatter_next(kept_in, arrived_in, n)
     last_mid = following(last_mid, sums_in[0])
-    grad_out = added(last_out)
-    grad_mid = added(last_mid).reshape(conv_mid.shape)
+    grad_mid = added(last_mid)
+    grad_mid, grad_out = grad_mid[:9].reshape(conv_mid.shape), grad_mid[9:]
+    if aligned:
+        grad_out = grad_out.reshape(2, 2, fan_in, fan_out).transpose(0, 2, 1, 3)
+    grad_out = grad_out.reshape(conv_out.shape)
     grad_in = added(scatter_last(sums_in, n))
 
+    everything = following(everything, sums_in[0])
     pooled = lax.dynamic_slice_in_dim(everything, dp * tall, tall, axis=1)
     upper_logits = lax.dynamic_slice_in_dim(everything, wide + chan * space, space, axis=1)
     grad_head = 0.5 * dot(pooled, upper_logits, ((0,), (0,)))[:, :classes]

time: 316 us -> 296 us (0.937)
  local copies, waits for them, and re-layouts: 33.9 us -> 10.1 us
  waiting for transfers between devices: 93.8 us -> 112 us
  starting transfers between devices: 109 us -> 100 us
  other arithmetic: 14.3 us -> 7.99 us
    unnamed x129 -> x93, local copies, waits for them, and re-layouts: 29.5 us -> 8.45 us
    ppermute x99 -> x83, waiting for transfers between devices: 93.7 us -> 112 us  [swap(): return lax.ppermute(array, AXES, [(d, d ^ mask) for d in range(n)])]
    ppermute x99 -> x83, starting transfers between devices: 108 us -> 100 us  [swap(): return lax.ppermute(array, AXES, [(d, d ^ mask) for d in range(n)])]
    pallas_call x20 -> x16, Pallas kernels: 46.5 us -> 47.7 us  [call(): pl.pallas_call(kernel, out_shape=shapes, in_specs=specs, out_specs=[pl.Bl...]
  transfers between devices with their start and end apart: 101 -> 85, of which waited for: 41 -> 45; matrix products, arithmetic and copies ran while one was open for 7% -> 4% of each run, Pallas kernels for 8% -> 8%
where the time goes in v3:
time: 296 us
  waiting for transfers between devices  112 us (38%)
  starting transfers between devices  100 us (34%)
  Pallas kernels  47.7 us (16%)
  between operations  15.6 us (5%)
  local copies, waits for them, and re-layouts  10.1 us (3%)
  other arithmetic  7.99 us (3%)
    ppermute x83, waiting for transfers between devices, swap(): return lax.ppermute(array, AXES, [(d, d ^ mask) for d in range(n)])  112 us
    ppermute x83, starting transfers between devices, swap(): return lax.ppermute(array, AXES, [(d, d ^ mask) for d in range(n)])  100 us
    pallas_call x16, Pallas kernels, call(): pl.pallas_call(kernel, out_shape=shapes, in_specs=specs, out_specs=[pl.Bl...  47.7 us
    unnamed x93, local copies, waits for them, and re-layouts  8.45 us
  transfers between devices with their start and end apart: 85, of which 45 were waited for; matrix products, arithmetic and copies ran while one was open for 4% of the time, Pallas kernels for 8%

profile of v3, /device:TPU:0, one launch (start us, length us, event | category | flops | bytes accessed | tf_op | source)
XLA Modules:
  0.0 295.9 jit_solution(13181104814310641725)
XLA Ops:
  7.3 3.7 %shard_map.345 = (bf16[400,512]{1,0:T(8,128)(2,1)S(1)}, bf16[400,512]{1,0:T(8,128)(2,1)S(1)}, bf16[400,512]{1,0:T(8,128)(2,1)S(1)}, bf16[400,512]{1,0:T(8,128)(2...) custom-call(s32[2]{0:T(128)S(1)} %pad_add_fusion.me, ...), custom_call_target="tpu_custom_call" | custom-call | bytes 4499464 | tf_op jit(solution)/shard_map/pallas_call | solution.py:118
  12.6 3.0 %collective-permute-start.4 = (bf16[400,512]{1,0:T(8,128)(2,1)S(1)}, bf16[400,512]{1,0:T(8,128)(2,1)S(1)}, u32[]{:S(2)}, u32[]{:S(2)}) collective-permute-start(bf16[400,512]{1,0:T(8,128)(2,1)S(1)} %get-tuple-element.94), channel_id=1, source_target_pairs={{0,2},{1,3},{2,0},{3,1},{4,6},{5,7},{6,4},{7,5},{8,10},{9,11},{10,... | collective-permute-start | bytes 1228808 | tf_op jit(solution)/shard_map/ppermute | solution.py:24
  15.7 2.0 collective-permute-start
  17.7 2.2 collective-permute-done
  20.0 2.0 collective-permute-start.21
  22.0 2.6 collective-permute-start.1
  24.6 4.5 %collective-permute-done.1 = bf16[256,128]{1,0:T(8,128)(2,1)S(1)} collective-permute-done((bf16[256,128]{1,0:T(8,128)(2,1)S(1)}, bf16[256,128]{1,0:T(8,128)(2,1)S(1)}, u32[]{:S(2)}, u32[]{:S(2)}) %collective-permute-start.1) | collective-permute-done | bytes 65568 | tf_op jit(solution)/shard_map/ppermute | solution.py:24
  29.1 3.4 %collective-permute-start.22 = (bf16[13,64,128]{2,1,0:T(8,128)(2,1)S(1)}, bf16[13,64,128]{2,1,0:T(8,128)(2,1)S(1)}, u32[]{:S(2)}, u32[]{:S(2)}) collective-permute-start(bf16[13,64,128]{2,1,0:T(8,128)(2,1)S(1)} %get-tuple-element.101), channel_id=1, source_target_pairs={{0,16},{1,17},{2,18},{3,19},{4,20},{5,21},{6,22},{7,23},{8,24},{9,... | collective-permute-start | bytes 638984 | tf_op jit(solution)/shard_map/ppermute | solution.py:24
  39.2 8.2 %collective-permute-done.22 = bf16[13,64,128]{2,1,0:T(8,128)(2,1)S(1)} collective-permute-done((bf16[13,64,128]{2,1,0:T(8,128)(2,1)S(1)}, bf16[13,64,128]{2,1,0:T(8,128)(2,1)S(1)}, u32[]{:S(2)}, u32[]{:S(2)}) %collective-permute-start.22) | collective-permute-done | bytes 213024 | tf_op jit(solution)/shard_map/ppermute | solution.py:24
  58.0 3.4 %shard_map.347 = (f32[400,512]{1,0:T(8,128)S(1)}, f32[15,512]{1,0:T(8,128)S(1)}) custom-call(s32[2]{0:T(128)S(1)} %pad_add_fusion.me, f32[13,512]{1,0:T(8,128)S(1)} %concatenate.10.carried, bf16[2048,512]{1,0:T(8,128)(2,1)S(1)} %shard_map.346.weights, bf16[400,512]{1,0:T(8,128)(2,1)} %copy-done.1, bf16[400,512]{1,0:T(8,128)(2,1)} %collective-permute-done.12.refs_1_, ...), custom_call_target="tpu_custom_call" | custom-call | flops 838860800 | bytes 4612104 | tf_op jit(solution)/shard_map/pallas_call | solution.py:118
  63.7 2.5 collective-permute-start.17
  66.2 8.3 %collective-permute-done.15 = f32[15,512]{1,0:T(8,128)S(1)} collective-permute-done((f32[15,512]{1,0:T(8,128)S(1)}, f32[15,512]{1,0:T(8,128)S(1)}, u32[]{:S(2)}, u32[]{:S(2)}) %collective-permute-start.15) | collective-permute-done | bytes 30752 | tf_op jit(solution)/shard_map/ppermute | solution.py:24
  76.1 8.1 %collective-permute-start.18 = (f32[15,512]{1,0:T(8,128)S(1)}, f32[15,512]{1,0:T(8,128)S(1)}, u32[]{:S(2)}, u32[]{:S(2)}) collective-permute-start(f32[15,512]{1,0:T(8,128)S(1)} %add_add_fusion.3), channel_id=1, source_target_pairs={{0,8},{1,9},{2,10},{3,11},{4,12},{5,13},{6,14},{7,15},{8,0},{9,1},... | collective-permute-start | bytes 92168 | tf_op jit(solution)/shard_map/ppermute | solution.py:24
  84.2 2.4 collective-permute-start.20
  87.6 3.3 %collective-permute-start.27 = (bf16[2,13,64,128]{3,2,1,0:T(8,128)(2,1)S(1)}, bf16[2,13,64,128]{3,2,1,0:T(8,128)(2,1)}, u32[]{:S(2)}, u32[]{:S(2)}) collective-permute-start(bf16[2,13,64,128]{3,2,1,0:T(8,128)(2,1)S(1)} %slice.48), channel_id=1, source_target_pairs={{0,2},{1,3},{2,0},{3,1},{4,6},{5,7},{6,4},{7,5},{8,10},{9,11},{10,... | collective-permute-start | bytes 1277960 | tf_op jit(solution)/shard_map/ppermute | solution.py:24
  91.4 3.7 %collective-permute-done.26.refs_3_ = bf16[2,13,64,128]{3,2,1,0:T(8,128)(2,1)} collective-permute-done((bf16[2,13,64,128]{3,2,1,0:T(8,128)(2,1)S(1)}, bf16[2,13,64,128]{3,2,1,0:T(8,128)(2,1)}, u32[]{:S(2)}, u32[]{:S(2)}) %collective-permute-start.26) | collective-permute-done | bytes 426016 | tf_op jit(solution)/shard_map/ppermute | solution.py:24
  99.2 3.5 %shard_map.348 = (bf16[9,512,512]{2,1,0:T(8,128)(2,1)S(1)}, bf16[512,2048]{1,0:T(8,128)(2,1)S(1)}) custom-call(s32[2]{0:T(128)S(1)} %pad_add_fusion.me, bf16[4,13,64,128]{3,2,1,0:T(8,128)(2,1)S(1)} %pad_maximum_fusion.refs_0_, bf16[4,13,64,128]{3,2,1,0:T(8,128)(2,1)S(1)} %collective-permute-done.24.refs_1_, ...), custom_call_target="tpu_custom_call" | custom-call | bytes 13631496 | tf_op jit(solution)/shard_map/pallas_call | solution.py:118
  102.7 2.8 shard_map.349
  107.4 2.0 collective-permute-start.34
  111.1 2.0 collective-permute-done.35
  116.5 2.4 collective-permute-start.39
  130.7 2.1 collective-permute-done.43
  132.9 3.0 %collective-permute-start.45 = (f32[2,2048]{1,0:T(2,128)S(1)}, f32[2,2048]{1,0:T(2,128)S(1)}, u32[]{:S(2)}, u32[]{:S(2)}) collective-permute-start(f32[2,2048]{1,0:T(2,128)S(1)} %add_add_fusion.7), channel_id=1, source_target_pairs={{0,16},{1,17},{2,18},{3,19},{4,20},{5,21},{6,22},{7,23},{8,24},{9,... | collective-permute-start | bytes 49160 | tf_op jit(solution)/shard_map/ppermute | solution.py:24
  137.6 3.8 %collective-permute-done.46 = f32[2,2048]{1,0:T(2,128)S(1)} collective-permute-done((f32[2,2048]{1,0:T(2,128)S(1)}, f32[2,2048]{1,0:T(2,128)S(1)}, u32[]{:S(2)}, u32[]{:S(2)}) %collective-permute-start.46) | collective-permute-done | bytes 16416 | tf_op jit(solution)/shard_map/ppermute | solution.py:24
  141.5 7.8 %shard_map.351 = (f32[400,2048]{1,0:T(8,128)S(1)}, f32[2,2176]{1,0:T(2,128)S(1)}, bf16[8,3072]{1,0:T(8,128)(2,1)}, f32[1,1]{1,0:T(1,128)}) custom-call(s32[2]{0:T(128)S(1)} %pad_add_fusion.me, f32[400,2048]{1,0:T(8,128)S(1)} %get-tuple-element.107.hidden, f32[2,2048]{1,0:T(2,128)S(1)} %add_add_fusion.6.sums, f32[2,2048]{1,0:T(2,128)S(1)} %bitcast.70, ...), custom_call_target="tpu_custom_call" | custom-call | flops 67108864 | bytes 12518476 | tf_op jit(solution)/shard_map/pallas_call | solution.py:118
  154.3 2.1 collective-permute-done.49
  159.7 2.4 collective-permute-start.53
  162.5 2.8 collective-permute-done.53
  165.3 2.1 shard_map.352
  172.4 2.4 collective-permute-done.57
  174.9 3.0 %collective-permute-start.59 = (f32[2,512]{1,0:T(2,128)S(1)}, f32[2,512]{1,0:T(2,128)S(1)}, u32[]{:S(2)}, u32[]{:S(2)}) collective-permute-start(f32[2,512]{1,0:T(2,128)S(1)} %add_add_fusion.11), channel_id=1, source_target_pairs={{0,16},{1,17},{2,18},{3,19},{4,20},{5,21},{6,22},{7,23},{8,24},{9,... | collective-permute-start | bytes 12296 | tf_op jit(solution)/shard_map/ppermute | solution.py:24
  179.4 3.8 %collective-permute-done.60 = f32[2,512]{1,0:T(2,128)S(1)} collective-permute-done((f32[2,512]{1,0:T(2,128)S(1)}, f32[2,512]{1,0:T(2,128)S(1)}, u32[]{:S(2)}, u32[]{:S(2)}) %collective-permute-start.60) | collective-permute-done | bytes 4128 | tf_op jit(solution)/shard_map/ppermute | solution.py:24
  183.3 3.0 %shard_map.353 = (bf16[400,512]{1,0:T(8,128)(2,1)S(1)}, f32[400,512]{1,0:T(8,128)S(1)}, f32[2,512]{1,0:T(2,128)S(1)}) custom-call(s32[2]{0:T(128)S(1)} %pad_add_fusion.me, f32[400,512]{1,0:T(8,128)S(1)} %get-tuple-element.112.upper, f32[400,512]{1,0:T(8,128)S(1)} %copy-done.3, f32[2,512]{1,0:T(2,128)S(1)} %add_add_fusion.12.sums.sums_two, ...), custom_call_target="tpu_custom_call" | custom-call | flops 1887436800 | bytes 8456200 | tf_op jit(solution)/shard_map/pallas_call | solution.py:118
  188.4 7.2 %shard_map.354 = (bf16[16,13,64,128]{3,2,1,0:T(8,128)(2,1)S(1)}, bf16[16,13,64,128]{3,2,1,0:T(8,128)(2,1)}) custom-call(s32[2]{0:T(128)S(1)} %pad_add_fusion.me, bf16[400,512]{1,0:T(8,128)(2,1)S(1)} %copy-done.17, bf16[400,512]{1,0:T(8,128)(2,1)S(1)} %get-tuple-element.118.down, bf16[400,512]{1,0:T(8,128)(2,1)S(1)} %copy-done.15, ...), custom_call_target="tpu_custom_call" | custom-call | flops 1887436800 | bytes 9682952 | tf_op jit(solution)/shard_map/pallas_call | solution.py:118
  195.8 2.0 collective-permute-start.63
  202.8 3.1 %shard_map.355 = (bf16[8,7,64,128]{3,2,1,0:T(8,128)(2,1)S(1)}, bf16[8,7,64,128]{3,2,1,0:T(8,128)(2,1)S(1)}, bf16[8,6,64,128]{3,2,1,0:T(8,128)(2,1)S(1)}, bf16[8,6,64,128]{3,2,1,0:T(8,128)(2,1)S(1)}) custom-call(bf16[16,13,64,128]{3,2,1,0:T(8,128)(2,1)} %collective-permute-done.62.arrived, bf16[16,13,64,128]{3,2,1,0:T(8,128)(2,1)S(1)} %get-tuple-element.122.own), custom_call_target="tpu_custom_call" | custom-call | bytes 10223616 | tf_op jit(solution)/shard_map/pallas_call | solution.py:118
  209.5 2.5 collective-permute-start.70
  212.1 2.9 collective-permute-done.70
  215.0 11.8 %collective-permute-done.67.refs_1_ = bf16[8,6,64,128]{3,2,1,0:T(8,128)(2,1)S(1)} collective-permute-done((bf16[8,6,64,128]{3,2,1,0:T(8,128)(2,1)S(1)}, bf16[8,6,64,128]{3,2,1,0:T(8,128)(2,1)S(1)}, u32[]{:S(2)}, u32[]{:S(2)}) %collective-permute-start.67) | collective-permute-done | bytes 786464 | tf_op jit(solution)/shard_map/ppermute | solution.py:24
  229.5 5.1 %shard_map.357 = (bf16[16,256,128]{2,1,0:T(8,128)(2,1)S(1)}, bf16[16,256,128]{2,1,0:T(8,128)(2,1)}) custom-call(s32[2]{0:T(128)S(1)} %pad_add_fusion.me, f32[400,512]{1,0:T(8,128)S(1)} %copy-done.10, f32[400,512]{1,0:T(8,128)S(1)} %copy-done.6, f32[15,512]{1,0:T(8,128)S(1)} %add_add_fusion.2.sums.sums_one, f32[2,512]{1,0:T(2,128)S(1)} %bitcast.76, ...), custom_call_target="tpu_custom_call" | custom-call | flops 838860800 | bytes 5412872 | tf_op jit(solution)/shard_map/pallas_call | solution.py:118
  234.7 2.0 collective-permute-start.75
  237.9 11.8 %collective-permute-done.76.refs_1_ = bf16[4,6,64,128]{3,2,1,0:T(8,128)(2,1)} collective-permute-done((bf16[4,6,64,128]{3,2,1,0:T(8,128)(2,1)}, bf16[4,6,64,128]{3,2,1,0:T(8,128)(2,1)}, u32[]{:S(2)}, u32[]{:S(2)}) %collective-permute-start.76) | collective-permute-done | bytes 393248 | tf_op jit(solution)/shard_map/ppermute | solution.py:24
  257.2 2.2 collective-permute-start.78
  259.4 2.2 collective-permute-start.79
  262.7 12.2 %collective-permute-done.78 = bf16[13,64,128]{2,1,0:T(8,128)(2,1)S(1)} collective-permute-done((bf16[13,64,128]{2,1,0:T(8,128)(2,1)S(1)}, bf16[13,64,128]{2,1,0:T(8,128)(2,1)S(1)}, u32[]{:S(2)}, u32[]{:S(2)}) %collective-permute-start.78) | collective-permute-done | bytes 213024 | tf_op jit(solution)/shard_map/ppermute | solution.py:24
  275.4 3.9 %collective-permute-start.80 = (bf16[256,128]{1,0:T(8,128)(2,1)S(1)}, bf16[256,128]{1,0:T(8,128)(2,1)S(1)}, u32[]{:S(2)}, u32[]{:S(2)}) collective-permute-start(bf16[256,128]{1,0:T(8,128)(2,1)S(1)} %get-tuple-element.149), channel_id=1, source_target_pairs={{0,8},{1,9},{2,10},{3,11},{4,12},{5,13},{6,14},{7,15},{8,0},{9,1},... | collective-permute-start | bytes 196616 | tf_op jit(solution)/shard_map/ppermute | solution.py:24
  279.4 2.4 collective-permute-start.82
  281.7 2.0 fusion.9
  (298 shorter events, 92.9 us)
Async XLA Ops:
  7.2 134.2 %all-gather.6.cloned.1.call-start = ((), (), s32[]{:S(2)}) async-start(), calls=%async_computation.1 | async-start | bytes 4325376 | tf_op jit(solution)/shard_map/all_gather | solution.py:625
  12.6 262.8 %all-gather.4.cloned.1.call-start = ((), (), s32[]{:S(2)}) async-start(), calls=%async_computation | async-start | bytes 1622016 | tf_op jit(solution)/shard_map/all_gather | solution.py:703
  12.6 23.0 %collective-permute-start.4 = (bf16[400,512]{1,0:T(8,128)(2,1)S(1)}, bf16[400,512]{1,0:T(8,128)(2,1)S(1)}, u32[]{:S(2)}, u32[]{:S(2)}) collective-permute-start(bf16[400,512]{1,0:T(8,128)(2,1)S(1)} %get-tuple-element.94), channel_id=1, source_target_pairs={{0,2},{1,3},{2,0},{3,1},{4,6},{5,7},{6,4},{7,5},{8,10},{9,11},{10,... | collective-permute-start | bytes 1228808 | tf_op jit(solution)/shard_map/ppermute | solution.py:24
  15.6 20.0 %collective-permute-start.3 = (bf16[400,512]{1,0:T(8,128)(2,1)S(1)}, bf16[400,512]{1,0:T(8,128)(2,1)}, u32[]{:S(2)}, u32[]{:S(2)}) collective-permute-start(bf16[400,512]{1,0:T(8,128)(2,1)S(1)} %get-tuple-element.93), channel_id=1, source_target_pairs={{0,2},{1,3},{2,0},{3,1},{4,6},{5,7},{6,4},{7,5},{8,10},{9,11},{10,... | collective-permute-start | bytes 1228808 | tf_op jit(solution)/shard_map/ppermute | solution.py:24
  20.0 18.6 %collective-permute-start.21 = (bf16[13,64,128]{2,1,0:T(8,128)(2,1)S(1)}, bf16[13,64,128]{2,1,0:T(8,128)(2,1)S(1)}, u32[]{:S(2)}, u32[]{:S(2)}) collective-permute-start(bf16[13,64,128]{2,1,0:T(8,128)(2,1)S(1)} %get-tuple-element.101), channel_id=1, source_target_pairs={{0,8},{1,9},{2,10},{3,11},{4,12},{5,13},{6,14},{7,15},{8,0},{9,1},... | collective-permute-start | bytes 638984 | tf_op jit(solution)/shard_map/ppermute | solution.py:24
  22.0 7.1 %collective-permute-start.1 = (bf16[256,128]{1,0:T(8,128)(2,1)S(1)}, bf16[256,128]{1,0:T(8,128)(2,1)S(1)}, u32[]{:S(2)}, u32[]{:S(2)}) collective-permute-start(bf16[256,128]{1,0:T(8,128)(2,1)S(1)} %get-tuple-element.92), channel_id=1, source_target_pairs={{0,16},{1,17},{2,18},{3,19},{4,20},{5,21},{6,22},{7,23},{8,24},{9,... | collective-permute-start | bytes 196616 | tf_op jit(solution)/shard_map/ppermute | solution.py:24
  24.6 9.6 %collective-permute-start.2 = (bf16[256,128]{1,0:T(8,128)(2,1)S(1)}, bf16[256,128]{1,0:T(8,128)(2,1)S(1)}, u32[]{:S(2)}, u32[]{:S(2)}) collective-permute-start(bf16[256,128]{1,0:T(8,128)(2,1)S(1)} %get-tuple-element.92), channel_id=1, source_target_pairs={{0,24},{1,25},{2,26},{3,27},{4,28},{5,29},{6,30},{7,31},{8,16},{9,... | collective-permute-start | bytes 196616 | tf_op jit(solution)/shard_map/ppermute | solution.py:24
  29.1 18.3 %collective-permute-start.22 = (bf16[13,64,128]{2,1,0:T(8,128)(2,1)S(1)}, bf16[13,64,128]{2,1,0:T(8,128)(2,1)S(1)}, u32[]{:S(2)}, u32[]{:S(2)}) collective-permute-start(bf16[13,64,128]{2,1,0:T(8,128)(2,1)S(1)} %get-tuple-element.101), channel_id=1, source_target_pairs={{0,16},{1,17},{2,18},{3,19},{4,20},{5,21},{6,22},{7,23},{8,24},{9,... | collective-permute-start | bytes 638984 | tf_op jit(solution)/shard_map/ppermute | solution.py:24
  34.1 13.8 %collective-permute-start.23 = (bf16[13,64,128]{2,1,0:T(8,128)(2,1)S(1)}, bf16[13,64,128]{2,1,0:T(8,128)(2,1)S(1)}, u32[]{:S(2)}, u32[]{:S(2)}) collective-permute-start(bf16[13,64,128]{2,1,0:T(8,128)(2,1)S(1)} %get-tuple-element.101), channel_id=1, source_target_pairs={{0,24},{1,25},{2,26},{3,27},{4,28},{5,29},{6,30},{7,31},{8,16},{9,... | collective-permute-start | bytes 638984 | tf_op jit(solution)/shard_map/ppermute | solution.py:24
  35.6 11.8 %collective-permute-start.5 = (bf16[4,256,128]{2,1,0:T(8,128)(2,1)S(1)}, bf16[4,256,128]{2,1,0:T(8,128)(2,1)S(1)}, u32[]{:S(2)}, u32[]{:S(2)}) collective-permute-start(bf16[4,256,128]{2,1,0:T(8,128)(2,1)S(1)} %pad_maximum_fusion.1.refs_0_), channel_id=1, source_target_pairs={{0,4},{1,5},{2,6},{3,7},{4,0},{5,1},{6,2},{7,3},{8,12},{9,13},{10,... | collective-permute-start | bytes 786440 | tf_op jit(solution)/shard_map/ppermute | solution.py:24
  37.1 12.5 %collective-permute-start.6 = (bf16[4,256,128]{2,1,0:T(8,128)(2,1)S(1)}, bf16[4,256,128]{2,1,0:T(8,128)(2,1)S(1)}, u32[]{:S(2)}, u32[]{:S(2)}) collective-permute-start(bf16[4,256,128]{2,1,0:T(8,128)(2,1)S(1)} %pad_maximum_fusion.1.refs_0_), channel_id=1, source_target_pairs={{0,2},{1,3},{2,0},{3,1},{4,6},{5,7},{6,4},{7,5},{8,10},{9,11},{10,... | collective-permute-start | bytes 786440 | tf_op jit(solution)/shard_map/ppermute | solution.py:24
  38.6 12.6 %collective-permute-start.7 = (bf16[4,256,128]{2,1,0:T(8,128)(2,1)S(1)}, bf16[4,256,128]{2,1,0:T(8,128)(2,1)S(1)}, u32[]{:S(2)}, u32[]{:S(2)}) collective-permute-start(bf16[4,256,128]{2,1,0:T(8,128)(2,1)S(1)} %pad_maximum_fusion.1.refs_0_), channel_id=1, source_target_pairs={{0,6},{1,7},{2,4},{3,5},{4,2},{5,3},{6,0},{7,1},{8,14},{9,15},{10,... | collective-permute-start | bytes 786440 | tf_op jit(solution)/shard_map/ppermute | solution.py:24
  47.4 5.1 %collective-permute-start.9 = (bf16[4,256,128]{2,1,0:T(8,128)(2,1)S(1)}, bf16[4,256,128]{2,1,0:T(8,128)(2,1)}, u32[]{:S(2)}, u32[]{:S(2)}) collective-permute-start(bf16[4,256,128]{2,1,0:T(8,128)(2,1)S(1)} %collective-permute-done.5.refs_1_), channel_id=1, source_target_pairs={{0,1},{1,0},{2,3},{3,2},{4,5},{5,4},{6,7},{7,6},{8,9},{9,8},{10,11... | collective-permute-start | bytes 786440 | tf_op jit(solution)/shard_map/ppermute | solution.py:24
  48.1 38.6 %collective-permute-start.25 = (bf16[4,13,64,128]{3,2,1,0:T(8,128)(2,1)S(1)}, bf16[4,13,64,128]{3,2,1,0:T(8,128)(2,1)S(1)}, u32[]{:S(2)}, u32[]{:S(2)}) collective-permute-start(bf16[4,13,64,128]{3,2,1,0:T(8,128)(2,1)S(1)} %pad_maximum_fusion.refs_0_), channel_id=1, source_target_pairs={{0,2},{1,3},{2,0},{3,1},{4,6},{5,7},{6,4},{7,5},{8,10},{9,11},{10,... | collective-permute-start | bytes 2555912 | tf_op jit(solution)/shard_map/ppermute | solution.py:24
  49.7 37.9 %collective-permute-start.24 = (bf16[4,13,64,128]{3,2,1,0:T(8,128)(2,1)S(1)}, bf16[4,13,64,128]{3,2,1,0:T(8,128)(2,1)S(1)}, u32[]{:S(2)}, u32[]{:S(2)}) collective-permute-start(bf16[4,13,64,128]{3,2,1,0:T(8,128)(2,1)S(1)} %pad_maximum_fusion.refs_0_), channel_id=1, source_target_pairs={{0,4},{1,5},{2,6},{3,7},{4,0},{5,1},{6,2},{7,3},{8,12},{9,13},{10,... | collective-permute-start | bytes 2555912 | tf_op jit(solution)/shard_map/ppermute | solution.py:24
  52.1 5.9 %collective-permute-start.12 = (bf16[400,512]{1,0:T(8,128)(2,1)}, bf16[400,512]{1,0:T(8,128)(2,1)}, u32[]{:S(2)}, u32[]{:S(2)}) collective-permute-start(bf16[400,512]{1,0:T(8,128)(2,1)} %copy-done.13), channel_id=1, source_target_pairs={{0,1},{1,0},{2,3},{3,2},{4,5},{5,4},{6,7},{7,6},{8,9},{9,8},{10,11... | collective-permute-start | bytes 1228808 | tf_op jit(solution)/shard_map/ppermute | solution.py:24
  52.6 5.4 %collective-permute-start.13 = (bf16[400,512]{1,0:T(8,128)(2,1)}, bf16[400,512]{1,0:T(8,128)(2,1)}, u32[]{:S(2)}, u32[]{:S(2)}) collective-permute-start(bf16[400,512]{1,0:T(8,128)(2,1)} %collective-permute-done.3), channel_id=1, source_target_pairs={{0,1},{1,0},{2,3},{3,2},{4,5},{5,4},{6,7},{7,6},{8,9},{9,8},{10,11... | collective-permute-start | bytes 1228808 | tf_op jit(solution)/shard_map/ppermute | solution.py:24
  62.8 11.8 %collective-permute-start.15 = (f32[15,512]{1,0:T(8,128)S(1)}, f32[15,512]{1,0:T(8,128)S(1)}, u32[]{:S(2)}, u32[]{:S(2)}) collective-permute-start(f32[15,512]{1,0:T(8,128)S(1)} %add.220), channel_id=1, source_target_pairs={{0,2},{1,3},{2,0},{3,1},{4,6},{5,7},{6,4},{7,5},{8,10},{9,11},{10,... | collective-permute-start | bytes 92168 | tf_op jit(solution)/shard_map/ppermute | solution.py:24
  63.3 11.3 %collective-permute-start.16 = (f32[15,512]{1,0:T(8,128)S(1)}, f32[15,512]{1,0:T(8,128)S(1)}, u32[]{:S(2)}, u32[]{:S(2)}) collective-permute-start(f32[15,512]{1,0:T(8,128)S(1)} %add.220), channel_id=1, source_target_pairs={{0,4},{1,5},{2,6},{3,7},{4,0},{5,1},{6,2},{7,3},{8,12},{9,13},{10,... | collective-permute-start | bytes 92168 | tf_op jit(solution)/shard_map/ppermute | solution.py:24
  63.7 12.4 %collective-permute-start.17 = (f32[15,512]{1,0:T(8,128)S(1)}, f32[15,512]{1,0:T(8,128)S(1)}, u32[]{:S(2)}, u32[]{:S(2)}) collective-permute-start(f32[15,512]{1,0:T(8,128)S(1)} %add.220), channel_id=1, source_target_pairs={{0,6},{1,7},{2,4},{3,5},{4,2},{5,3},{6,0},{7,1},{8,14},{9,15},{10,... | collective-permute-start | bytes 92168 | tf_op jit(solution)/shard_map/ppermute | solution.py:24
  76.1 14.7 %collective-permute-start.18 = (f32[15,512]{1,0:T(8,128)S(1)}, f32[15,512]{1,0:T(8,128)S(1)}, u32[]{:S(2)}, u32[]{:S(2)}) collective-permute-start(f32[15,512]{1,0:T(8,128)S(1)} %add_add_fusion.3), channel_id=1, source_target_pairs={{0,8},{1,9},{2,10},{3,11},{4,12},{5,13},{6,14},{7,15},{8,0},{9,1},... | collective-permute-start | bytes 92168 | tf_op jit(solution)/shard_map/ppermute | solution.py:24
  84.2 6.6 %collective-permute-start.19 = (f32[15,512]{1,0:T(8,128)S(1)}, f32[15,512]{1,0:T(8,128)S(1)}, u32[]{:S(2)}, u32[]{:S(2)}) collective-permute-start(f32[15,512]{1,0:T(8,128)S(1)} %add_add_fusion.3), channel_id=1, source_target_pairs={{0,16},{1,17},{2,18},{3,19},{4,20},{5,21},{6,22},{7,23},{8,24},{9,... | collective-permute-start | bytes 92168 | tf_op jit(solution)/shard_map/ppermute | solution.py:24
  84.2 7.1 %collective-permute-start.20 = (f32[15,512]{1,0:T(8,128)S(1)}, f32[15,512]{1,0:T(8,128)S(1)}, u32[]{:S(2)}, u32[]{:S(2)}) collective-permute-start(f32[15,512]{1,0:T(8,128)S(1)} %add_add_fusion.3), channel_id=1, source_target_pairs={{0,24},{1,25},{2,26},{3,27},{4,28},{5,29},{6,30},{7,31},{8,16},{9,... | collective-permute-start | bytes 92168 | tf_op jit(solution)/shard_map/ppermute | solution.py:24
  86.7 8.4 %collective-permute-start.26 = (bf16[2,13,64,128]{3,2,1,0:T(8,128)(2,1)S(1)}, bf16[2,13,64,128]{3,2,1,0:T(8,128)(2,1)}, u32[]{:S(2)}, u32[]{:S(2)}) collective-permute-start(bf16[2,13,64,128]{3,2,1,0:T(8,128)(2,1)S(1)} %slice.47), channel_id=1, source_target_pairs={{0,4},{1,5},{2,6},{3,7},{4,0},{5,1},{6,2},{7,3},{8,12},{9,13},{10,... | collective-permute-start | bytes 1277960 | tf_op jit(solution)/shard_map/ppermute | solution.py:24
  87.6 9.5 %collective-permute-start.27 = (bf16[2,13,64,128]{3,2,1,0:T(8,128)(2,1)S(1)}, bf16[2,13,64,128]{3,2,1,0:T(8,128)(2,1)}, u32[]{:S(2)}, u32[]{:S(2)}) collective-permute-start(bf16[2,13,64,128]{3,2,1,0:T(8,128)(2,1)S(1)} %slice.48), channel_id=1, source_target_pairs={{0,2},{1,3},{2,0},{3,1},{4,6},{5,7},{6,4},{7,5},{8,10},{9,11},{10,... | collective-permute-start | bytes 1277960 | tf_op jit(solution)/shard_map/ppermute | solution.py:24
  90.8 6.3 %collective-permute-start.28 = (bf16[4,13,64,128]{3,2,1,0:T(8,128)(2,1)S(1)}, bf16[4,13,64,128]{3,2,1,0:T(8,128)(2,1)}, u32[]{:S(2)}, u32[]{:S(2)}) collective-permute-start(bf16[4,13,64,128]{3,2,1,0:T(8,128)(2,1)S(1)} %pad_maximum_fusion.refs_0_), channel_id=1, source_target_pairs={{0,1},{1,0},{2,3},{3,2},{4,5},{5,4},{6,7},{7,6},{8,9},{9,8},{10,11... | collective-permute-start | bytes 2555912 | tf_op jit(solution)/shard_map/ppermute | solution.py:24
  90.8 8.3 %collective-permute-start.29 = (bf16[4,13,64,128]{3,2,1,0:T(8,128)(2,1)S(1)}, bf16[4,13,64,128]{3,2,1,0:T(8,128)(2,1)}, u32[]{:S(2)}, u32[]{:S(2)}) collective-permute-start(bf16[4,13,64,128]{3,2,1,0:T(8,128)(2,1)S(1)} %collective-permute-done.24.refs_1_), channel_id=1, source_target_pairs={{0,1},{1,0},{2,3},{3,2},{4,5},{5,4},{6,7},{7,6},{8,9},{9,8},{10,11... | collective-permute-start | bytes 2555912 | tf_op jit(solution)/shard_map/ppermute | solution.py:24
  91.4 7.8 %collective-permute-start.30 = (bf16[4,13,64,128]{3,2,1,0:T(8,128)(2,1)S(1)}, bf16[4,13,64,128]{3,2,1,0:T(8,128)(2,1)}, u32[]{:S(2)}, u32[]{:S(2)}) collective-permute-start(bf16[4,13,64,128]{3,2,1,0:T(8,128)(2,1)S(1)} %collective-permute-done.25.refs_2_), channel_id=1, source_target_pairs={{0,1},{1,0},{2,3},{3,2},{4,5},{5,4},{6,7},{7,6},{8,9},{9,8},{10,11... | collective-permute-start | bytes 2555912 | tf_op jit(solution)/shard_map/ppermute | solution.py:24
  116.5 5.4 %collective-permute-start.39 = (f32[2,512]{1,0:T(2,128)S(1)}, f32[2,512]{1,0:T(2,128)S(1)}, u32[]{:S(2)}, u32[]{:S(2)}) collective-permute-start(f32[2,512]{1,0:T(2,128)S(1)} %add_add_fusion.13), channel_id=1, source_target_pairs={{0,24},{1,25},{2,26},{3,27},{4,28},{5,29},{6,30},{7,31},{8,16},{9,... | collective-permute-start | bytes 12296 | tf_op jit(solution)/shard_map/ppermute | solution.py:24
  135.9 5.5 %collective-permute-start.46 = (f32[2,2048]{1,0:T(2,128)S(1)}, f32[2,2048]{1,0:T(2,128)S(1)}, u32[]{:S(2)}, u32[]{:S(2)}) collective-permute-start(f32[2,2048]{1,0:T(2,128)S(1)} %add_add_fusion.7), channel_id=1, source_target_pairs={{0,24},{1,25},{2,26},{3,27},{4,28},{5,29},{6,30},{7,31},{8,16},{9,... | collective-permute-start | bytes 49160 | tf_op jit(solution)/shard_map/ppermute | solution.py:24
  159.7 5.5 %collective-permute-start.53 = (f32[2,2176]{1,0:T(2,128)S(1)}, f32[2,2176]{1,0:T(2,128)S(1)}, u32[]{:S(2)}, u32[]{:S(2)}) collective-permute-start(f32[2,2176]{1,0:T(2,128)S(1)} %add_add_fusion.5), channel_id=1, source_target_pairs={{0,24},{1,25},{2,26},{3,27},{4,28},{5,29},{6,30},{7,31},{8,16},{9,... | collective-permute-start | bytes 52232 | tf_op jit(solution)/shard_map/ppermute | solution.py:24
  177.9 5.4 %collective-permute-start.60 = (f32[2,512]{1,0:T(2,128)S(1)}, f32[2,512]{1,0:T(2,128)S(1)}, u32[]{:S(2)}, u32[]{:S(2)}) collective-permute-start(f32[2,512]{1,0:T(2,128)S(1)} %add_add_fusion.11), channel_id=1, source_target_pairs={{0,24},{1,25},{2,26},{3,27},{4,28},{5,29},{6,30},{7,31},{8,16},{9,... | collective-permute-start | bytes 12296 | tf_op jit(solution)/shard_map/ppermute | solution.py:24
  195.6 7.2 %collective-permute-start.62 = (bf16[16,13,64,128]{3,2,1,0:T(8,128)(2,1)}, bf16[16,13,64,128]{3,2,1,0:T(8,128)(2,1)}, u32[]{:S(2)}, u32[]{:S(2)}) collective-permute-start(bf16[16,13,64,128]{3,2,1,0:T(8,128)(2,1)} %get-tuple-element.121), channel_id=1, source_target_pairs={{0,1},{1,0},{2,3},{3,2},{4,5},{5,4},{6,7},{7,6},{8,9},{9,8},{10,11... | collective-permute-start | bytes 10223624 | tf_op jit(solution)/shard_map/ppermute | solution.py:24
  205.9 22.3 %collective-permute-start.66 = (bf16[8,7,64,128]{3,2,1,0:T(8,128)(2,1)S(1)}, bf16[8,7,64,128]{3,2,1,0:T(8,128)(2,1)S(1)}, u32[]{:S(2)}, u32[]{:S(2)}) collective-permute-start(bf16[8,7,64,128]{3,2,1,0:T(8,128)(2,1)S(1)} %get-tuple-element.126), channel_id=1, source_target_pairs={{0,4},{1,5},{2,6},{3,7},{4,0},{5,1},{6,2},{7,3},{8,12},{9,13},{10,... | collective-permute-start | bytes 2752520 | tf_op jit(solution)/shard_map/ppermute | solution.py:24
  207.5 19.2 %collective-permute-start.67 = (bf16[8,6,64,128]{3,2,1,0:T(8,128)(2,1)S(1)}, bf16[8,6,64,128]{3,2,1,0:T(8,128)(2,1)S(1)}, u32[]{:S(2)}, u32[]{:S(2)}) collective-permute-start(bf16[8,6,64,128]{3,2,1,0:T(8,128)(2,1)S(1)} %get-tuple-element.127), channel_id=1, source_target_pairs={{0,2},{1,3},{2,0},{3,1},{4,6},{5,7},{6,4},{7,5},{8,10},{9,11},{10,... | collective-permute-start | bytes 2359304 | tf_op jit(solution)/shard_map/ppermute | solution.py:24
  209.5 5.4 %collective-permute-start.70 = (f32[2,512]{1,0:T(2,128)S(1)}, f32[2,512]{1,0:T(2,128)S(1)}, u32[]{:S(2)}, u32[]{:S(2)}) collective-permute-start(f32[2,512]{1,0:T(2,128)S(1)} %add_add_fusion.9), channel_id=1, source_target_pairs={{0,24},{1,25},{2,26},{3,27},{4,28},{5,29},{6,30},{7,31},{8,16},{9,... | collective-permute-start | bytes 12296 | tf_op jit(solution)/shard_map/ppermute | solution.py:24
  234.6 17.5 %collective-permute-start.71 = (bf16[16,256,128]{2,1,0:T(8,128)(2,1)}, bf16[16,256,128]{2,1,0:T(8,128)(2,1)S(1)}, u32[]{:S(2)}, u32[]{:S(2)}) collective-permute-start(bf16[16,256,128]{2,1,0:T(8,128)(2,1)} %get-tuple-element.133), channel_id=1, source_target_pairs={{0,1},{1,0},{2,3},{3,2},{4,5},{5,4},{6,7},{7,6},{8,9},{9,8},{10,11... | collective-permute-start | bytes 3145736 | tf_op jit(solution)/shard_map/ppermute | solution.py:24
  234.7 16.1 %collective-permute-start.75 = (bf16[4,7,64,128]{3,2,1,0:T(8,128)(2,1)}, bf16[4,7,64,128]{3,2,1,0:T(8,128)(2,1)S(1)}, u32[]{:S(2)}, u32[]{:S(2)}) collective-permute-start(bf16[4,7,64,128]{3,2,1,0:T(8,128)(2,1)} %get-tuple-element.130), channel_id=1, source_target_pairs={{0,2},{1,3},{2,0},{3,1},{4,6},{5,7},{6,4},{7,5},{8,10},{9,11},{10,... | collective-permute-start | bytes 1376264 | tf_op jit(solution)/shard_map/ppermute | solution.py:24
  236.7 13.0 %collective-permute-start.76 = (bf16[4,6,64,128]{3,2,1,0:T(8,128)(2,1)}, bf16[4,6,64,128]{3,2,1,0:T(8,128)(2,1)}, u32[]{:S(2)}, u32[]{:S(2)}) collective-permute-start(bf16[4,6,64,128]{3,2,1,0:T(8,128)(2,1)} %get-tuple-element.131), channel_id=1, source_target_pairs={{0,4},{1,5},{2,6},{3,7},{4,0},{5,1},{6,2},{7,3},{8,12},{9,13},{10,... | collective-permute-start | bytes 1179656 | tf_op jit(solution)/shard_map/ppermute | solution.py:24
  252.0 7.3 %collective-permute-start.77 = (bf16[13,64,128]{2,1,0:T(8,128)(2,1)S(1)}, bf16[13,64,128]{2,1,0:T(8,128)(2,1)S(1)}, u32[]{:S(2)}, u32[]{:S(2)}) collective-permute-start(bf16[13,64,128]{2,1,0:T(8,128)(2,1)S(1)} %get-tuple-element.142), channel_id=1, source_target_pairs={{0,8},{1,9},{2,10},{3,11},{4,12},{5,13},{6,14},{7,15},{8,0},{9,1},... | collective-permute-start | bytes 638984 | tf_op jit(solution)/shard_map/ppermute | solution.py:24
  252.4 22.5 %collective-permute-start.72 = (bf16[4,256,128]{2,1,0:T(8,128)(2,1)S(1)}, bf16[4,256,128]{2,1,0:T(8,128)(2,1)S(1)}, u32[]{:S(2)}, u32[]{:S(2)}) collective-permute-start(bf16[4,256,128]{2,1,0:T(8,128)(2,1)S(1)} %get-tuple-element.136), channel_id=1, source_target_pairs={{0,2},{1,3},{2,0},{3,1},{4,6},{5,7},{6,4},{7,5},{8,10},{9,11},{10,... | collective-permute-start | bytes 786440 | tf_op jit(solution)/shard_map/ppermute | solution.py:24
  252.9 22.0 %collective-permute-start.73 = (bf16[4,256,128]{2,1,0:T(8,128)(2,1)S(1)}, bf16[4,256,128]{2,1,0:T(8,128)(2,1)S(1)}, u32[]{:S(2)}, u32[]{:S(2)}) collective-permute-start(bf16[4,256,128]{2,1,0:T(8,128)(2,1)S(1)} %get-tuple-element.137), channel_id=1, source_target_pairs={{0,4},{1,5},{2,6},{3,7},{4,0},{5,1},{6,2},{7,3},{8,12},{9,13},{10,... | collective-permute-start | bytes 786440 | tf_op jit(solution)/shard_map/ppermute | solution.py:24
  254.6 20.3 %collective-permute-start.74 = (bf16[4,256,128]{2,1,0:T(8,128)(2,1)S(1)}, bf16[4,256,128]{2,1,0:T(8,128)(2,1)S(1)}, u32[]{:S(2)}, u32[]{:S(2)}) collective-permute-start(bf16[4,256,128]{2,1,0:T(8,128)(2,1)S(1)} %get-tuple-element.138), channel_id=1, source_target_pairs={{0,6},{1,7},{2,4},{3,5},{4,2},{5,3},{6,0},{7,1},{8,14},{9,15},{10,... | collective-permute-start | bytes 786440 | tf_op jit(solution)/shard_map/ppermute | solution.py:24
  257.2 17.8 %collective-permute-start.78 = (bf16[13,64,128]{2,1,0:T(8,128)(2,1)S(1)}, bf16[13,64,128]{2,1,0:T(8,128)(2,1)S(1)}, u32[]{:S(2)}, u32[]{:S(2)}) collective-permute-start(bf16[13,64,128]{2,1,0:T(8,128)(2,1)S(1)} %get-tuple-element.143), channel_id=1, source_target_pairs={{0,16},{1,17},{2,18},{3,19},{4,20},{5,21},{6,22},{7,23},{8,24},{9,... | collective-permute-start | bytes 638984 | tf_op jit(solution)/shard_map/ppermute | solution.py:24
  259.4 15.6 %collective-permute-start.79 = (bf16[13,64,128]{2,1,0:T(8,128)(2,1)S(1)}, bf16[13,64,128]{2,1,0:T(8,128)(2,1)S(1)}, u32[]{:S(2)}, u32[]{:S(2)}) collective-permute-start(bf16[13,64,128]{2,1,0:T(8,128)(2,1)S(1)} %get-tuple-element.144), channel_id=1, source_target_pairs={{0,24},{1,25},{2,26},{3,27},{4,28},{5,29},{6,30},{7,31},{8,16},{9,... | collective-permute-start | bytes 638984 | tf_op jit(solution)/shard_map/ppermute | solution.py:24
  275.4 12.2 %collective-permute-start.80 = (bf16[256,128]{1,0:T(8,128)(2,1)S(1)}, bf16[256,128]{1,0:T(8,128)(2,1)S(1)}, u32[]{:S(2)}, u32[]{:S(2)}) collective-permute-start(bf16[256,128]{1,0:T(8,128)(2,1)S(1)} %get-tuple-element.149), channel_id=1, source_target_pairs={{0,8},{1,9},{2,10},{3,11},{4,12},{5,13},{6,14},{7,15},{8,0},{9,1},... | collective-permute-start | bytes 196616 | tf_op jit(solution)/shard_map/ppermute | solution.py:24
  279.3 8.3 %collective-permute-start.81 = (bf16[256,128]{1,0:T(8,128)(2,1)S(1)}, bf16[256,128]{1,0:T(8,128)(2,1)S(1)}, u32[]{:S(2)}, u32[]{:S(2)}) collective-permute-start(bf16[256,128]{1,0:T(8,128)(2,1)S(1)} %get-tuple-element.150), channel_id=1, source_target_pairs={{0,16},{1,17},{2,18},{3,19},{4,20},{5,21},{6,22},{7,23},{8,24},{9,... | collective-permute-start | bytes 196616 | tf_op jit(solution)/shard_map/ppermute | solution.py:24
  279.4 8.3 %collective-permute-start.82 = (bf16[256,128]{1,0:T(8,128)(2,1)S(1)}, bf16[256,128]{1,0:T(8,128)(2,1)S(1)}, u32[]{:S(2)}, u32[]{:S(2)}) collective-permute-start(bf16[256,128]{1,0:T(8,128)(2,1)S(1)} %get-tuple-element.151), channel_id=1, source_target_pairs={{0,24},{1,25},{2,26},{3,27},{4,28},{5,29},{6,30},{7,31},{8,16},{9,... | collective-permute-start | bytes 196616 | tf_op jit(solution)/shard_map/ppermute | solution.py:24
  (79 other events, 692.5 us)
Sparse Core Ops, SparseCore 0:
  12.7 82.0 all-gather.5
  195.9 56.4 all-gather.3

commit v4 on v3

--- a/solution.py
+++ b/solution.py
@@ -50,17 +50,23 @@
 
 
 def gather_low(parts, halves, n, after=None):
-    stack, masks = following(jnp.stack(parts), after), high_masks(n)
+    stack = following(jnp.stack(parts), after)
     near, side = swap(stack, 2, n), swap(stack, 4, n)
+    if halves:
+        return gather_cross(stack, near, side, n), side
+    masks = high_masks(n)
+    pairs = list(zip((stack, side, near, swap(stack, 6, n)), ([m ^ low for m in masks] for low in (0, 4, 2, 6))))
+    return pairs + [(swap(array, 1, n), [m ^ 1 for m in row]) for array, row in pairs], side
+
+
+def gather_cross(stack, near, side, n, after=None):
+    masks = high_masks(n)
     half = len(masks) // 2
+    first, second = following((near[:half], side[half:]), after)
     pairs = [(stack, masks), (side, [m ^ 4 for m in masks]), (near, [m ^ 2 for m in masks])]
-    if halves:
-        pairs.append((swap(near[:half], 4, n), [m ^ 6 for m in masks[:half]]))
-        pairs.append((swap(side[half:], 2, n), [m ^ 6 for m in masks[half:]]))
-    else:
-        pairs.append((swap(stack, 6, n), [m ^ 6 for m in masks]))
-    pairs += [(swap(array, 1, n), [m ^ 1 for m in row]) for array, row in pairs]
-    return pairs, side
+    pairs.append((swap(first, 4, n), [m ^ 6 for m in masks[:half]]))
+    pairs.append((swap(second, 2, n), [m ^ 6 for m in masks[half:]]))
+    return pairs + [(swap(array, 1, n), [m ^ 1 for m in row]) for array, row in pairs]
 
 
 def slot_masks(n):
@@ -319,24 +325,25 @@
         out_sums[1:2, block] = col_sum(value * value)
 
 
-def head_kernel(count, pixels, group, classes, c, me, hidden, sums, norms, row_weights, target, shards, *refs):
-    sources, (upper, out_sums, packed, loss, features, weights, arrived) = refs[:c], refs[c:]
+def head_kernel(count, pixels, group, classes, c, plan, me, hidden, sums, norms, row_weights, target, *refs):
+    shards, refs = refs[: len(plan)], refs[len(plan) :]
+    sources, (upper, out_sums, packed, loss, features, weights, held, arrived) = refs[:c], refs[c:]
     chan, rows = me[1], hidden.shape[0]
     width = features.shape[2]
     twice = 2 * group
     copies = fetch(sources, [features.at[k] for k in range(c)], arrived)
-    devices, tall = shards.shape[0], weights.shape[0] * c // shards.shape[0]
+    number = me[0] * c + chan
     halves = weights.shape[1] // (c * LANES)
-    copies += fetch(
-        [shards.at[a, pl.ds(k * tall, tall), :] for a in range(devices) for k in range(halves)],
-        [
-            weights.at[pl.ds(a // c * tall, tall), pl.ds((a % c * halves + k) * LANES, LANES)]
-            for a in range(devices)
-            for k in range(halves)
-        ],
-        arrived,
-        c,
-    )
+    tall = shards[0].shape[1] // halves
+    starts, ends = [], []
+    for part, masks in zip(shards, plan):
+        for a, mask in enumerate(masks):
+            other = number ^ mask
+            i, j = lax.div(other, c), lax.rem(other, c)
+            for k in range(halves):
+                starts.append(part.at[a, pl.ds(k * tall, tall), :])
+                ends.append(weights.at[at(i, tall), at(j * halves + k, LANES)])
+    copies += fetch(starts, ends, arrived, c)
     blocks = [pl.ds(pl.multiple_of((chan ^ k) * width, width), width) for k in range(c)]
     for k, cols in enumerate(blocks):
         mean, scale = statistics(sums, count, cols)
@@ -354,11 +361,11 @@
 
         pool = lax.fori_loop(0, rows // CHUNK, forward, jnp.zeros((twice, width), F32))
         pool = (pool + pltpu.roll(pool, group, 0)) / pixels
-        packed[:, cols] = pool.astype(BF16)
+        held[:, cols] = pool.astype(BF16)
     depth, space = weights.shape
     for copy in copies[c:]:
         copy.wait()
-    pooled = packed[:, 0:depth]
+    pooled = held[...]
     logits = dot(pooled, weights[...])
     column = lax.broadcasted_iota(jnp.int32, logits.shape, 1)
     valid = lax.rem(column, space // c) < classes
@@ -370,8 +377,11 @@
     weight, share = row_weights[:, 0:1], row_weights[:, 1:2]
     loss[...] = 0.5 * jnp.sum(weight * (spread - picked), axis=0, keepdims=True)
     down = share * (jnp.where(valid, jnp.exp(logits - spread), 0.0) - wanted)
-    packed[:, depth:] = down.astype(BF16)
     low_down = down.astype(BF16)
+    row = lax.broadcasted_iota(jnp.int32, (twice, 1), 0)
+    length = packed.shape[1]
+    full = jnp.concatenate([pooled.astype(F32), low_down.astype(F32)], axis=1)
+    packed[...] = jnp.where(row < group, full[:, :length], full[:, length:]).astype(BF16)
     for k, cols in enumerate(blocks):
         mean, scale = statistics(sums, count, cols)
         back = dot(low_down, weights[cols, :], ((1,), (1,))) / pixels
@@ -514,8 +524,26 @@
     )
 
 
+def grad_head_kernel(c, tall, space, group, me, *refs):
+    *parts, out = refs
+    length = parts[0].shape[2]
+    wide = 2 * length - c * space
+    start = me[0] * tall
+    late = start >= length
+    row = lax.broadcasted_iota(jnp.int32, (2 * group, 1), 0)
+    left, right = [], []
+    for part in parts:
+        for a in range(part.shape[0]):
+            one = part[a, :, at(jnp.where(late, start - length, start) // tall, tall)].astype(F32)
+            left.append(jnp.where(late, one, pltpu.roll(one, group, 0)))
+            two = part[a, :, at((wide - length) // space + me[1], space)].astype(F32)
+            right.append(jnp.where(row < group, 0.0, two))
+    left, right = jnp.concatenate(left).astype(BF16), jnp.concatenate(right).astype(BF16)
+    out[...] = dot(left, right, ((0,), (0,)))
+
+
 def add_low(one, other):
-    return (one.astype(F32) + other.astype(F32)).astype(BF16)
+    return one + other
 
 
 def add_quarters_kernel(arrived, own, *outs):
@@ -622,11 +650,11 @@
         low_mid = jnp.concatenate([low_mid, conv_out.astype(BF16).reshape(4, fan_in, fan_out)])
     away, other = swap(away, 2, n), swap(other, 2, n)
     high_in = gather_high(low_in, n)
-    low_head = lax.all_gather(low_head, AXES)
     pieces = [own, swap(mate, 1, n), other, swap(away, 1, n)]
     low_in, side_in = gather_low(high_in, False, n, (away, other))
     high_mid = gather_high(following(low_mid, high_in[1]), n)
-    low_mid, _ = gather_low(high_mid, True, n, side_in)
+    low_mid, side_mid = gather_low(high_mid, True, n, side_in)
+    high_head = gather_high(following(low_head, side_mid), n)
 
     narrow = conv_in.shape[1]
     own = lax.dynamic_index_in_dim(labels.reshape(c, group), chan, 0, keepdims=False)
@@ -681,7 +709,10 @@
         me, hidden_one, sums_one, norms_one, whole_mid,
         flops=18 * rows * mid * mid, scratch=[padded, many],
     )
-    sums_two, *_ = total(sums_two, n)
+    stack_head = following(jnp.stack(high_head), [low_mid[3][0], low_mid[4][0]])
+    near_head, side_head = swap(stack_head, 2, n), swap(stack_head, 4, n)
+    sums_two, middle_two = total(sums_two, n)
+    hidden_two = following(hidden_two, (near_head, side_head))
 
     act_two, hidden_three, sums_three = call(
         functools.partial(third_kernel, count),
@@ -689,18 +720,18 @@
         me, hidden_two, sums_two, norms_two, whole_out,
         flops=2 * rows * mid * wide,
     )
-    sums_three, *_ = total(sums_three, n)
+    sums_three, middle_three = total(sums_three, n)
+    low_head = gather_cross(stack_head, near_head, side_head, n, middle_two)
 
     row_weights = jnp.stack([weight_row, weight_row / weight_sum], axis=1)
     upper_three, back_three, packed, _ = call(
-        functools.partial(head_kernel, count, pixels, group, classes, c),
-        [((rows, wide), F32), ((2, wide + LANES), F32), ((2 * group, wide + c * space), BF16), ((1, 1), F32)],
-        me, hidden_three, sums_three, norms_three, row_weights, target, low_head, *pieces,
-        flops=4 * 8 * wide * c * space, remain=1 + c,
-        scratch=feature_space + [((wide, c * space), jnp.bfloat16)],
+        functools.partial(head_kernel, count, pixels, group, classes, c, [masks for _, masks in low_head]),
+        [((rows, wide), F32), ((2, wide + LANES), F32), ((2 * group, (wide + c * space) // 2), BF16), ((1, 1), F32)],
+        me, hidden_three, sums_three, norms_three, row_weights, target, *[array for array, _ in low_head], *pieces,
+        flops=4 * 8 * wide * c * space, remain=len(low_head) + c,
+        scratch=feature_space + [((wide, c * space), jnp.bfloat16), ((2 * group, wide), jnp.bfloat16)],
         semaphores=[pltpu.SemaphoreType.DMA((c + n * (space // LANES),))],
     )
-    everything = lax.all_gather(packed, AXES, axis=0, tiled=True)
     back_three, *_ = total(back_three, n)
     loss_sum = back_three[0, wide]
 
@@ -761,7 +792,8 @@
     )
     arrived = [swap(send, order[1], n) for send, (_, _, order) in zip(sends, plan)]
     kept_in, *sends_in = scatter_start(*parts_in, n)
-    last_mid = scatter_last(split_third(arrived, keeps, plan, n), n)
+    sums_mid = split_third(arrived, keeps, plan, n)
+    last_mid = scatter_last(sums_mid, n)
     arrived_in = [swap(send, mask, n) for send, mask in zip(sends_in, (2, 4, 6))]
     arrived_in, last_mid = lax.optimization_barrier((arrived_in, last_mid))
     sums_in = scatter_next(kept_in, arrived_in, n)
@@ -773,10 +805,21 @@
     grad_out = grad_out.reshape(conv_out.shape)
     grad_in = added(scatter_last(sums_in, n))
 
-    everything = following(everything, sums_in[0])
-    pooled = lax.dynamic_slice_in_dim(everything, dp * tall, tall, axis=1)
-    upper_logits = lax.dynamic_slice_in_dim(everything, wide + chan * space, space, axis=1)
-    grad_head = 0.5 * dot(pooled, upper_logits, ((0,), (0,)))[:, :classes]
+    pairs, _ = gather_low(gather_high(packed, n), False, n)
+    pairs = [(array, masks) for array, (_, masks) in zip(following([array for array, _ in pairs], sums_in[0]), pairs)]
+    if aligned:
+        (grad_head,) = call(
+            functools.partial(grad_head_kernel, c, tall, space, group), [((tall, space), F32)],
+            me, *[array for array, _ in pairs],
+        )
+    else:
+        everything = jnp.concatenate([array for array, _ in pairs])
+        everything = jnp.concatenate([everything[:, :group], everything[:, group:]], axis=2)
+        everything = everything.reshape(-1, wide + c * space)
+        pooled = lax.dynamic_slice_in_dim(everything, dp * tall, tall, axis=1)
+        upper_logits = lax.dynamic_slice_in_dim(everything, wide + chan * space, space, axis=1)
+        grad_head = dot(pooled, upper_logits, ((0,), (0,)))
+    grad_head = grad_head[:, :classes]
 
     def mine(sums, width):
         return lax.dynamic_slice_in_dim(sums[:2], chan * width, width, axis=1)[::-1]

time: 296 us -> 281 us (0.949)
  waiting for transfers between devices: 112 us -> 94.4 us
  between operations: 15.6 us -> 2.35 us
  starting transfers between devices: 100 us -> 112 us
  local copies, waits for them, and re-layouts: 10.1 us -> 16.7 us
  Pallas kernels: 47.7 us -> 42 us
  other arithmetic: 7.99 us -> 12.6 us
    ppermute x83 -> x105, waiting for transfers between devices: 112 us -> 94.4 us  [swap(): return lax.ppermute(array, AXES, [(d, d ^ mask) for d in range(n)])]
    ppermute x83 -> x105, starting transfers between devices: 100 us -> 112 us  [swap(): return lax.ppermute(array, AXES, [(d, d ^ mask) for d in range(n)])]
    pallas_call x16 -> x17, Pallas kernels: 47.7 us -> 42 us  [call(): pl.pallas_call(kernel, out_shape=shapes, in_specs=specs, out_specs=[pl.Bl...]
    slice x2 -> x4, local copies, waits for them, and re-layouts: 0.06 us -> 3.39 us  [gather_cross(): first, second = following((near[:half], side[half:]), after)]
    unnamed x93 -> x109, local copies, waits for them, and re-layouts: 8.45 us -> 9.82 us
  transfers between devices with their start and end apart: 85 -> 105, of which waited for: 45 -> 50; matrix products, arithmetic and copies ran while one was open for 4% -> 7% of each run, Pallas kernels for 8% -> 5%
where the time goes in v4:
time: 281 us; the launch traced here: 280 us
  starting transfers between devices  112 us (40%)
  waiting for transfers between devices  94.4 us (34%)
  Pallas kernels  42 us (15%)
  local copies, waits for them, and re-layouts  16.7 us (6%)
  other arithmetic  12.6 us (4%)
    ppermute x105, starting transfers between devices, swap(): return lax.ppermute(array, AXES, [(d, d ^ mask) for d in range(n)])  112 us
    ppermute x105, waiting for transfers between devices, swap(): return lax.ppermute(array, AXES, [(d, d ^ mask) for d in range(n)])  94.4 us
    pallas_call x17, Pallas kernels, call(): pl.pallas_call(kernel, out_shape=shapes, in_specs=specs, out_specs=[pl.Bl...  42 us
    unnamed x109, local copies, waits for them, and re-layouts  9.82 us
  transfers between devices with their start and end apart: 105, of which 50 were waited for; matrix products, arithmetic and copies ran while one was open for 7% of the time, Pallas kernels for 5%

profile of v4, /device:TPU:0, one launch (start us, length us, event | category | flops | bytes accessed | tf_op | source)
XLA Modules:
  0.0 280.4 jit_solution(5617467125608672827)
XLA Ops:
  0.8 3.0 %shard_map.345 = (bf16[400,512]{1,0:T(8,128)(2,1)S(1)}, bf16[400,512]{1,0:T(8,128)(2,1)S(1)}, bf16[400,512]{1,0:T(8,128)(2,1)S(1)}, bf16[400,512]{1,0:T(8,128)(2...) custom-call(s32[2]{0:T(128)S(1)} %pad_add_fusion.me, ...), custom_call_target="tpu_custom_call" | custom-call | bytes 4499464 | tf_op jit(solution)/shard_map/pallas_call | solution.py:124
  4.5 2.9 %collective-permute-start.4 = (bf16[400,512]{1,0:T(8,128)(2,1)S(1)}, bf16[400,512]{1,0:T(8,128)(2,1)S(1)}, u32[]{:S(2)}, u32[]{:S(2)}) collective-permute-start(bf16[400,512]{1,0:T(8,128)(2,1)S(1)} %get-tuple-element.106), channel_id=1, source_target_pairs={{0,2},{1,3},{2,0},{3,1},{4,6},{5,7},{6,4},{7,5},{8,10},{9,11},{10,... | collective-permute-start | bytes 1228808 | tf_op jit(solution)/shard_map/ppermute | solution.py:24
  7.5 2.1 collective-permute-start
  9.6 2.2 collective-permute-done
  11.8 2.0 collective-permute-start.21
  13.8 2.6 collective-permute-start.1
  16.4 3.3 %collective-permute-done.1 = bf16[256,128]{1,0:T(8,128)(2,1)S(1)} collective-permute-done((bf16[256,128]{1,0:T(8,128)(2,1)S(1)}, bf16[256,128]{1,0:T(8,128)(2,1)S(1)}, u32[]{:S(2)}, u32[]{:S(2)}) %collective-permute-start.1) | collective-permute-done | bytes 65568 | tf_op jit(solution)/shard_map/ppermute | solution.py:24
  19.7 2.9 %collective-permute-start.22 = (bf16[13,64,128]{2,1,0:T(8,128)(2,1)S(1)}, bf16[13,64,128]{2,1,0:T(8,128)(2,1)S(1)}, u32[]{:S(2)}, u32[]{:S(2)}) collective-permute-start(bf16[13,64,128]{2,1,0:T(8,128)(2,1)S(1)} %get-tuple-element.113), channel_id=1, source_target_pairs={{0,16},{1,17},{2,18},{3,19},{4,20},{5,21},{6,22},{7,23},{8,24},{9,... | collective-permute-start | bytes 638984 | tf_op jit(solution)/shard_map/ppermute | solution.py:24
  29.9 6.6 %collective-permute-done.22 = bf16[13,64,128]{2,1,0:T(8,128)(2,1)S(1)} collective-permute-done((bf16[13,64,128]{2,1,0:T(8,128)(2,1)S(1)}, bf16[13,64,128]{2,1,0:T(8,128)(2,1)S(1)}, u32[]{:S(2)}, u32[]{:S(2)}) %collective-permute-start.22) | collective-permute-done | bytes 213024 | tf_op jit(solution)/shard_map/ppermute | solution.py:24
  47.1 3.4 %shard_map.347 = (f32[400,512]{1,0:T(8,128)S(1)}, f32[15,512]{1,0:T(8,128)S(1)}) custom-call(s32[2]{0:T(128)S(1)} %pad_add_fusion.me, f32[13,512]{1,0:T(8,128)S(1)} %concatenate.10.carried, bf16[2048,512]{1,0:T(8,128)(2,1)S(1)} %shard_map.346.weights, bf16[400,512]{1,0:T(8,128)(2,1)} %copy-done.1, bf16[400,512]{1,0:T(8,128)(2,1)} %collective-permute-done.12.refs_1_.refs_11_, ...), custom_call_target="tpu_custom_call" | custom-call | flops 838860800 | bytes 4612104 | tf_op jit(solution)/shard_map/pallas_call | solution.py:124
  55.3 5.1 %collective-permute-done.15 = f32[15,512]{1,0:T(8,128)S(1)} collective-permute-done((f32[15,512]{1,0:T(8,128)S(1)}, f32[15,512]{1,0:T(8,128)S(1)}, u32[]{:S(2)}, u32[]{:S(2)}) %collective-permute-start.15) | collective-permute-done | bytes 30752 | tf_op jit(solution)/shard_map/ppermute | solution.py:24
  60.7 3.3 %collective-permute-start.18 = (f32[15,512]{1,0:T(8,128)S(1)}, f32[15,512]{1,0:T(8,128)S(1)}, u32[]{:S(2)}, u32[]{:S(2)}) collective-permute-start(f32[15,512]{1,0:T(8,128)S(1)} %add_add_fusion.3), channel_id=1, source_target_pairs={{0,8},{1,9},{2,10},{3,11},{4,12},{5,13},{6,14},{7,15},{8,0},{9,1},... | collective-permute-start | bytes 92168 | tf_op jit(solution)/shard_map/ppermute | solution.py:24
  70.7 5.7 %collective-permute-done.27.refs_4_ = bf16[2,13,64,128]{3,2,1,0:T(8,128)(2,1)} collective-permute-done((bf16[2,13,64,128]{3,2,1,0:T(8,128)(2,1)S(1)}, bf16[2,13,64,128]{3,2,1,0:T(8,128)(2,1)}, u32[]{:S(2)}, u32[]{:S(2)}) %collective-permute-start.27) | collective-permute-done | bytes 426016 | tf_op jit(solution)/shard_map/ppermute | solution.py:24
  81.3 1.9 collective-permute-start.34
  84.9 3.5 %shard_map.348 = (bf16[9,512,512]{2,1,0:T(8,128)(2,1)S(1)}, bf16[512,2048]{1,0:T(8,128)(2,1)S(1)}) custom-call(s32[2]{0:T(128)S(1)} %pad_add_fusion.me, bf16[4,13,64,128]{3,2,1,0:T(8,128)(2,1)S(1)} %pad_maximum_fusion.refs_0_, bf16[4,13,64,128]{3,2,1,0:T(8,128)(2,1)S(1)} %collective-permute-done.24.refs_1_, ...), custom_call_target="tpu_custom_call" | custom-call | bytes 13631496 | tf_op jit(solution)/shard_map/pallas_call | solution.py:124
  88.4 2.8 shard_map.349
  100.0 2.6 collective-permute-start.43
  104.5 3.5 %collective-permute-done.44 = f32[2,512]{1,0:T(2,128)S(1)} collective-permute-done((f32[2,512]{1,0:T(2,128)S(1)}, f32[2,512]{1,0:T(2,128)S(1)}, u32[]{:S(2)}, u32[]{:S(2)}) %collective-permute-start.44) | collective-permute-done | bytes 4128 | tf_op jit(solution)/shard_map/ppermute | solution.py:24
  108.0 3.0 %collective-permute-done.36.refs_2_ = bf16[4,512,128]{2,1,0:T(8,128)(2,1)} collective-permute-done((bf16[4,512,128]{2,1,0:T(8,128)(2,1)}, bf16[4,512,128]{2,1,0:T(8,128)(2,1)}, u32[]{:S(2)}, u32[]{:S(2)}) %collective-permute-start.36) | collective-permute-done | bytes 524320 | tf_op jit(solution)/shard_map/ppermute | solution.py:24
  125.0 2.4 collective-permute-start.50
  130.4 2.6 collective-permute-done.51
  136.5 7.7 %shard_map.351 = (f32[400,2048]{1,0:T(8,128)S(1)}, f32[2,2176]{1,0:T(2,128)S(1)}, bf16[8,1536]{1,0:T(8,128)(2,1)}, f32[1,1]{1,0:T(1,128)}) custom-call(s32[2]{0:T(128)S(1)} %pad_add_fusion.me, f32[400,2048]{1,0:T(8,128)S(1)} %get-tuple-element.123.hidden, f32[2,2048]{1,0:T(2,128)S(1)} %add_add_fusion.6.sums, f32[2,2048]{1,0:T(2,128)S(1)} %bitcast.77, ...), custom_call_target="tpu_custom_call" | custom-call | flops 67108864 | bytes 12493900 | tf_op jit(solution)/shard_map/pallas_call | solution.py:124
  146.8 2.3 collective-permute-start.62
  151.5 2.3 collective-permute-start.64
  153.8 2.1 collective-permute-start.65
  156.2 3.1 %collective-permute-done.65 = f32[2,2176]{1,0:T(2,128)S(1)} collective-permute-done((f32[2,2176]{1,0:T(2,128)S(1)}, f32[2,2176]{1,0:T(2,128)S(1)}, u32[]{:S(2)}, u32[]{:S(2)}) %collective-permute-start.65) | collective-permute-done | bytes 17440 | tf_op jit(solution)/shard_map/ppermute | solution.py:24
  159.4 2.0 shard_map.352
  167.6 2.4 collective-permute-done.69
  170.1 2.7 collective-permute-start.71
  174.7 3.5 %collective-permute-done.72 = f32[2,512]{1,0:T(2,128)S(1)} collective-permute-done((f32[2,512]{1,0:T(2,128)S(1)}, f32[2,512]{1,0:T(2,128)S(1)}, u32[]{:S(2)}, u32[]{:S(2)}) %collective-permute-start.72) | collective-permute-done | bytes 4128 | tf_op jit(solution)/shard_map/ppermute | solution.py:24
  178.2 2.9 %shard_map.353 = (bf16[400,512]{1,0:T(8,128)(2,1)S(1)}, f32[400,512]{1,0:T(8,128)S(1)}, f32[2,512]{1,0:T(2,128)S(1)}) custom-call(s32[2]{0:T(128)S(1)} %pad_add_fusion.me, f32[400,512]{1,0:T(8,128)S(1)} %get-tuple-element.129.upper, f32[400,512]{1,0:T(8,128)S(1)} %copy-done.3, f32[2,512]{1,0:T(2,128)S(1)} %add_add_fusion.12.sums.sums_two, ...), custom_call_target="tpu_custom_call" | custom-call | flops 1887436800 | bytes 8456200 | tf_op jit(solution)/shard_map/pallas_call | solution.py:124
  182.4 5.7 %shard_map.354 = (bf16[16,13,64,128]{3,2,1,0:T(8,128)(2,1)S(1)}, bf16[16,13,64,128]{3,2,1,0:T(8,128)(2,1)S(1)}) custom-call(s32[2]{0:T(128)S(1)} %pad_add_fusion.me, bf16[400,512]{1,0:T(8,128)(2,1)S(1)} %copy-done.18, bf16[400,512]{1,0:T(8,128)(2,1)S(1)} %get-tuple-element.135.down, bf16[400,512]{1,0:T(8,128)(2,1)S(1)} %copy-done.16, ...), custom_call_target="tpu_custom_call" | custom-call | flops 1887436800 | bytes 9682952 | tf_op jit(solution)/shard_map/pallas_call | solution.py:124
  189.6 2.3 collective-permute-start.77
  197.8 2.3 collective-permute-start.81
  200.1 2.1 collective-permute-start.82
  202.3 3.2 %collective-permute-done.82 = f32[2,512]{1,0:T(2,128)S(1)} collective-permute-done((f32[2,512]{1,0:T(2,128)S(1)}, f32[2,512]{1,0:T(2,128)S(1)}, u32[]{:S(2)}, u32[]{:S(2)}) %collective-permute-start.82) | collective-permute-done | bytes 4128 | tf_op jit(solution)/shard_map/ppermute | solution.py:24
  205.5 9.4 %collective-permute-done.79.refs_1_ = bf16[8,6,64,128]{3,2,1,0:T(8,128)(2,1)S(1)} collective-permute-done((bf16[8,6,64,128]{3,2,1,0:T(8,128)(2,1)S(1)}, bf16[8,6,64,128]{3,2,1,0:T(8,128)(2,1)S(1)}, u32[]{:S(2)}, u32[]{:S(2)}) %collective-permute-start.79) | collective-permute-done | bytes 786464 | tf_op jit(solution)/shard_map/ppermute | solution.py:24
  214.9 2.6 collective-permute-done.78.refs_0_
  219.5 4.8 %shard_map.357 = (bf16[16,256,128]{2,1,0:T(8,128)(2,1)S(1)}, bf16[16,256,128]{2,1,0:T(8,128)(2,1)}) custom-call(s32[2]{0:T(128)S(1)} %pad_add_fusion.me, f32[400,512]{1,0:T(8,128)S(1)} %get-tuple-element.149.upper, f32[400,512]{1,0:T(8,128)S(1)} %copy-done.5, f32[15,512]{1,0:T(8,128)S(1)} %add_add_fusion.2.sums.sums_one, f32[2,512]{1,0:T(2,128)S(1)} %bitcast.84, ...), custom_call_target="tpu_custom_call" | custom-call | flops 838860800 | bytes 5412872 | tf_op jit(solution)/shard_map/pallas_call | solution.py:124
  224.6 2.3 collective-permute-start.96
  226.8 2.1 collective-permute-start.97
  230.1 2.5 collective-permute-done.97
  236.0 5.2 %collective-permute-done.88.refs_1_ = bf16[4,6,64,128]{3,2,1,0:T(8,128)(2,1)S(1)} collective-permute-done((bf16[4,6,64,128]{3,2,1,0:T(8,128)(2,1)}, bf16[4,6,64,128]{3,2,1,0:T(8,128)(2,1)S(1)}, u32[]{:S(2)}, u32[]{:S(2)}) %collective-permute-start.88) | collective-permute-done | bytes 393248 | tf_op jit(solution)/shard_map/ppermute | solution.py:24
  249.6 2.2 collective-permute-start.90
  251.8 2.1 collective-permute-start.91
  255.8 8.7 %collective-permute-done.90 = bf16[13,64,128]{2,1,0:T(8,128)(2,1)S(1)} collective-permute-done((bf16[13,64,128]{2,1,0:T(8,128)(2,1)S(1)}, bf16[13,64,128]{2,1,0:T(8,128)(2,1)S(1)}, u32[]{:S(2)}, u32[]{:S(2)}) %collective-permute-start.90) | collective-permute-done | bytes 213024 | tf_op jit(solution)/shard_map/ppermute | solution.py:24
  266.7 3.7 %collective-permute-start.92 = (bf16[256,128]{1,0:T(8,128)(2,1)S(1)}, bf16[256,128]{1,0:T(8,128)(2,1)S(1)}, u32[]{:S(2)}, u32[]{:S(2)}) collective-permute-start(bf16[256,128]{1,0:T(8,128)(2,1)S(1)} %get-tuple-element.166), channel_id=1, source_target_pairs={{0,8},{1,9},{2,10},{3,11},{4,12},{5,13},{6,14},{7,15},{8,0},{9,1},... | collective-permute-start | bytes 196616 | tf_op jit(solution)/shard_map/ppermute | solution.py:24
  270.7 2.1 collective-permute-start.94
  (357 shorter events, 116.3 us)
Async XLA Ops:
  4.5 20.5 %collective-permute-start.4 = (bf16[400,512]{1,0:T(8,128)(2,1)S(1)}, bf16[400,512]{1,0:T(8,128)(2,1)S(1)}, u32[]{:S(2)}, u32[]{:S(2)}) collective-permute-start(bf16[400,512]{1,0:T(8,128)(2,1)S(1)} %get-tuple-element.106), channel_id=1, source_target_pairs={{0,2},{1,3},{2,0},{3,1},{4,6},{5,7},{6,4},{7,5},{8,10},{9,11},{10,... | collective-permute-start | bytes 1228808 | tf_op jit(solution)/shard_map/ppermute | solution.py:24
  7.5 18.2 %collective-permute-start.3 = (bf16[400,512]{1,0:T(8,128)(2,1)S(1)}, bf16[400,512]{1,0:T(8,128)(2,1)S(1)}, u32[]{:S(2)}, u32[]{:S(2)}) collective-permute-start(bf16[400,512]{1,0:T(8,128)(2,1)S(1)} %get-tuple-element.105), channel_id=1, source_target_pairs={{0,2},{1,3},{2,0},{3,1},{4,6},{5,7},{6,4},{7,5},{8,10},{9,11},{10,... | collective-permute-start | bytes 1228808 | tf_op jit(solution)/shard_map/ppermute | solution.py:24
  11.8 17.2 %collective-permute-start.21 = (bf16[13,64,128]{2,1,0:T(8,128)(2,1)S(1)}, bf16[13,64,128]{2,1,0:T(8,128)(2,1)S(1)}, u32[]{:S(2)}, u32[]{:S(2)}) collective-permute-start(bf16[13,64,128]{2,1,0:T(8,128)(2,1)S(1)} %get-tuple-element.113), channel_id=1, source_target_pairs={{0,8},{1,9},{2,10},{3,11},{4,12},{5,13},{6,14},{7,15},{8,0},{9,1},... | collective-permute-start | bytes 638984 | tf_op jit(solution)/shard_map/ppermute | solution.py:24
  16.4 7.0 %collective-permute-start.2 = (bf16[256,128]{1,0:T(8,128)(2,1)S(1)}, bf16[256,128]{1,0:T(8,128)(2,1)S(1)}, u32[]{:S(2)}, u32[]{:S(2)}) collective-permute-start(bf16[256,128]{1,0:T(8,128)(2,1)S(1)} %get-tuple-element.104), channel_id=1, source_target_pairs={{0,24},{1,25},{2,26},{3,27},{4,28},{5,29},{6,30},{7,31},{8,16},{9,... | collective-permute-start | bytes 196616 | tf_op jit(solution)/shard_map/ppermute | solution.py:24
  19.7 16.8 %collective-permute-start.22 = (bf16[13,64,128]{2,1,0:T(8,128)(2,1)S(1)}, bf16[13,64,128]{2,1,0:T(8,128)(2,1)S(1)}, u32[]{:S(2)}, u32[]{:S(2)}) collective-permute-start(bf16[13,64,128]{2,1,0:T(8,128)(2,1)S(1)} %get-tuple-element.113), channel_id=1, source_target_pairs={{0,16},{1,17},{2,18},{3,19},{4,20},{5,21},{6,22},{7,23},{8,24},{9,... | collective-permute-start | bytes 638984 | tf_op jit(solution)/shard_map/ppermute | solution.py:24
  23.4 13.6 %collective-permute-start.23 = (bf16[13,64,128]{2,1,0:T(8,128)(2,1)S(1)}, bf16[13,64,128]{2,1,0:T(8,128)(2,1)S(1)}, u32[]{:S(2)}, u32[]{:S(2)}) collective-permute-start(bf16[13,64,128]{2,1,0:T(8,128)(2,1)S(1)} %get-tuple-element.113), channel_id=1, source_target_pairs={{0,24},{1,25},{2,26},{3,27},{4,28},{5,29},{6,30},{7,31},{8,16},{9,... | collective-permute-start | bytes 638984 | tf_op jit(solution)/shard_map/ppermute | solution.py:24
  25.7 10.8 %collective-permute-start.5 = (bf16[4,256,128]{2,1,0:T(8,128)(2,1)S(1)}, bf16[4,256,128]{2,1,0:T(8,128)(2,1)S(1)}, u32[]{:S(2)}, u32[]{:S(2)}) collective-permute-start(bf16[4,256,128]{2,1,0:T(8,128)(2,1)S(1)} %pad_maximum_fusion.2.refs_0_), channel_id=1, source_target_pairs={{0,4},{1,5},{2,6},{3,7},{4,0},{5,1},{6,2},{7,3},{8,12},{9,13},{10,... | collective-permute-start | bytes 786440 | tf_op jit(solution)/shard_map/ppermute | solution.py:24
  27.5 11.3 %collective-permute-start.6 = (bf16[4,256,128]{2,1,0:T(8,128)(2,1)S(1)}, bf16[4,256,128]{2,1,0:T(8,128)(2,1)S(1)}, u32[]{:S(2)}, u32[]{:S(2)}) collective-permute-start(bf16[4,256,128]{2,1,0:T(8,128)(2,1)S(1)} %pad_maximum_fusion.2.refs_0_), channel_id=1, source_target_pairs={{0,2},{1,3},{2,0},{3,1},{4,6},{5,7},{6,4},{7,5},{8,10},{9,11},{10,... | collective-permute-start | bytes 786440 | tf_op jit(solution)/shard_map/ppermute | solution.py:24
  29.0 11.3 %collective-permute-start.7 = (bf16[4,256,128]{2,1,0:T(8,128)(2,1)S(1)}, bf16[4,256,128]{2,1,0:T(8,128)(2,1)S(1)}, u32[]{:S(2)}, u32[]{:S(2)}) collective-permute-start(bf16[4,256,128]{2,1,0:T(8,128)(2,1)S(1)} %pad_maximum_fusion.2.refs_0_), channel_id=1, source_target_pairs={{0,6},{1,7},{2,4},{3,5},{4,2},{5,3},{6,0},{7,1},{8,14},{9,15},{10,... | collective-permute-start | bytes 786440 | tf_op jit(solution)/shard_map/ppermute | solution.py:24
  37.2 29.2 %collective-permute-start.24 = (bf16[4,13,64,128]{3,2,1,0:T(8,128)(2,1)S(1)}, bf16[4,13,64,128]{3,2,1,0:T(8,128)(2,1)S(1)}, u32[]{:S(2)}, u32[]{:S(2)}) collective-permute-start(bf16[4,13,64,128]{3,2,1,0:T(8,128)(2,1)S(1)} %pad_maximum_fusion.refs_0_), channel_id=1, source_target_pairs={{0,4},{1,5},{2,6},{3,7},{4,0},{5,1},{6,2},{7,3},{8,12},{9,13},{10,... | collective-permute-start | bytes 2555912 | tf_op jit(solution)/shard_map/ppermute | solution.py:24
  38.8 29.2 %collective-permute-start.25 = (bf16[4,13,64,128]{3,2,1,0:T(8,128)(2,1)S(1)}, bf16[4,13,64,128]{3,2,1,0:T(8,128)(2,1)S(1)}, u32[]{:S(2)}, u32[]{:S(2)}) collective-permute-start(bf16[4,13,64,128]{3,2,1,0:T(8,128)(2,1)S(1)} %pad_maximum_fusion.refs_0_), channel_id=1, source_target_pairs={{0,2},{1,3},{2,0},{3,1},{4,6},{5,7},{6,4},{7,5},{8,10},{9,11},{10,... | collective-permute-start | bytes 2555912 | tf_op jit(solution)/shard_map/ppermute | solution.py:24
  51.8 8.6 %collective-permute-start.15 = (f32[15,512]{1,0:T(8,128)S(1)}, f32[15,512]{1,0:T(8,128)S(1)}, u32[]{:S(2)}, u32[]{:S(2)}) collective-permute-start(f32[15,512]{1,0:T(8,128)S(1)} %add.212), channel_id=1, source_target_pairs={{0,2},{1,3},{2,0},{3,1},{4,6},{5,7},{6,4},{7,5},{8,10},{9,11},{10,... | collective-permute-start | bytes 92168 | tf_op jit(solution)/shard_map/ppermute | solution.py:24
  53.0 7.4 %collective-permute-start.16 = (f32[15,512]{1,0:T(8,128)S(1)}, f32[15,512]{1,0:T(8,128)S(1)}, u32[]{:S(2)}, u32[]{:S(2)}) collective-permute-start(f32[15,512]{1,0:T(8,128)S(1)} %add.212), channel_id=1, source_target_pairs={{0,4},{1,5},{2,6},{3,7},{4,0},{5,1},{6,2},{7,3},{8,12},{9,13},{10,... | collective-permute-start | bytes 92168 | tf_op jit(solution)/shard_map/ppermute | solution.py:24
  54.5 6.2 %collective-permute-start.17 = (f32[15,512]{1,0:T(8,128)S(1)}, f32[15,512]{1,0:T(8,128)S(1)}, u32[]{:S(2)}, u32[]{:S(2)}) collective-permute-start(f32[15,512]{1,0:T(8,128)S(1)} %add.212), channel_id=1, source_target_pairs={{0,6},{1,7},{2,4},{3,5},{4,2},{5,3},{6,0},{7,1},{8,14},{9,15},{10,... | collective-permute-start | bytes 92168 | tf_op jit(solution)/shard_map/ppermute | solution.py:24
  60.7 8.9 %collective-permute-start.18 = (f32[15,512]{1,0:T(8,128)S(1)}, f32[15,512]{1,0:T(8,128)S(1)}, u32[]{:S(2)}, u32[]{:S(2)}) collective-permute-start(f32[15,512]{1,0:T(8,128)S(1)} %add_add_fusion.3), channel_id=1, source_target_pairs={{0,8},{1,9},{2,10},{3,11},{4,12},{5,13},{6,14},{7,15},{8,0},{9,1},... | collective-permute-start | bytes 92168 | tf_op jit(solution)/shard_map/ppermute | solution.py:24
  66.4 9.9 %collective-permute-start.27 = (bf16[2,13,64,128]{3,2,1,0:T(8,128)(2,1)S(1)}, bf16[2,13,64,128]{3,2,1,0:T(8,128)(2,1)}, u32[]{:S(2)}, u32[]{:S(2)}) collective-permute-start(bf16[2,13,64,128]{3,2,1,0:T(8,128)(2,1)S(1)} %slice.55), channel_id=1, source_target_pairs={{0,2},{1,3},{2,0},{3,1},{4,6},{5,7},{6,4},{7,5},{8,10},{9,11},{10,... | collective-permute-start | bytes 1277960 | tf_op jit(solution)/shard_map/ppermute | solution.py:24
  68.0 9.7 %collective-permute-start.26 = (bf16[2,13,64,128]{3,2,1,0:T(8,128)(2,1)S(1)}, bf16[2,13,64,128]{3,2,1,0:T(8,128)(2,1)}, u32[]{:S(2)}, u32[]{:S(2)}) collective-permute-start(bf16[2,13,64,128]{3,2,1,0:T(8,128)(2,1)S(1)} %slice.54), channel_id=1, source_target_pairs={{0,4},{1,5},{2,6},{3,7},{4,0},{5,1},{6,2},{7,3},{8,12},{9,13},{10,... | collective-permute-start | bytes 1277960 | tf_op jit(solution)/shard_map/ppermute | solution.py:24
  69.6 10.8 %collective-permute-start.28 = (bf16[4,13,64,128]{3,2,1,0:T(8,128)(2,1)S(1)}, bf16[4,13,64,128]{3,2,1,0:T(8,128)(2,1)}, u32[]{:S(2)}, u32[]{:S(2)}) collective-permute-start(bf16[4,13,64,128]{3,2,1,0:T(8,128)(2,1)S(1)} %pad_maximum_fusion.refs_0_), channel_id=1, source_target_pairs={{0,1},{1,0},{2,3},{3,2},{4,5},{5,4},{6,7},{7,6},{8,9},{9,8},{10,11... | collective-permute-start | bytes 2555912 | tf_op jit(solution)/shard_map/ppermute | solution.py:24
  69.6 15.3 %collective-permute-start.29 = (bf16[4,13,64,128]{3,2,1,0:T(8,128)(2,1)S(1)}, bf16[4,13,64,128]{3,2,1,0:T(8,128)(2,1)}, u32[]{:S(2)}, u32[]{:S(2)}) collective-permute-start(bf16[4,13,64,128]{3,2,1,0:T(8,128)(2,1)S(1)} %collective-permute-done.24.refs_1_), channel_id=1, source_target_pairs={{0,1},{1,0},{2,3},{3,2},{4,5},{5,4},{6,7},{7,6},{8,9},{9,8},{10,11... | collective-permute-start | bytes 2555912 | tf_op jit(solution)/shard_map/ppermute | solution.py:24
  70.7 14.2 %collective-permute-start.30 = (bf16[4,13,64,128]{3,2,1,0:T(8,128)(2,1)S(1)}, bf16[4,13,64,128]{3,2,1,0:T(8,128)(2,1)}, u32[]{:S(2)}, u32[]{:S(2)}) collective-permute-start(bf16[4,13,64,128]{3,2,1,0:T(8,128)(2,1)S(1)} %collective-permute-done.25.refs_2_), channel_id=1, source_target_pairs={{0,1},{1,0},{2,3},{3,2},{4,5},{5,4},{6,7},{7,6},{8,9},{9,8},{10,11... | collective-permute-start | bytes 2555912 | tf_op jit(solution)/shard_map/ppermute | solution.py:24
  80.4 14.9 %collective-permute-start.33 = (bf16[512,128]{1,0:T(8,128)(2,1)S(1)}, bf16[512,128]{1,0:T(8,128)(2,1)S(1)}, u32[]{:S(2)}, u32[]{:S(2)}) collective-permute-start(bf16[512,128]{1,0:T(8,128)(2,1)S(1)} %get-tuple-element.118), channel_id=1, source_target_pairs={{0,8},{1,9},{2,10},{3,11},{4,12},{5,13},{6,14},{7,15},{8,0},{9,1},... | collective-permute-start | bytes 393224 | tf_op jit(solution)/shard_map/ppermute | solution.py:24
  81.3 15.4 %collective-permute-start.34 = (bf16[512,128]{1,0:T(8,128)(2,1)S(1)}, bf16[512,128]{1,0:T(8,128)(2,1)S(1)}, u32[]{:S(2)}, u32[]{:S(2)}) collective-permute-start(bf16[512,128]{1,0:T(8,128)(2,1)S(1)} %get-tuple-element.118), channel_id=1, source_target_pairs={{0,16},{1,17},{2,18},{3,19},{4,20},{5,21},{6,22},{7,23},{8,24},{9,... | collective-permute-start | bytes 393224 | tf_op jit(solution)/shard_map/ppermute | solution.py:24
  83.2 13.5 %collective-permute-start.35 = (bf16[512,128]{1,0:T(8,128)(2,1)S(1)}, bf16[512,128]{1,0:T(8,128)(2,1)S(1)}, u32[]{:S(2)}, u32[]{:S(2)}) collective-permute-start(bf16[512,128]{1,0:T(8,128)(2,1)S(1)} %get-tuple-element.118), channel_id=1, source_target_pairs={{0,24},{1,25},{2,26},{3,27},{4,28},{5,29},{6,30},{7,31},{8,16},{9,... | collective-permute-start | bytes 393224 | tf_op jit(solution)/shard_map/ppermute | solution.py:24
  93.1 6.6 %collective-permute-start.39 = (f32[2,512]{1,0:T(2,128)S(1)}, f32[2,512]{1,0:T(2,128)S(1)}, u32[]{:S(2)}, u32[]{:S(2)}) collective-permute-start(f32[2,512]{1,0:T(2,128)S(1)} %add.219), channel_id=1, source_target_pairs={{0,2},{1,3},{2,0},{3,1},{4,6},{5,7},{6,4},{7,5},{8,10},{9,11},{10,... | collective-permute-start | bytes 12296 | tf_op jit(solution)/shard_map/ppermute | solution.py:24
  97.5 13.5 %collective-permute-start.36 = (bf16[4,512,128]{2,1,0:T(8,128)(2,1)}, bf16[4,512,128]{2,1,0:T(8,128)(2,1)}, u32[]{:S(2)}, u32[]{:S(2)}) collective-permute-start(bf16[4,512,128]{2,1,0:T(8,128)(2,1)} %pad_maximum_fusion.1.refs_0_), channel_id=1, source_target_pairs={{0,2},{1,3},{2,0},{3,1},{4,6},{5,7},{6,4},{7,5},{8,10},{9,11},{10,... | collective-permute-start | bytes 1572872 | tf_op jit(solution)/shard_map/ppermute | solution.py:24
  98.2 13.2 %collective-permute-start.37 = (bf16[4,512,128]{2,1,0:T(8,128)(2,1)}, bf16[4,512,128]{2,1,0:T(8,128)(2,1)}, u32[]{:S(2)}, u32[]{:S(2)}) collective-permute-start(bf16[4,512,128]{2,1,0:T(8,128)(2,1)} %pad_maximum_fusion.1.refs_0_), channel_id=1, source_target_pairs={{0,4},{1,5},{2,6},{3,7},{4,0},{5,1},{6,2},{7,3},{8,12},{9,13},{10,... | collective-permute-start | bytes 1572872 | tf_op jit(solution)/shard_map/ppermute | solution.py:24
  114.3 10.3 %collective-permute-start.46 = (f32[2,2048]{1,0:T(2,128)S(1)}, f32[2,2048]{1,0:T(2,128)S(1)}, u32[]{:S(2)}, u32[]{:S(2)}) collective-permute-start(f32[2,2048]{1,0:T(2,128)S(1)} %add.226), channel_id=1, source_target_pairs={{0,2},{1,3},{2,0},{3,1},{4,6},{5,7},{6,4},{7,5},{8,10},{9,11},{10,... | collective-permute-start | bytes 49160 | tf_op jit(solution)/shard_map/ppermute | solution.py:24
  115.7 8.9 %collective-permute-start.47 = (f32[2,2048]{1,0:T(2,128)S(1)}, f32[2,2048]{1,0:T(2,128)S(1)}, u32[]{:S(2)}, u32[]{:S(2)}) collective-permute-start(f32[2,2048]{1,0:T(2,128)S(1)} %add.226), channel_id=1, source_target_pairs={{0,4},{1,5},{2,6},{3,7},{4,0},{5,1},{6,2},{7,3},{8,12},{9,13},{10,... | collective-permute-start | bytes 49160 | tf_op jit(solution)/shard_map/ppermute | solution.py:24
  117.3 7.4 %collective-permute-start.48 = (f32[2,2048]{1,0:T(2,128)S(1)}, f32[2,2048]{1,0:T(2,128)S(1)}, u32[]{:S(2)}, u32[]{:S(2)}) collective-permute-start(f32[2,2048]{1,0:T(2,128)S(1)} %add.226), channel_id=1, source_target_pairs={{0,6},{1,7},{2,4},{3,5},{4,2},{5,3},{6,0},{7,1},{8,14},{9,15},{10,... | collective-permute-start | bytes 49160 | tf_op jit(solution)/shard_map/ppermute | solution.py:24
  121.8 11.3 %collective-permute-start.52 = (bf16[2,512,128]{2,1,0:T(8,128)(2,1)}, bf16[2,512,128]{2,1,0:T(8,128)(2,1)}, u32[]{:S(2)}, u32[]{:S(2)}) collective-permute-start(bf16[2,512,128]{2,1,0:T(8,128)(2,1)} %slice.59), channel_id=1, source_target_pairs={{0,4},{1,5},{2,6},{3,7},{4,0},{5,1},{6,2},{7,3},{8,12},{9,13},{10,... | collective-permute-start | bytes 786440 | tf_op jit(solution)/shard_map/ppermute | solution.py:24
  123.3 10.3 %collective-permute-start.53 = (bf16[2,512,128]{2,1,0:T(8,128)(2,1)}, bf16[2,512,128]{2,1,0:T(8,128)(2,1)}, u32[]{:S(2)}, u32[]{:S(2)}) collective-permute-start(bf16[2,512,128]{2,1,0:T(8,128)(2,1)} %slice.60), channel_id=1, source_target_pairs={{0,2},{1,3},{2,0},{3,1},{4,6},{5,7},{6,4},{7,5},{8,10},{9,11},{10,... | collective-permute-start | bytes 786440 | tf_op jit(solution)/shard_map/ppermute | solution.py:24
  195.0 22.5 %collective-permute-start.78 = (bf16[8,7,64,128]{3,2,1,0:T(8,128)(2,1)S(1)}, bf16[8,7,64,128]{3,2,1,0:T(8,128)(2,1)S(1)}, u32[]{:S(2)}, u32[]{:S(2)}) collective-permute-start(bf16[8,7,64,128]{3,2,1,0:T(8,128)(2,1)S(1)} %get-tuple-element.143), channel_id=1, source_target_pairs={{0,4},{1,5},{2,6},{3,7},{4,0},{5,1},{6,2},{7,3},{8,12},{9,13},{10,... | collective-permute-start | bytes 2752520 | tf_op jit(solution)/shard_map/ppermute | solution.py:24
  196.4 18.5 %collective-permute-start.79 = (bf16[8,6,64,128]{3,2,1,0:T(8,128)(2,1)S(1)}, bf16[8,6,64,128]{3,2,1,0:T(8,128)(2,1)S(1)}, u32[]{:S(2)}, u32[]{:S(2)}) collective-permute-start(bf16[8,6,64,128]{3,2,1,0:T(8,128)(2,1)S(1)} %get-tuple-element.144), channel_id=1, source_target_pairs={{0,2},{1,3},{2,0},{3,1},{4,6},{5,7},{6,4},{7,5},{8,10},{9,11},{10,... | collective-permute-start | bytes 2359304 | tf_op jit(solution)/shard_map/ppermute | solution.py:24
  224.4 19.5 %collective-permute-start.83 = (bf16[16,256,128]{2,1,0:T(8,128)(2,1)}, bf16[16,256,128]{2,1,0:T(8,128)(2,1)S(1)}, u32[]{:S(2)}, u32[]{:S(2)}) collective-permute-start(bf16[16,256,128]{2,1,0:T(8,128)(2,1)} %get-tuple-element.150), channel_id=1, source_target_pairs={{0,1},{1,0},{2,3},{3,2},{4,5},{5,4},{6,7},{7,6},{8,9},{9,8},{10,11... | collective-permute-start | bytes 3145736 | tf_op jit(solution)/shard_map/ppermute | solution.py:24
  228.9 13.7 %collective-permute-start.87 = (bf16[4,7,64,128]{3,2,1,0:T(8,128)(2,1)}, bf16[4,7,64,128]{3,2,1,0:T(8,128)(2,1)S(1)}, u32[]{:S(2)}, u32[]{:S(2)}) collective-permute-start(bf16[4,7,64,128]{3,2,1,0:T(8,128)(2,1)} %copy-done.12), channel_id=1, source_target_pairs={{0,2},{1,3},{2,0},{3,1},{4,6},{5,7},{6,4},{7,5},{8,10},{9,11},{10,... | collective-permute-start | bytes 1376264 | tf_op jit(solution)/shard_map/ppermute | solution.py:24
  229.6 11.6 %collective-permute-start.88 = (bf16[4,6,64,128]{3,2,1,0:T(8,128)(2,1)}, bf16[4,6,64,128]{3,2,1,0:T(8,128)(2,1)S(1)}, u32[]{:S(2)}, u32[]{:S(2)}) collective-permute-start(bf16[4,6,64,128]{3,2,1,0:T(8,128)(2,1)} %copy-done.14), channel_id=1, source_target_pairs={{0,4},{1,5},{2,6},{3,7},{4,0},{5,1},{6,2},{7,3},{8,12},{9,13},{10,... | collective-permute-start | bytes 1179656 | tf_op jit(solution)/shard_map/ppermute | solution.py:24
  234.1 10.8 %collective-permute-start.98 = (bf16[4,8,1536]{2,1,0:T(8,128)(2,1)S(1)}, bf16[4,8,1536]{2,1,0:T(8,128)(2,1)}, u32[]{:S(2)}, u32[]{:S(2)}) collective-permute-start(bf16[4,8,1536]{2,1,0:T(8,128)(2,1)S(1)} %pad_maximum_fusion.3.refs_0_), channel_id=1, source_target_pairs={{0,4},{1,5},{2,6},{3,7},{4,0},{5,1},{6,2},{7,3},{8,12},{9,13},{10,... | collective-permute-start | bytes 294920 | tf_op jit(solution)/shard_map/ppermute | solution.py:24
  234.6 11.7 %collective-permute-start.99 = (bf16[4,8,1536]{2,1,0:T(8,128)(2,1)S(1)}, bf16[4,8,1536]{2,1,0:T(8,128)(2,1)}, u32[]{:S(2)}, u32[]{:S(2)}) collective-permute-start(bf16[4,8,1536]{2,1,0:T(8,128)(2,1)S(1)} %pad_maximum_fusion.3.refs_0_), channel_id=1, source_target_pairs={{0,2},{1,3},{2,0},{3,1},{4,6},{5,7},{6,4},{7,5},{8,10},{9,11},{10,... | collective-permute-start | bytes 294920 | tf_op jit(solution)/shard_map/ppermute | solution.py:24
  241.2 8.4 %collective-permute-start.100 = (bf16[4,8,1536]{2,1,0:T(8,128)(2,1)S(1)}, bf16[4,8,1536]{2,1,0:T(8,128)(2,1)S(1)}, u32[]{:S(2)}, u32[]{:S(2)}) collective-permute-start(bf16[4,8,1536]{2,1,0:T(8,128)(2,1)S(1)} %pad_maximum_fusion.3.refs_0_), channel_id=1, source_target_pairs={{0,6},{1,7},{2,4},{3,5},{4,2},{5,3},{6,0},{7,1},{8,14},{9,15},{10,... | collective-permute-start | bytes 294920 | tf_op jit(solution)/shard_map/ppermute | solution.py:24
  243.8 8.0 %collective-permute-start.89 = (bf16[13,64,128]{2,1,0:T(8,128)(2,1)S(1)}, bf16[13,64,128]{2,1,0:T(8,128)(2,1)S(1)}, u32[]{:S(2)}, u32[]{:S(2)}) collective-permute-start(bf16[13,64,128]{2,1,0:T(8,128)(2,1)S(1)} %get-tuple-element.159), channel_id=1, source_target_pairs={{0,8},{1,9},{2,10},{3,11},{4,12},{5,13},{6,14},{7,15},{8,0},{9,1},... | collective-permute-start | bytes 638984 | tf_op jit(solution)/shard_map/ppermute | solution.py:24
  244.1 20.9 %collective-permute-start.84 = (bf16[4,256,128]{2,1,0:T(8,128)(2,1)S(1)}, bf16[4,256,128]{2,1,0:T(8,128)(2,1)S(1)}, u32[]{:S(2)}, u32[]{:S(2)}) collective-permute-start(bf16[4,256,128]{2,1,0:T(8,128)(2,1)S(1)} %get-tuple-element.153), channel_id=1, source_target_pairs={{0,2},{1,3},{2,0},{3,1},{4,6},{5,7},{6,4},{7,5},{8,10},{9,11},{10,... | collective-permute-start | bytes 786440 | tf_op jit(solution)/shard_map/ppermute | solution.py:24
  244.9 20.2 %collective-permute-start.85 = (bf16[4,256,128]{2,1,0:T(8,128)(2,1)S(1)}, bf16[4,256,128]{2,1,0:T(8,128)(2,1)S(1)}, u32[]{:S(2)}, u32[]{:S(2)}) collective-permute-start(bf16[4,256,128]{2,1,0:T(8,128)(2,1)S(1)} %get-tuple-element.154), channel_id=1, source_target_pairs={{0,4},{1,5},{2,6},{3,7},{4,0},{5,1},{6,2},{7,3},{8,12},{9,13},{10,... | collective-permute-start | bytes 786440 | tf_op jit(solution)/shard_map/ppermute | solution.py:24
  246.4 19.2 %collective-permute-start.86 = (bf16[4,256,128]{2,1,0:T(8,128)(2,1)S(1)}, bf16[4,256,128]{2,1,0:T(8,128)(2,1)S(1)}, u32[]{:S(2)}, u32[]{:S(2)}) collective-permute-start(bf16[4,256,128]{2,1,0:T(8,128)(2,1)S(1)} %get-tuple-element.155), channel_id=1, source_target_pairs={{0,6},{1,7},{2,4},{3,5},{4,2},{5,3},{6,0},{7,1},{8,14},{9,15},{10,... | collective-permute-start | bytes 786440 | tf_op jit(solution)/shard_map/ppermute | solution.py:24
  249.6 14.9 %collective-permute-start.90 = (bf16[13,64,128]{2,1,0:T(8,128)(2,1)S(1)}, bf16[13,64,128]{2,1,0:T(8,128)(2,1)S(1)}, u32[]{:S(2)}, u32[]{:S(2)}) collective-permute-start(bf16[13,64,128]{2,1,0:T(8,128)(2,1)S(1)} %get-tuple-element.160), channel_id=1, source_target_pairs={{0,16},{1,17},{2,18},{3,19},{4,20},{5,21},{6,22},{7,23},{8,24},{9,... | collective-permute-start | bytes 638984 | tf_op jit(solution)/shard_map/ppermute | solution.py:24
  251.8 12.7 %collective-permute-start.91 = (bf16[13,64,128]{2,1,0:T(8,128)(2,1)S(1)}, bf16[13,64,128]{2,1,0:T(8,128)(2,1)S(1)}, u32[]{:S(2)}, u32[]{:S(2)}) collective-permute-start(bf16[13,64,128]{2,1,0:T(8,128)(2,1)S(1)} %get-tuple-element.161), channel_id=1, source_target_pairs={{0,24},{1,25},{2,26},{3,27},{4,28},{5,29},{6,30},{7,31},{8,16},{9,... | collective-permute-start | bytes 638984 | tf_op jit(solution)/shard_map/ppermute | solution.py:24
  266.7 12.0 %collective-permute-start.92 = (bf16[256,128]{1,0:T(8,128)(2,1)S(1)}, bf16[256,128]{1,0:T(8,128)(2,1)S(1)}, u32[]{:S(2)}, u32[]{:S(2)}) collective-permute-start(bf16[256,128]{1,0:T(8,128)(2,1)S(1)} %get-tuple-element.166), channel_id=1, source_target_pairs={{0,8},{1,9},{2,10},{3,11},{4,12},{5,13},{6,14},{7,15},{8,0},{9,1},... | collective-permute-start | bytes 196616 | tf_op jit(solution)/shard_map/ppermute | solution.py:24
  270.4 8.3 %collective-permute-start.93 = (bf16[256,128]{1,0:T(8,128)(2,1)S(1)}, bf16[256,128]{1,0:T(8,128)(2,1)S(1)}, u32[]{:S(2)}, u32[]{:S(2)}) collective-permute-start(bf16[256,128]{1,0:T(8,128)(2,1)S(1)} %get-tuple-element.167), channel_id=1, source_target_pairs={{0,16},{1,17},{2,18},{3,19},{4,20},{5,21},{6,22},{7,23},{8,24},{9,... | collective-permute-start | bytes 196616 | tf_op jit(solution)/shard_map/ppermute | solution.py:24
  270.7 8.0 %collective-permute-start.94 = (bf16[256,128]{1,0:T(8,128)(2,1)S(1)}, bf16[256,128]{1,0:T(8,128)(2,1)S(1)}, u32[]{:S(2)}, u32[]{:S(2)}) collective-permute-start(bf16[256,128]{1,0:T(8,128)(2,1)S(1)} %get-tuple-element.168), channel_id=1, source_target_pairs={{0,24},{1,25},{2,26},{3,27},{4,28},{5,29},{6,30},{7,31},{8,16},{9,... | collective-permute-start | bytes 196616 | tf_op jit(solution)/shard_map/ppermute | solution.py:24
  (107 other events, 864.1 us)

commit v5 on v4

--- a/solution.py
+++ b/solution.py
@@ -712,7 +712,7 @@
     stack_head = following(jnp.stack(high_head), [low_mid[3][0], low_mid[4][0]])
     near_head, side_head = swap(stack_head, 2, n), swap(stack_head, 4, n)
     sums_two, middle_two = total(sums_two, n)
-    hidden_two = following(hidden_two, (near_head, side_head))
+    hidden_two = following(hidden_two, near_head)
 
     act_two, hidden_three, sums_three = call(
         functools.partial(third_kernel, count),

time: 281 us -> 280 us (level)
  transfers between devices with their start and end apart: 105 -> 105, of which waited for: 50 -> 47; matrix products, arithmetic and copies ran while one was open for 7% -> 7% of each run, Pallas kernels for 5% -> 5%
where the time goes in v5:
time: 280 us; the launch traced here: 279 us
  starting transfers between devices  111 us (40%)
  waiting for transfers between devices  94.8 us (34%)
  Pallas kernels  42 us (15%)
  local copies, waits for them, and re-layouts  16.7 us (6%)
  other arithmetic  12.6 us (4%)
    ppermute x105, starting transfers between devices, swap(): return lax.ppermute(array, AXES, [(d, d ^ mask) for d in range(n)])  111 us
    ppermute x105, waiting for transfers between devices, swap(): return lax.ppermute(array, AXES, [(d, d ^ mask) for d in range(n)])  94.8 us
    pallas_call x17, Pallas kernels, call(): pl.pallas_call(kernel, out_shape=shapes, in_specs=specs, out_specs=[pl.Bl...  42 us
    unnamed x109, local copies, waits for them, and re-layouts  9.82 us
  transfers between devices with their start and end apart: 105, of which 47 were waited for; matrix products, arithmetic and copies ran while one was open for 7% of the time, Pallas kernels for 5%

profile of v5, /device:TPU:0, one launch (start us, length us, event | category | flops | bytes accessed | tf_op | source)
XLA Modules:
  0.0 279.3 jit_solution(8756182251632633434)
XLA Ops:
  0.8 3.0 %shard_map.345 = (bf16[400,512]{1,0:T(8,128)(2,1)S(1)}, bf16[400,512]{1,0:T(8,128)(2,1)S(1)}, bf16[400,512]{1,0:T(8,128)(2,1)S(1)}, bf16[400,512]{1,0:T(8,128)(2...) custom-call(s32[2]{0:T(128)S(1)} %pad_add_fusion.me, ...), custom_call_target="tpu_custom_call" | custom-call | bytes 4499464 | tf_op jit(solution)/shard_map/pallas_call | solution.py:124
  4.5 2.9 %collective-permute-start.4 = (bf16[400,512]{1,0:T(8,128)(2,1)S(1)}, bf16[400,512]{1,0:T(8,128)(2,1)S(1)}, u32[]{:S(2)}, u32[]{:S(2)}) collective-permute-start(bf16[400,512]{1,0:T(8,128)(2,1)S(1)} %get-tuple-element.106), channel_id=1, source_target_pairs={{0,2},{1,3},{2,0},{3,1},{4,6},{5,7},{6,4},{7,5},{8,10},{9,11},{10,... | collective-permute-start | bytes 1228808 | tf_op jit(solution)/shard_map/ppermute | solution.py:24
  7.5 2.1 collective-permute-start
  9.6 2.2 collective-permute-done
  11.8 2.0 collective-permute-start.21
  13.8 2.6 collective-permute-start.1
  16.4 3.3 %collective-permute-done.1 = bf16[256,128]{1,0:T(8,128)(2,1)S(1)} collective-permute-done((bf16[256,128]{1,0:T(8,128)(2,1)S(1)}, bf16[256,128]{1,0:T(8,128)(2,1)S(1)}, u32[]{:S(2)}, u32[]{:S(2)}) %collective-permute-start.1) | collective-permute-done | bytes 65568 | tf_op jit(solution)/shard_map/ppermute | solution.py:24
  19.7 2.9 %collective-permute-start.22 = (bf16[13,64,128]{2,1,0:T(8,128)(2,1)S(1)}, bf16[13,64,128]{2,1,0:T(8,128)(2,1)S(1)}, u32[]{:S(2)}, u32[]{:S(2)}) collective-permute-start(bf16[13,64,128]{2,1,0:T(8,128)(2,1)S(1)} %get-tuple-element.113), channel_id=1, source_target_pairs={{0,16},{1,17},{2,18},{3,19},{4,20},{5,21},{6,22},{7,23},{8,24},{9,... | collective-permute-start | bytes 638984 | tf_op jit(solution)/shard_map/ppermute | solution.py:24
  25.7 1.8 collective-permute-start.5
  29.9 6.6 %collective-permute-done.22 = bf16[13,64,128]{2,1,0:T(8,128)(2,1)S(1)} collective-permute-done((bf16[13,64,128]{2,1,0:T(8,128)(2,1)S(1)}, bf16[13,64,128]{2,1,0:T(8,128)(2,1)S(1)}, u32[]{:S(2)}, u32[]{:S(2)}) %collective-permute-start.22) | collective-permute-done | bytes 213024 | tf_op jit(solution)/shard_map/ppermute | solution.py:24
  47.1 3.4 %shard_map.347 = (f32[400,512]{1,0:T(8,128)S(1)}, f32[15,512]{1,0:T(8,128)S(1)}) custom-call(s32[2]{0:T(128)S(1)} %pad_add_fusion.me, f32[13,512]{1,0:T(8,128)S(1)} %concatenate.10.carried, bf16[2048,512]{1,0:T(8,128)(2,1)S(1)} %shard_map.346.weights, bf16[400,512]{1,0:T(8,128)(2,1)} %copy-done.1, bf16[400,512]{1,0:T(8,128)(2,1)} %collective-permute-done.12.refs_1_.refs_11_, ...), custom_call_target="tpu_custom_call" | custom-call | flops 838860800 | bytes 4612104 | tf_op jit(solution)/shard_map/pallas_call | solution.py:124
  55.3 5.1 %collective-permute-done.15 = f32[15,512]{1,0:T(8,128)S(1)} collective-permute-done((f32[15,512]{1,0:T(8,128)S(1)}, f32[15,512]{1,0:T(8,128)S(1)}, u32[]{:S(2)}, u32[]{:S(2)}) %collective-permute-start.15) | collective-permute-done | bytes 30752 | tf_op jit(solution)/shard_map/ppermute | solution.py:24
  60.7 3.3 %collective-permute-start.18 = (f32[15,512]{1,0:T(8,128)S(1)}, f32[15,512]{1,0:T(8,128)S(1)}, u32[]{:S(2)}, u32[]{:S(2)}) collective-permute-start(f32[15,512]{1,0:T(8,128)S(1)} %add_add_fusion.3), channel_id=1, source_target_pairs={{0,8},{1,9},{2,10},{3,11},{4,12},{5,13},{6,14},{7,15},{8,0},{9,1},... | collective-permute-start | bytes 92168 | tf_op jit(solution)/shard_map/ppermute | solution.py:24
  70.7 5.7 %collective-permute-done.27.refs_4_ = bf16[2,13,64,128]{3,2,1,0:T(8,128)(2,1)} collective-permute-done((bf16[2,13,64,128]{3,2,1,0:T(8,128)(2,1)S(1)}, bf16[2,13,64,128]{3,2,1,0:T(8,128)(2,1)}, u32[]{:S(2)}, u32[]{:S(2)}) %collective-permute-start.27) | collective-permute-done | bytes 426016 | tf_op jit(solution)/shard_map/ppermute | solution.py:24
  81.3 1.9 collective-permute-start.34
  84.9 3.5 %shard_map.348 = (bf16[9,512,512]{2,1,0:T(8,128)(2,1)S(1)}, bf16[512,2048]{1,0:T(8,128)(2,1)S(1)}) custom-call(s32[2]{0:T(128)S(1)} %pad_add_fusion.me, bf16[4,13,64,128]{3,2,1,0:T(8,128)(2,1)S(1)} %pad_maximum_fusion.refs_0_, bf16[4,13,64,128]{3,2,1,0:T(8,128)(2,1)S(1)} %collective-permute-done.24.refs_1_, ...), custom_call_target="tpu_custom_call" | custom-call | bytes 13631496 | tf_op jit(solution)/shard_map/pallas_call | solution.py:124
  88.4 2.8 shard_map.349
  100.0 2.6 collective-permute-start.42
  104.9 3.1 %collective-permute-done.43 = f32[2,512]{1,0:T(2,128)S(1)} collective-permute-done((f32[2,512]{1,0:T(2,128)S(1)}, f32[2,512]{1,0:T(2,128)S(1)}, u32[]{:S(2)}, u32[]{:S(2)}) %collective-permute-start.43) | collective-permute-done | bytes 4128 | tf_op jit(solution)/shard_map/ppermute | solution.py:24
  108.0 3.0 %collective-permute-done.36.refs_2_ = bf16[4,512,128]{2,1,0:T(8,128)(2,1)} collective-permute-done((bf16[4,512,128]{2,1,0:T(8,128)(2,1)}, bf16[4,512,128]{2,1,0:T(8,128)(2,1)}, u32[]{:S(2)}, u32[]{:S(2)}) %collective-permute-start.36) | collective-permute-done | bytes 524320 | tf_op jit(solution)/shard_map/ppermute | solution.py:24
  123.7 2.6 collective-permute-start.49
  129.3 2.5 collective-permute-done.50
  132.6 1.8 collective-permute-done.57.refs_8_
  135.5 7.7 %shard_map.351 = (f32[400,2048]{1,0:T(8,128)S(1)}, f32[2,2176]{1,0:T(2,128)S(1)}, bf16[8,1536]{1,0:T(8,128)(2,1)}, f32[1,1]{1,0:T(1,128)}) custom-call(s32[2]{0:T(128)S(1)} %pad_add_fusion.me, f32[400,2048]{1,0:T(8,128)S(1)} %get-tuple-element.123.hidden, f32[2,2048]{1,0:T(2,128)S(1)} %add_add_fusion.6.sums, f32[2,2048]{1,0:T(2,128)S(1)} %bitcast.77, ...), custom_call_target="tpu_custom_call" | custom-call | flops 67108864 | bytes 12493900 | tf_op jit(solution)/shard_map/pallas_call | solution.py:124
  151.1 2.3 collective-permute-start.64
  153.4 2.1 collective-permute-start.65
  155.8 3.1 %collective-permute-done.65 = f32[2,2176]{1,0:T(2,128)S(1)} collective-permute-done((f32[2,2176]{1,0:T(2,128)S(1)}, f32[2,2176]{1,0:T(2,128)S(1)}, u32[]{:S(2)}, u32[]{:S(2)}) %collective-permute-start.65) | collective-permute-done | bytes 17440 | tf_op jit(solution)/shard_map/ppermute | solution.py:24
  159.0 2.0 shard_map.352
  166.6 2.4 collective-permute-done.69
  169.1 2.6 collective-permute-start.71
  173.6 3.5 %collective-permute-done.72 = f32[2,512]{1,0:T(2,128)S(1)} collective-permute-done((f32[2,512]{1,0:T(2,128)S(1)}, f32[2,512]{1,0:T(2,128)S(1)}, u32[]{:S(2)}, u32[]{:S(2)}) %collective-permute-start.72) | collective-permute-done | bytes 4128 | tf_op jit(solution)/shard_map/ppermute | solution.py:24
  177.2 2.9 %shard_map.353 = (bf16[400,512]{1,0:T(8,128)(2,1)S(1)}, f32[400,512]{1,0:T(8,128)S(1)}, f32[2,512]{1,0:T(2,128)S(1)}) custom-call(s32[2]{0:T(128)S(1)} %pad_add_fusion.me, f32[400,512]{1,0:T(8,128)S(1)} %get-tuple-element.129.upper, f32[400,512]{1,0:T(8,128)S(1)} %copy-done.3, f32[2,512]{1,0:T(2,128)S(1)} %add_add_fusion.12.sums.sums_two, ...), custom_call_target="tpu_custom_call" | custom-call | flops 1887436800 | bytes 8456200 | tf_op jit(solution)/shard_map/pallas_call | solution.py:124
  181.4 5.7 %shard_map.354 = (bf16[16,13,64,128]{3,2,1,0:T(8,128)(2,1)S(1)}, bf16[16,13,64,128]{3,2,1,0:T(8,128)(2,1)S(1)}) custom-call(s32[2]{0:T(128)S(1)} %pad_add_fusion.me, bf16[400,512]{1,0:T(8,128)(2,1)S(1)} %copy-done.18, bf16[400,512]{1,0:T(8,128)(2,1)S(1)} %get-tuple-element.135.down, bf16[400,512]{1,0:T(8,128)(2,1)S(1)} %copy-done.16, ...), custom_call_target="tpu_custom_call" | custom-call | flops 1887436800 | bytes 9682952 | tf_op jit(solution)/shard_map/pallas_call | solution.py:124
  196.7 2.3 collective-permute-start.81
  199.0 2.1 collective-permute-start.82
  201.2 3.2 %collective-permute-done.82 = f32[2,512]{1,0:T(2,128)S(1)} collective-permute-done((f32[2,512]{1,0:T(2,128)S(1)}, f32[2,512]{1,0:T(2,128)S(1)}, u32[]{:S(2)}, u32[]{:S(2)}) %collective-permute-start.82) | collective-permute-done | bytes 4128 | tf_op jit(solution)/shard_map/ppermute | solution.py:24
  204.4 9.4 %collective-permute-done.79.refs_1_ = bf16[8,6,64,128]{3,2,1,0:T(8,128)(2,1)S(1)} collective-permute-done((bf16[8,6,64,128]{3,2,1,0:T(8,128)(2,1)S(1)}, bf16[8,6,64,128]{3,2,1,0:T(8,128)(2,1)S(1)}, u32[]{:S(2)}, u32[]{:S(2)}) %collective-permute-start.79) | collective-permute-done | bytes 786464 | tf_op jit(solution)/shard_map/ppermute | solution.py:24
  213.9 2.6 collective-permute-done.78.refs_0_
  218.5 4.8 %shard_map.357 = (bf16[16,256,128]{2,1,0:T(8,128)(2,1)S(1)}, bf16[16,256,128]{2,1,0:T(8,128)(2,1)}) custom-call(s32[2]{0:T(128)S(1)} %pad_add_fusion.me, f32[400,512]{1,0:T(8,128)S(1)} %get-tuple-element.149.upper, f32[400,512]{1,0:T(8,128)S(1)} %copy-done.5, f32[15,512]{1,0:T(8,128)S(1)} %add_add_fusion.2.sums.sums_one, f32[2,512]{1,0:T(2,128)S(1)} %bitcast.84, ...), custom_call_target="tpu_custom_call" | custom-call | flops 838860800 | bytes 5412872 | tf_op jit(solution)/shard_map/pallas_call | solution.py:124
  223.5 2.3 collective-permute-start.96
  225.8 2.1 collective-permute-start.97
  229.7 1.9 collective-permute-done.97
  235.6 5.2 %collective-permute-done.88.refs_1_ = bf16[4,6,64,128]{3,2,1,0:T(8,128)(2,1)S(1)} collective-permute-done((bf16[4,6,64,128]{3,2,1,0:T(8,128)(2,1)}, bf16[4,6,64,128]{3,2,1,0:T(8,128)(2,1)S(1)}, u32[]{:S(2)}, u32[]{:S(2)}) %collective-permute-start.88) | collective-permute-done | bytes 393248 | tf_op jit(solution)/shard_map/ppermute | solution.py:24
  248.5 2.2 collective-permute-start.90
  250.8 2.1 collective-permute-start.91
  254.8 8.7 %collective-permute-done.90 = bf16[13,64,128]{2,1,0:T(8,128)(2,1)S(1)} collective-permute-done((bf16[13,64,128]{2,1,0:T(8,128)(2,1)S(1)}, bf16[13,64,128]{2,1,0:T(8,128)(2,1)S(1)}, u32[]{:S(2)}, u32[]{:S(2)}) %collective-permute-start.90) | collective-permute-done | bytes 213024 | tf_op jit(solution)/shard_map/ppermute | solution.py:24
  265.6 3.7 %collective-permute-start.92 = (bf16[256,128]{1,0:T(8,128)(2,1)S(1)}, bf16[256,128]{1,0:T(8,128)(2,1)S(1)}, u32[]{:S(2)}, u32[]{:S(2)}) collective-permute-start(bf16[256,128]{1,0:T(8,128)(2,1)S(1)} %get-tuple-element.166), channel_id=1, source_target_pairs={{0,8},{1,9},{2,10},{3,11},{4,12},{5,13},{6,14},{7,15},{8,0},{9,1},... | collective-permute-start | bytes 196616 | tf_op jit(solution)/shard_map/ppermute | solution.py:24
  269.7 2.1 collective-permute-start.94
  (357 shorter events, 117.1 us)
Async XLA Ops:
  4.5 20.5 %collective-permute-start.4 = (bf16[400,512]{1,0:T(8,128)(2,1)S(1)}, bf16[400,512]{1,0:T(8,128)(2,1)S(1)}, u32[]{:S(2)}, u32[]{:S(2)}) collective-permute-start(bf16[400,512]{1,0:T(8,128)(2,1)S(1)} %get-tuple-element.106), channel_id=1, source_target_pairs={{0,2},{1,3},{2,0},{3,1},{4,6},{5,7},{6,4},{7,5},{8,10},{9,11},{10,... | collective-permute-start | bytes 1228808 | tf_op jit(solution)/shard_map/ppermute | solution.py:24
  7.5 18.2 %collective-permute-start.3 = (bf16[400,512]{1,0:T(8,128)(2,1)S(1)}, bf16[400,512]{1,0:T(8,128)(2,1)S(1)}, u32[]{:S(2)}, u32[]{:S(2)}) collective-permute-start(bf16[400,512]{1,0:T(8,128)(2,1)S(1)} %get-tuple-element.105), channel_id=1, source_target_pairs={{0,2},{1,3},{2,0},{3,1},{4,6},{5,7},{6,4},{7,5},{8,10},{9,11},{10,... | collective-permute-start | bytes 1228808 | tf_op jit(solution)/shard_map/ppermute | solution.py:24
  11.8 17.2 %collective-permute-start.21 = (bf16[13,64,128]{2,1,0:T(8,128)(2,1)S(1)}, bf16[13,64,128]{2,1,0:T(8,128)(2,1)S(1)}, u32[]{:S(2)}, u32[]{:S(2)}) collective-permute-start(bf16[13,64,128]{2,1,0:T(8,128)(2,1)S(1)} %get-tuple-element.113), channel_id=1, source_target_pairs={{0,8},{1,9},{2,10},{3,11},{4,12},{5,13},{6,14},{7,15},{8,0},{9,1},... | collective-permute-start | bytes 638984 | tf_op jit(solution)/shard_map/ppermute | solution.py:24
  16.4 7.0 %collective-permute-start.2 = (bf16[256,128]{1,0:T(8,128)(2,1)S(1)}, bf16[256,128]{1,0:T(8,128)(2,1)S(1)}, u32[]{:S(2)}, u32[]{:S(2)}) collective-permute-start(bf16[256,128]{1,0:T(8,128)(2,1)S(1)} %get-tuple-element.104), channel_id=1, source_target_pairs={{0,24},{1,25},{2,26},{3,27},{4,28},{5,29},{6,30},{7,31},{8,16},{9,... | collective-permute-start | bytes 196616 | tf_op jit(solution)/shard_map/ppermute | solution.py:24
  19.7 16.8 %collective-permute-start.22 = (bf16[13,64,128]{2,1,0:T(8,128)(2,1)S(1)}, bf16[13,64,128]{2,1,0:T(8,128)(2,1)S(1)}, u32[]{:S(2)}, u32[]{:S(2)}) collective-permute-start(bf16[13,64,128]{2,1,0:T(8,128)(2,1)S(1)} %get-tuple-element.113), channel_id=1, source_target_pairs={{0,16},{1,17},{2,18},{3,19},{4,20},{5,21},{6,22},{7,23},{8,24},{9,... | collective-permute-start | bytes 638984 | tf_op jit(solution)/shard_map/ppermute | solution.py:24
  23.4 13.6 %collective-permute-start.23 = (bf16[13,64,128]{2,1,0:T(8,128)(2,1)S(1)}, bf16[13,64,128]{2,1,0:T(8,128)(2,1)S(1)}, u32[]{:S(2)}, u32[]{:S(2)}) collective-permute-start(bf16[13,64,128]{2,1,0:T(8,128)(2,1)S(1)} %get-tuple-element.113), channel_id=1, source_target_pairs={{0,24},{1,25},{2,26},{3,27},{4,28},{5,29},{6,30},{7,31},{8,16},{9,... | collective-permute-start | bytes 638984 | tf_op jit(solution)/shard_map/ppermute | solution.py:24
  25.7 10.8 %collective-permute-start.5 = (bf16[4,256,128]{2,1,0:T(8,128)(2,1)S(1)}, bf16[4,256,128]{2,1,0:T(8,128)(2,1)S(1)}, u32[]{:S(2)}, u32[]{:S(2)}) collective-permute-start(bf16[4,256,128]{2,1,0:T(8,128)(2,1)S(1)} %pad_maximum_fusion.2.refs_0_), channel_id=1, source_target_pairs={{0,4},{1,5},{2,6},{3,7},{4,0},{5,1},{6,2},{7,3},{8,12},{9,13},{10,... | collective-permute-start | bytes 786440 | tf_op jit(solution)/shard_map/ppermute | solution.py:24
  27.5 11.3 %collective-permute-start.6 = (bf16[4,256,128]{2,1,0:T(8,128)(2,1)S(1)}, bf16[4,256,128]{2,1,0:T(8,128)(2,1)S(1)}, u32[]{:S(2)}, u32[]{:S(2)}) collective-permute-start(bf16[4,256,128]{2,1,0:T(8,128)(2,1)S(1)} %pad_maximum_fusion.2.refs_0_), channel_id=1, source_target_pairs={{0,2},{1,3},{2,0},{3,1},{4,6},{5,7},{6,4},{7,5},{8,10},{9,11},{10,... | collective-permute-start | bytes 786440 | tf_op jit(solution)/shard_map/ppermute | solution.py:24
  29.0 11.3 %collective-permute-start.7 = (bf16[4,256,128]{2,1,0:T(8,128)(2,1)S(1)}, bf16[4,256,128]{2,1,0:T(8,128)(2,1)S(1)}, u32[]{:S(2)}, u32[]{:S(2)}) collective-permute-start(bf16[4,256,128]{2,1,0:T(8,128)(2,1)S(1)} %pad_maximum_fusion.2.refs_0_), channel_id=1, source_target_pairs={{0,6},{1,7},{2,4},{3,5},{4,2},{5,3},{6,0},{7,1},{8,14},{9,15},{10,... | collective-permute-start | bytes 786440 | tf_op jit(solution)/shard_map/ppermute | solution.py:24
  37.2 29.2 %collective-permute-start.24 = (bf16[4,13,64,128]{3,2,1,0:T(8,128)(2,1)S(1)}, bf16[4,13,64,128]{3,2,1,0:T(8,128)(2,1)S(1)}, u32[]{:S(2)}, u32[]{:S(2)}) collective-permute-start(bf16[4,13,64,128]{3,2,1,0:T(8,128)(2,1)S(1)} %pad_maximum_fusion.refs_0_), channel_id=1, source_target_pairs={{0,4},{1,5},{2,6},{3,7},{4,0},{5,1},{6,2},{7,3},{8,12},{9,13},{10,... | collective-permute-start | bytes 2555912 | tf_op jit(solution)/shard_map/ppermute | solution.py:24
  38.8 29.2 %collective-permute-start.25 = (bf16[4,13,64,128]{3,2,1,0:T(8,128)(2,1)S(1)}, bf16[4,13,64,128]{3,2,1,0:T(8,128)(2,1)S(1)}, u32[]{:S(2)}, u32[]{:S(2)}) collective-permute-start(bf16[4,13,64,128]{3,2,1,0:T(8,128)(2,1)S(1)} %pad_maximum_fusion.refs_0_), channel_id=1, source_target_pairs={{0,2},{1,3},{2,0},{3,1},{4,6},{5,7},{6,4},{7,5},{8,10},{9,11},{10,... | collective-permute-start | bytes 2555912 | tf_op jit(solution)/shard_map/ppermute | solution.py:24
  51.8 8.6 %collective-permute-start.15 = (f32[15,512]{1,0:T(8,128)S(1)}, f32[15,512]{1,0:T(8,128)S(1)}, u32[]{:S(2)}, u32[]{:S(2)}) collective-permute-start(f32[15,512]{1,0:T(8,128)S(1)} %add.212), channel_id=1, source_target_pairs={{0,2},{1,3},{2,0},{3,1},{4,6},{5,7},{6,4},{7,5},{8,10},{9,11},{10,... | collective-permute-start | bytes 92168 | tf_op jit(solution)/shard_map/ppermute | solution.py:24
  53.0 7.4 %collective-permute-start.16 = (f32[15,512]{1,0:T(8,128)S(1)}, f32[15,512]{1,0:T(8,128)S(1)}, u32[]{:S(2)}, u32[]{:S(2)}) collective-permute-start(f32[15,512]{1,0:T(8,128)S(1)} %add.212), channel_id=1, source_target_pairs={{0,4},{1,5},{2,6},{3,7},{4,0},{5,1},{6,2},{7,3},{8,12},{9,13},{10,... | collective-permute-start | bytes 92168 | tf_op jit(solution)/shard_map/ppermute | solution.py:24
  60.7 8.9 %collective-permute-start.18 = (f32[15,512]{1,0:T(8,128)S(1)}, f32[15,512]{1,0:T(8,128)S(1)}, u32[]{:S(2)}, u32[]{:S(2)}) collective-permute-start(f32[15,512]{1,0:T(8,128)S(1)} %add_add_fusion.3), channel_id=1, source_target_pairs={{0,8},{1,9},{2,10},{3,11},{4,12},{5,13},{6,14},{7,15},{8,0},{9,1},... | collective-permute-start | bytes 92168 | tf_op jit(solution)/shard_map/ppermute | solution.py:24
  66.4 9.9 %collective-permute-start.27 = (bf16[2,13,64,128]{3,2,1,0:T(8,128)(2,1)S(1)}, bf16[2,13,64,128]{3,2,1,0:T(8,128)(2,1)}, u32[]{:S(2)}, u32[]{:S(2)}) collective-permute-start(bf16[2,13,64,128]{3,2,1,0:T(8,128)(2,1)S(1)} %slice.55), channel_id=1, source_target_pairs={{0,2},{1,3},{2,0},{3,1},{4,6},{5,7},{6,4},{7,5},{8,10},{9,11},{10,... | collective-permute-start | bytes 1277960 | tf_op jit(solution)/shard_map/ppermute | solution.py:24
  68.0 9.7 %collective-permute-start.26 = (bf16[2,13,64,128]{3,2,1,0:T(8,128)(2,1)S(1)}, bf16[2,13,64,128]{3,2,1,0:T(8,128)(2,1)}, u32[]{:S(2)}, u32[]{:S(2)}) collective-permute-start(bf16[2,13,64,128]{3,2,1,0:T(8,128)(2,1)S(1)} %slice.54), channel_id=1, source_target_pairs={{0,4},{1,5},{2,6},{3,7},{4,0},{5,1},{6,2},{7,3},{8,12},{9,13},{10,... | collective-permute-start | bytes 1277960 | tf_op jit(solution)/shard_map/ppermute | solution.py:24
  69.6 10.8 %collective-permute-start.28 = (bf16[4,13,64,128]{3,2,1,0:T(8,128)(2,1)S(1)}, bf16[4,13,64,128]{3,2,1,0:T(8,128)(2,1)}, u32[]{:S(2)}, u32[]{:S(2)}) collective-permute-start(bf16[4,13,64,128]{3,2,1,0:T(8,128)(2,1)S(1)} %pad_maximum_fusion.refs_0_), channel_id=1, source_target_pairs={{0,1},{1,0},{2,3},{3,2},{4,5},{5,4},{6,7},{7,6},{8,9},{9,8},{10,11... | collective-permute-start | bytes 2555912 | tf_op jit(solution)/shard_map/ppermute | solution.py:24
  69.6 15.3 %collective-permute-start.29 = (bf16[4,13,64,128]{3,2,1,0:T(8,128)(2,1)S(1)}, bf16[4,13,64,128]{3,2,1,0:T(8,128)(2,1)}, u32[]{:S(2)}, u32[]{:S(2)}) collective-permute-start(bf16[4,13,64,128]{3,2,1,0:T(8,128)(2,1)S(1)} %collective-permute-done.24.refs_1_), channel_id=1, source_target_pairs={{0,1},{1,0},{2,3},{3,2},{4,5},{5,4},{6,7},{7,6},{8,9},{9,8},{10,11... | collective-permute-start | bytes 2555912 | tf_op jit(solution)/shard_map/ppermute | solution.py:24
  70.7 14.2 %collective-permute-start.30 = (bf16[4,13,64,128]{3,2,1,0:T(8,128)(2,1)S(1)}, bf16[4,13,64,128]{3,2,1,0:T(8,128)(2,1)}, u32[]{:S(2)}, u32[]{:S(2)}) collective-permute-start(bf16[4,13,64,128]{3,2,1,0:T(8,128)(2,1)S(1)} %collective-permute-done.25.refs_2_), channel_id=1, source_target_pairs={{0,1},{1,0},{2,3},{3,2},{4,5},{5,4},{6,7},{7,6},{8,9},{9,8},{10,11... | collective-permute-start | bytes 2555912 | tf_op jit(solution)/shard_map/ppermute | solution.py:24
  80.4 14.9 %collective-permute-start.33 = (bf16[512,128]{1,0:T(8,128)(2,1)S(1)}, bf16[512,128]{1,0:T(8,128)(2,1)S(1)}, u32[]{:S(2)}, u32[]{:S(2)}) collective-permute-start(bf16[512,128]{1,0:T(8,128)(2,1)S(1)} %get-tuple-element.118), channel_id=1, source_target_pairs={{0,8},{1,9},{2,10},{3,11},{4,12},{5,13},{6,14},{7,15},{8,0},{9,1},... | collective-permute-start | bytes 393224 | tf_op jit(solution)/shard_map/ppermute | solution.py:24
  81.3 15.4 %collective-permute-start.34 = (bf16[512,128]{1,0:T(8,128)(2,1)S(1)}, bf16[512,128]{1,0:T(8,128)(2,1)S(1)}, u32[]{:S(2)}, u32[]{:S(2)}) collective-permute-start(bf16[512,128]{1,0:T(8,128)(2,1)S(1)} %get-tuple-element.118), channel_id=1, source_target_pairs={{0,16},{1,17},{2,18},{3,19},{4,20},{5,21},{6,22},{7,23},{8,24},{9,... | collective-permute-start | bytes 393224 | tf_op jit(solution)/shard_map/ppermute | solution.py:24
  83.2 13.5 %collective-permute-start.35 = (bf16[512,128]{1,0:T(8,128)(2,1)S(1)}, bf16[512,128]{1,0:T(8,128)(2,1)S(1)}, u32[]{:S(2)}, u32[]{:S(2)}) collective-permute-start(bf16[512,128]{1,0:T(8,128)(2,1)S(1)} %get-tuple-element.118), channel_id=1, source_target_pairs={{0,24},{1,25},{2,26},{3,27},{4,28},{5,29},{6,30},{7,31},{8,16},{9,... | collective-permute-start | bytes 393224 | tf_op jit(solution)/shard_map/ppermute | solution.py:24
  97.5 13.5 %collective-permute-start.36 = (bf16[4,512,128]{2,1,0:T(8,128)(2,1)}, bf16[4,512,128]{2,1,0:T(8,128)(2,1)}, u32[]{:S(2)}, u32[]{:S(2)}) collective-permute-start(bf16[4,512,128]{2,1,0:T(8,128)(2,1)} %pad_maximum_fusion.1.refs_0_), channel_id=1, source_target_pairs={{0,2},{1,3},{2,0},{3,1},{4,6},{5,7},{6,4},{7,5},{8,10},{9,11},{10,... | collective-permute-start | bytes 1572872 | tf_op jit(solution)/shard_map/ppermute | solution.py:24
  104.3 15.3 %collective-permute-start.51 = (bf16[4,512,128]{2,1,0:T(8,128)(2,1)}, bf16[4,512,128]{2,1,0:T(8,128)(2,1)}, u32[]{:S(2)}, u32[]{:S(2)}) collective-permute-start(bf16[4,512,128]{2,1,0:T(8,128)(2,1)} %pad_maximum_fusion.1.refs_0_), channel_id=1, source_target_pairs={{0,4},{1,5},{2,6},{3,7},{4,0},{5,1},{6,2},{7,3},{8,12},{9,13},{10,... | collective-permute-start | bytes 1572872 | tf_op jit(solution)/shard_map/ppermute | solution.py:24
  113.9 9.6 %collective-permute-start.45 = (f32[2,2048]{1,0:T(2,128)S(1)}, f32[2,2048]{1,0:T(2,128)S(1)}, u32[]{:S(2)}, u32[]{:S(2)}) collective-permute-start(f32[2,2048]{1,0:T(2,128)S(1)} %add.226), channel_id=1, source_target_pairs={{0,2},{1,3},{2,0},{3,1},{4,6},{5,7},{6,4},{7,5},{8,10},{9,11},{10,... | collective-permute-start | bytes 49160 | tf_op jit(solution)/shard_map/ppermute | solution.py:24
  114.7 8.9 %collective-permute-start.46 = (f32[2,2048]{1,0:T(2,128)S(1)}, f32[2,2048]{1,0:T(2,128)S(1)}, u32[]{:S(2)}, u32[]{:S(2)}) collective-permute-start(f32[2,2048]{1,0:T(2,128)S(1)} %add.226), channel_id=1, source_target_pairs={{0,4},{1,5},{2,6},{3,7},{4,0},{5,1},{6,2},{7,3},{8,12},{9,13},{10,... | collective-permute-start | bytes 49160 | tf_op jit(solution)/shard_map/ppermute | solution.py:24
  116.2 7.4 %collective-permute-start.47 = (f32[2,2048]{1,0:T(2,128)S(1)}, f32[2,2048]{1,0:T(2,128)S(1)}, u32[]{:S(2)}, u32[]{:S(2)}) collective-permute-start(f32[2,2048]{1,0:T(2,128)S(1)} %add.226), channel_id=1, source_target_pairs={{0,6},{1,7},{2,4},{3,5},{4,2},{5,3},{6,0},{7,1},{8,14},{9,15},{10,... | collective-permute-start | bytes 49160 | tf_op jit(solution)/shard_map/ppermute | solution.py:24
  121.3 10.6 %collective-permute-start.52 = (bf16[2,512,128]{2,1,0:T(8,128)(2,1)}, bf16[2,512,128]{2,1,0:T(8,128)(2,1)}, u32[]{:S(2)}, u32[]{:S(2)}) collective-permute-start(bf16[2,512,128]{2,1,0:T(8,128)(2,1)} %slice.59), channel_id=1, source_target_pairs={{0,4},{1,5},{2,6},{3,7},{4,0},{5,1},{6,2},{7,3},{8,12},{9,13},{10,... | collective-permute-start | bytes 786440 | tf_op jit(solution)/shard_map/ppermute | solution.py:24
  122.9 9.6 %collective-permute-start.53 = (bf16[2,512,128]{2,1,0:T(8,128)(2,1)}, bf16[2,512,128]{2,1,0:T(8,128)(2,1)}, u32[]{:S(2)}, u32[]{:S(2)}) collective-permute-start(bf16[2,512,128]{2,1,0:T(8,128)(2,1)} %slice.60), channel_id=1, source_target_pairs={{0,2},{1,3},{2,0},{3,1},{4,6},{5,7},{6,4},{7,5},{8,10},{9,11},{10,... | collective-permute-start | bytes 786440 | tf_op jit(solution)/shard_map/ppermute | solution.py:24
  187.1 6.6 %collective-permute-start.74 = (bf16[16,13,64,128]{3,2,1,0:T(8,128)(2,1)S(1)}, bf16[16,13,64,128]{3,2,1,0:T(8,128)(2,1)S(1)}, u32[]{:S(2)}, u32[]{:S(2)}) collective-permute-start(bf16[16,13,64,128]{3,2,1,0:T(8,128)(2,1)S(1)} %get-tuple-element.138), channel_id=1, source_target_pairs={{0,1},{1,0},{2,3},{3,2},{4,5},{5,4},{6,7},{7,6},{8,9},{9,8},{10,11... | collective-permute-start | bytes 10223624 | tf_op jit(solution)/shard_map/ppermute | solution.py:24
  194.4 22.0 %collective-permute-start.78 = (bf16[8,7,64,128]{3,2,1,0:T(8,128)(2,1)S(1)}, bf16[8,7,64,128]{3,2,1,0:T(8,128)(2,1)S(1)}, u32[]{:S(2)}, u32[]{:S(2)}) collective-permute-start(bf16[8,7,64,128]{3,2,1,0:T(8,128)(2,1)S(1)} %get-tuple-element.143), channel_id=1, source_target_pairs={{0,4},{1,5},{2,6},{3,7},{4,0},{5,1},{6,2},{7,3},{8,12},{9,13},{10,... | collective-permute-start | bytes 2752520 | tf_op jit(solution)/shard_map/ppermute | solution.py:24
  196.0 17.8 %collective-permute-start.79 = (bf16[8,6,64,128]{3,2,1,0:T(8,128)(2,1)S(1)}, bf16[8,6,64,128]{3,2,1,0:T(8,128)(2,1)S(1)}, u32[]{:S(2)}, u32[]{:S(2)}) collective-permute-start(bf16[8,6,64,128]{3,2,1,0:T(8,128)(2,1)S(1)} %get-tuple-element.144), channel_id=1, source_target_pairs={{0,2},{1,3},{2,0},{3,1},{4,6},{5,7},{6,4},{7,5},{8,10},{9,11},{10,... | collective-permute-start | bytes 2359304 | tf_op jit(solution)/shard_map/ppermute | solution.py:24
  223.3 19.5 %collective-permute-start.83 = (bf16[16,256,128]{2,1,0:T(8,128)(2,1)}, bf16[16,256,128]{2,1,0:T(8,128)(2,1)S(1)}, u32[]{:S(2)}, u32[]{:S(2)}) collective-permute-start(bf16[16,256,128]{2,1,0:T(8,128)(2,1)} %get-tuple-element.150), channel_id=1, source_target_pairs={{0,1},{1,0},{2,3},{3,2},{4,5},{5,4},{6,7},{7,6},{8,9},{9,8},{10,11... | collective-permute-start | bytes 3145736 | tf_op jit(solution)/shard_map/ppermute | solution.py:24
  223.5 6.2 %collective-permute-start.96 = (bf16[8,1536]{1,0:T(8,128)(2,1)}, bf16[8,1536]{1,0:T(8,128)(2,1)S(1)}, u32[]{:S(2)}, u32[]{:S(2)}) collective-permute-start(bf16[8,1536]{1,0:T(8,128)(2,1)} %get-tuple-element.177), channel_id=1, source_target_pairs={{0,16},{1,17},{2,18},{3,19},{4,20},{5,21},{6,22},{7,23},{8,24},{9,... | collective-permute-start | bytes 73736 | tf_op jit(solution)/shard_map/ppermute | solution.py:24
  227.9 13.7 %collective-permute-start.87 = (bf16[4,7,64,128]{3,2,1,0:T(8,128)(2,1)}, bf16[4,7,64,128]{3,2,1,0:T(8,128)(2,1)S(1)}, u32[]{:S(2)}, u32[]{:S(2)}) collective-permute-start(bf16[4,7,64,128]{3,2,1,0:T(8,128)(2,1)} %copy-done.12), channel_id=1, source_target_pairs={{0,2},{1,3},{2,0},{3,1},{4,6},{5,7},{6,4},{7,5},{8,10},{9,11},{10,... | collective-permute-start | bytes 1376264 | tf_op jit(solution)/shard_map/ppermute | solution.py:24
  229.2 11.6 %collective-permute-start.88 = (bf16[4,6,64,128]{3,2,1,0:T(8,128)(2,1)}, bf16[4,6,64,128]{3,2,1,0:T(8,128)(2,1)S(1)}, u32[]{:S(2)}, u32[]{:S(2)}) collective-permute-start(bf16[4,6,64,128]{3,2,1,0:T(8,128)(2,1)} %copy-done.14), channel_id=1, source_target_pairs={{0,4},{1,5},{2,6},{3,7},{4,0},{5,1},{6,2},{7,3},{8,12},{9,13},{10,... | collective-permute-start | bytes 1179656 | tf_op jit(solution)/shard_map/ppermute | solution.py:24
  233.0 11.5 %collective-permute-start.98 = (bf16[4,8,1536]{2,1,0:T(8,128)(2,1)S(1)}, bf16[4,8,1536]{2,1,0:T(8,128)(2,1)}, u32[]{:S(2)}, u32[]{:S(2)}) collective-permute-start(bf16[4,8,1536]{2,1,0:T(8,128)(2,1)S(1)} %pad_maximum_fusion.3.refs_0_), channel_id=1, source_target_pairs={{0,4},{1,5},{2,6},{3,7},{4,0},{5,1},{6,2},{7,3},{8,12},{9,13},{10,... | collective-permute-start | bytes 294920 | tf_op jit(solution)/shard_map/ppermute | solution.py:24
  233.6 12.4 %collective-permute-start.99 = (bf16[4,8,1536]{2,1,0:T(8,128)(2,1)S(1)}, bf16[4,8,1536]{2,1,0:T(8,128)(2,1)}, u32[]{:S(2)}, u32[]{:S(2)}) collective-permute-start(bf16[4,8,1536]{2,1,0:T(8,128)(2,1)S(1)} %pad_maximum_fusion.3.refs_0_), channel_id=1, source_target_pairs={{0,2},{1,3},{2,0},{3,1},{4,6},{5,7},{6,4},{7,5},{8,10},{9,11},{10,... | collective-permute-start | bytes 294920 | tf_op jit(solution)/shard_map/ppermute | solution.py:24
  240.8 7.7 %collective-permute-start.100 = (bf16[4,8,1536]{2,1,0:T(8,128)(2,1)S(1)}, bf16[4,8,1536]{2,1,0:T(8,128)(2,1)S(1)}, u32[]{:S(2)}, u32[]{:S(2)}) collective-permute-start(bf16[4,8,1536]{2,1,0:T(8,128)(2,1)S(1)} %pad_maximum_fusion.3.refs_0_), channel_id=1, source_target_pairs={{0,6},{1,7},{2,4},{3,5},{4,2},{5,3},{6,0},{7,1},{8,14},{9,15},{10,... | collective-permute-start | bytes 294920 | tf_op jit(solution)/shard_map/ppermute | solution.py:24
  242.7 8.1 %collective-permute-start.89 = (bf16[13,64,128]{2,1,0:T(8,128)(2,1)S(1)}, bf16[13,64,128]{2,1,0:T(8,128)(2,1)S(1)}, u32[]{:S(2)}, u32[]{:S(2)}) collective-permute-start(bf16[13,64,128]{2,1,0:T(8,128)(2,1)S(1)} %get-tuple-element.159), channel_id=1, source_target_pairs={{0,8},{1,9},{2,10},{3,11},{4,12},{5,13},{6,14},{7,15},{8,0},{9,1},... | collective-permute-start | bytes 638984 | tf_op jit(solution)/shard_map/ppermute | solution.py:24
  243.1 20.9 %collective-permute-start.84 = (bf16[4,256,128]{2,1,0:T(8,128)(2,1)S(1)}, bf16[4,256,128]{2,1,0:T(8,128)(2,1)S(1)}, u32[]{:S(2)}, u32[]{:S(2)}) collective-permute-start(bf16[4,256,128]{2,1,0:T(8,128)(2,1)S(1)} %get-tuple-element.153), channel_id=1, source_target_pairs={{0,2},{1,3},{2,0},{3,1},{4,6},{5,7},{6,4},{7,5},{8,10},{9,11},{10,... | collective-permute-start | bytes 786440 | tf_op jit(solution)/shard_map/ppermute | solution.py:24
  244.5 19.6 %collective-permute-start.85 = (bf16[4,256,128]{2,1,0:T(8,128)(2,1)S(1)}, bf16[4,256,128]{2,1,0:T(8,128)(2,1)S(1)}, u32[]{:S(2)}, u32[]{:S(2)}) collective-permute-start(bf16[4,256,128]{2,1,0:T(8,128)(2,1)S(1)} %get-tuple-element.154), channel_id=1, source_target_pairs={{0,4},{1,5},{2,6},{3,7},{4,0},{5,1},{6,2},{7,3},{8,12},{9,13},{10,... | collective-permute-start | bytes 786440 | tf_op jit(solution)/shard_map/ppermute | solution.py:24
  246.0 18.6 %collective-permute-start.86 = (bf16[4,256,128]{2,1,0:T(8,128)(2,1)S(1)}, bf16[4,256,128]{2,1,0:T(8,128)(2,1)S(1)}, u32[]{:S(2)}, u32[]{:S(2)}) collective-permute-start(bf16[4,256,128]{2,1,0:T(8,128)(2,1)S(1)} %get-tuple-element.155), channel_id=1, source_target_pairs={{0,6},{1,7},{2,4},{3,5},{4,2},{5,3},{6,0},{7,1},{8,14},{9,15},{10,... | collective-permute-start | bytes 786440 | tf_op jit(solution)/shard_map/ppermute | solution.py:24
  248.5 14.9 %collective-permute-start.90 = (bf16[13,64,128]{2,1,0:T(8,128)(2,1)S(1)}, bf16[13,64,128]{2,1,0:T(8,128)(2,1)S(1)}, u32[]{:S(2)}, u32[]{:S(2)}) collective-permute-start(bf16[13,64,128]{2,1,0:T(8,128)(2,1)S(1)} %get-tuple-element.160), channel_id=1, source_target_pairs={{0,16},{1,17},{2,18},{3,19},{4,20},{5,21},{6,22},{7,23},{8,24},{9,... | collective-permute-start | bytes 638984 | tf_op jit(solution)/shard_map/ppermute | solution.py:24
  250.8 12.7 %collective-permute-start.91 = (bf16[13,64,128]{2,1,0:T(8,128)(2,1)S(1)}, bf16[13,64,128]{2,1,0:T(8,128)(2,1)S(1)}, u32[]{:S(2)}, u32[]{:S(2)}) collective-permute-start(bf16[13,64,128]{2,1,0:T(8,128)(2,1)S(1)} %get-tuple-element.161), channel_id=1, source_target_pairs={{0,24},{1,25},{2,26},{3,27},{4,28},{5,29},{6,30},{7,31},{8,16},{9,... | collective-permute-start | bytes 638984 | tf_op jit(solution)/shard_map/ppermute | solution.py:24
  265.6 12.0 %collective-permute-start.92 = (bf16[256,128]{1,0:T(8,128)(2,1)S(1)}, bf16[256,128]{1,0:T(8,128)(2,1)S(1)}, u32[]{:S(2)}, u32[]{:S(2)}) collective-permute-start(bf16[256,128]{1,0:T(8,128)(2,1)S(1)} %get-tuple-element.166), channel_id=1, source_target_pairs={{0,8},{1,9},{2,10},{3,11},{4,12},{5,13},{6,14},{7,15},{8,0},{9,1},... | collective-permute-start | bytes 196616 | tf_op jit(solution)/shard_map/ppermute | solution.py:24
  269.3 8.3 %collective-permute-start.93 = (bf16[256,128]{1,0:T(8,128)(2,1)S(1)}, bf16[256,128]{1,0:T(8,128)(2,1)S(1)}, u32[]{:S(2)}, u32[]{:S(2)}) collective-permute-start(bf16[256,128]{1,0:T(8,128)(2,1)S(1)} %get-tuple-element.167), channel_id=1, source_target_pairs={{0,16},{1,17},{2,18},{3,19},{4,20},{5,21},{6,22},{7,23},{8,24},{9,... | collective-permute-start | bytes 196616 | tf_op jit(solution)/shard_map/ppermute | solution.py:24
  269.7 8.0 %collective-permute-start.94 = (bf16[256,128]{1,0:T(8,128)(2,1)S(1)}, bf16[256,128]{1,0:T(8,128)(2,1)S(1)}, u32[]{:S(2)}, u32[]{:S(2)}) collective-permute-start(bf16[256,128]{1,0:T(8,128)(2,1)S(1)} %get-tuple-element.168), channel_id=1, source_target_pairs={{0,24},{1,25},{2,26},{3,27},{4,28},{5,29},{6,30},{7,31},{8,16},{9,... | collective-permute-start | bytes 196616 | tf_op jit(solution)/shard_map/ppermute | solution.py:24
  (107 other events, 860.8 us)
